TPU v7x, 32 devices: a whole 2x2x4 slice. The times are simulated.
32 devices in a mesh: parts: 2 (over y), ep: 4 (over z), fs: 4 (over x, core).
Axes of the slice: x: 2, y: 2, z: 4, core: 2. Of those that a mesh axis runs over, the one named last changes fastest.
Arguments:
- hidden_states: bfloat16 [8, 512, 1152], P(('parts', 'fs'), 'ep'), parts along dimension 0, may hold values from -6 to 6
- expert_ids: int32 [8, 512, 2], P(('parts', 'fs'), 'ep'), parts along dimension 0, may hold values from 0 to 15, all different within a row; in each aligned block of 128 rows (0 to 127, 128 to 255, ..., all dimensions but the last counted through in order) at most 20 rows name the same one
- modulation: float32 [8, 3, 1152], P(('parts', 'fs')), parts along dimension 0, may hold values from -4 to 4
- router_weight: bfloat16 [1152, 16], replicated, may hold values from -0.1875 to 0.1875
- w_in: bfloat16 [32, 1152, 2304], P('ep', 'fs'), may hold values from -0.1875 to 0.1875
- b_in: float32 [32, 2304], P('ep'), may hold values from -3 to 3
- w_out: bfloat16 [32, 2304, 1152], P('ep', 'fs'), may hold values from -0.09375 to 0.09375
Outputs:
- layer_out: bfloat16 [8, 512, 1152], P(('parts', 'fs'), 'ep'), parts along dimension 0
There are 2 independent parts, one for each index of `parts`. A program takes and returns all parts, laid end to end along the dimension named above; an argument that names none is the same for every part. Nothing has to cross between parts.
Inputs may be any that keep to these rules, and one draw needn't show every extreme that they name: `expert_ids`: the two ids of a token differ. In each aligned block of 128 tokens of an image, no expert is named by more than 20 tokens, a bound that some block reaches.
All inputs are finite; a program needn't handle non-finite values.
Results may differ from a plain program's by a relative error of at most 0.0046.
Values may be sent and summed in bfloat16 or wider, within the bound.
No kernel may reach another device: no remote copies, remote signals or barrier semaphores. Data moves between devices by JAX's collectives and lax.ppermute only.
A program may use at most 192 MiB of HBM per device.

v0:
```python
import jax
import jax.numpy as jnp
from jax import lax
from jax.sharding import PartitionSpec as P

EXPERTS = 16
SPLIT = 2
CAP = 20


norm_eps = 1e-06


def swapped(block, axis, distance):
    count = lax.axis_size(axis)
    route = []
    for low in range(count):
        high = low | 1 << distance
        if high != low and high < count:
            route += [(low, high), (high, low)]
    return lax.ppermute(block, axis, route)


def modulate(tokens, shift, scale):
    values = tokens.astype(jnp.float32)
    center = jnp.mean(values, axis=-1, keepdims=True)
    spread = jnp.mean(jnp.square(values - center), axis=-1, keepdims=True)
    normal = (values - center) * lax.rsqrt(spread + norm_eps)
    return (normal * (1.0 + scale) + shift).astype(jnp.bfloat16)


def slot_index(block_ids):
    flat_ids = block_ids.reshape(-1)
    one_hot = (flat_ids[:, None] == jnp.arange(EXPERTS, dtype=jnp.int32)[None, :]).astype(jnp.int32)
    earlier = jnp.cumsum(one_hot, axis=0, dtype=jnp.int32) - one_hot
    slots = jnp.sum(earlier * one_hot, axis=1, dtype=jnp.int32)
    return (flat_ids * CAP + slots).reshape(block_ids.shape)


def dispatch_rows(normed, flat_index):
    targets = jnp.arange(EXPERTS * CAP, dtype=jnp.int32)
    select = jnp.sum(
        (flat_index[None, :, :] == targets[:, None, None]).astype(jnp.int32),
        axis=2,
        dtype=jnp.int32,
    )
    return jnp.dot(select.astype(jnp.bfloat16), normed, preferred_element_type=jnp.float32).astype(
        jnp.bfloat16
    )


def combine(tokens, normed, gate_row, router_weight, block_ids, flat_index, expert_out):
    logits = jnp.dot(normed, router_weight, preferred_element_type=jnp.float32)
    picked = jnp.take_along_axis(logits, block_ids, axis=1)
    gap = picked[:, 0:1] - picked[:, 1:2]
    first = jnp.take(expert_out, flat_index[:, 0], axis=0).astype(jnp.float32)
    second = jnp.take(expert_out, flat_index[:, 1], axis=0).astype(jnp.float32)
    branch = jax.nn.sigmoid(gap) * first + jax.nn.sigmoid(-gap) * second
    return (tokens.astype(jnp.float32) + gate_row[None, :] * branch).astype(jnp.bfloat16)


def expert_compute(incoming, w_in, b_in, w_out):
    columns = incoming
    pre_act = jnp.einsum(
        "urd,udf->urf",
        columns,
        lax.all_gather(w_in, "fs", axis=1, tiled=True),
        preferred_element_type=jnp.float32,
    )
    hidden = jax.nn.gelu(pre_act + b_in[:, None, :], approximate=True).astype(jnp.bfloat16)
    columns = hidden
    produced = jnp.einsum(
        "urf,ufd->urd",
        columns,
        lax.all_gather(w_out, "fs", axis=1, tiled=True),
        preferred_element_type=jnp.float32,
    )
    return produced.astype(jnp.bfloat16)


def local(hidden_states, expert_ids, modulation, router_weight, w_in, b_in, w_out):
    token_count = hidden_states.shape[1]
    width = hidden_states.shape[2]
    tokens = hidden_states.reshape(token_count, width)
    block_ids = expert_ids.reshape(token_count, 2)
    settings = modulation[0]
    normed = modulate(tokens, settings[0][None, :], settings[1][None, :])
    flat_index = slot_index(block_ids)
    outgoing = dispatch_rows(normed, flat_index)
    per_expert = outgoing.reshape(EXPERTS, CAP, width)
    members = lax.axis_size("ep")
    local_units = w_in.shape[0]
    paired = local_units == 1
    half_cap = CAP // 2
    if paired:
        sending = per_expert.reshape(members, half_cap, width)
    else:
        sending = per_expert
    received = lax.all_to_all(sending, "ep", split_axis=0, concat_axis=1, tiled=True)
    if paired:
        parity = lax.axis_index("ep") % 2
        partner = swapped(received, "ep", 0)
        own_blocks = received.reshape(members, half_cap, width)
        other_blocks = partner.reshape(members, half_cap, width)
        lower = jnp.where(parity == 0, own_blocks, other_blocks)
        upper = jnp.where(parity == 0, other_blocks, own_blocks)
        incoming = jnp.stack([lower, upper], axis=1).reshape(1, members * CAP, width)
    else:
        incoming = jnp.repeat(received, SPLIT, axis=0)
    produced = expert_compute(incoming, w_in, b_in, w_out)
    if paired:
        halves = produced.reshape(members, 2, half_cap, width)
        kept_rows = jnp.where(parity == 0, halves[:, 0], halves[:, 1])
        given_rows = jnp.where(parity == 0, halves[:, 1], halves[:, 0])
        partner_out = swapped(given_rows, "ep", 0)
        reply = (kept_rows.astype(jnp.float32) + partner_out.astype(jnp.float32)).astype(
            jnp.bfloat16
        )
    else:
        local_experts = local_units // SPLIT
        summed = jnp.sum(
            produced.astype(jnp.float32).reshape(local_experts, SPLIT, members, CAP, width), axis=1
        )
        reply = (
            summed.astype(jnp.bfloat16)
            .transpose(1, 0, 2, 3)
            .reshape(members, local_experts * CAP, width)
        )
    returned = lax.all_to_all(reply, "ep", split_axis=0, concat_axis=0, tiled=True)
    expert_out = returned.reshape(EXPERTS, CAP, width)
    result = combine(
        tokens,
        normed,
        settings[2],
        router_weight,
        block_ids,
        flat_index,
        expert_out.reshape(EXPERTS * CAP, width),
    )
    return result.reshape(1, token_count, width)


def solution(mesh):
    placed = (
        P(("parts", "fs"), "ep", None),
        P(("parts", "fs"), "ep", None),
        P(("parts", "fs"), None, None),
        P(),
        P("ep", "fs", None),
        P("ep", None),
        P("ep", "fs", None),
    )
    return jax.shard_map(
        local, mesh=mesh, in_specs=placed, out_specs=P(("parts", "fs"), "ep", None), check_vma=False
    )
```

profile of v0, /device:TPU:0, one launch (start us, length us, event | category | flops | bytes accessed | tf_op | source)
XLA Modules:
  0.0 587.8 jit_solution(5534716679597151099)
XLA Ops:
  6.5 0.7 all-gather.3.cloned.1.call-update
  7.3 0.7 all-gather.5.cloned.1.call-update
  8.5 0.6 reduce-window.6
  9.6 0.6 slice_reduce_fusion.2
  10.4 0.2 fusion.12
  10.7 0.5 convolution_convert_fusion.1
  11.1 1.1 reshape.117
  12.2 6.3 %all-to-all-start = ((bf16[16,20,1152]{2,1,0:T(8,128)(2,1)}), bf16[16,20,1152]{2,1,0:T(8,128)(2,1)S(1)}, u32[]{:S(2)}, u32[]{:S(2)}) async-start(bf16[16,20,1152]{2,1,0:T(8,128)(2,1)} %reshape.117), calls=%async_computation | async-start | bytes 1769472 | tf_op jit(solution)/shard_map/all_to_all | solution.py:99
  18.6 0.9 fusion.32
  19.5 21.3 %all-to-all-done = bf16[16,20,1152]{2,1,0:T(8,128)(2,1)S(1)} async-done(((bf16[16,20,1152]{2,1,0:T(8,128)(2,1)}), bf16[16,20,1152]{2,1,0:T(8,128)(2,1)S(1)}, u32[]{:S(2)}, u32[]{:S(2)}) %all-to-all-start) | async-done | bytes 737312 | tf_op jit(solution)/shard_map/all_to_all | solution.py:99
  40.8 0.3 copy.63
  41.1 223.4 %all-gather.3.cloned.1.call-done = bf16[8,1152,2304]{2,1,0:T(8,128)(2,1)} async-done(((bf16[8,288,2304]{2,1,0:T(8,128)(2,1)}), bf16[8,1152,2304]{2,1,0:T(8,128)(2,1)}) %all-gather.3.cloned.1.call-update) | async-done | bytes 42467344 | tf_op jit(solution)/shard_map/all_gather | solution.py:67
  264.6 254.5 %all-gather.5.cloned.1.call-done = bf16[8,2304,1152]{2,1,0:T(8,128)(2,1)} async-done(((bf16[8,576,1152]{2,1,0:T(8,128)(2,1)}), bf16[8,2304,1152]{2,1,0:T(8,128)(2,1)}) %all-gather.5.cloned.1.call-update) | async-done | bytes 42467344 | tf_op jit(solution)/shard_map/all_gather | solution.py:75
  519.2 30.4 %convolution_convert_fusion = bf16[8,80,1152]{2,1,0:T(8,128)(2,1)} fusion(bf16[8,2304,1152]{2,1,0:T(8,128)(2,1)} %all-gather.5.cloned.1.call-done, bf16[8,80,1152]{2,1,0:T(8,128)(2,1)S(1)} %bitcast.85, bf16[8,1152,2304]{2,1,0:T(8,128)(2,1)} %all-gather.3.cloned.1.call-done, f32[8,2304]{1,0:T(8,128)S(1)} %copy-done.11), kind=kOutput, calls=%fused_computation.12 | convolution fusion | flops 6810255360 | bytes 87957504 | tf_op jit(solution)/shard_map/urf,ufd->urd/dot_general | solution.py:72
  549.6 2.3 reshape.151
  551.9 0.8 reduce.1
  552.7 0.3 copy.70
  553.0 0.9 copy.67
  554.0 4.6 all-to-all-start.1
  559.0 2.0 gather_fusion
  561.4 16.7 %all-to-all-done.1 = bf16[4,80,1152]{2,1,0:T(8,128)(2,1)S(1)} async-done(((bf16[4,80,1152]{2,1,0:T(8,128)(2,1)}), bf16[4,80,1152]{2,1,0:T(8,128)(2,1)S(1)}, u32[]{:S(2)}, u32[]{:S(2)}) %all-to-all-start.1) | async-done | bytes 737312 | tf_op jit(solution)/shard_map/all_to_all | solution.py:129
  578.0 0.9 gather_fusion.2
  578.9 0.9 gather_fusion.1
  579.9 1.1 fusion.17
  (55 shorter events, 2.1 us)
Async XLA Ops:
  6.5 12.0 %copy-start = (bf16[1152,16]{0,1:T(8,128)(2,1)S(1)}, bf16[1152,16]{0,1:T(8,128)(2,1)}, u32[]{:S(2)}) copy-start(bf16[1152,16]{0,1:T(8,128)(2,1)} %param.12) | copy-start | bytes 110596
  6.5 258.0 %all-gather.3.cloned.1.call-start = ((), (), s32[]{:S(2)}) async-start(), calls=%async_computation.2 | async-start | bytes 53084160 | tf_op jit(solution)/shard_map/all_gather | solution.py:67
  7.3 0.8 copy-start.6
  7.3 2.3 copy-start.8
  7.3 3.0 copy-start.3
  7.3 511.8 %all-gather.5.cloned.1.call-start = ((), (), s32[]{:S(2)}) async-start(), calls=%async_computation.3 | async-start | bytes 53084160 | tf_op jit(solution)/shard_map/all_gather | solution.py:75
  8.4 510.8 %copy-start.11 = (f32[8,2304]{1,0:T(8,128)S(1)}, f32[8,2304]{1,0:T(8,128)}, u32[]{:S(2)}) copy-start(f32[8,2304]{1,0:T(8,128)} %param.14) | copy-start | bytes 221188
  9.4 1.3 copy-start.9
  12.2 28.5 %all-to-all-start = ((bf16[16,20,1152]{2,1,0:T(8,128)(2,1)}), bf16[16,20,1152]{2,1,0:T(8,128)(2,1)S(1)}, u32[]{:S(2)}, u32[]{:S(2)}) async-start(bf16[16,20,1152]{2,1,0:T(8,128)(2,1)} %reshape.117), calls=%async_computation | async-start | bytes 1769472 | tf_op jit(solution)/shard_map/all_to_all | solution.py:99
  549.6 9.0 %copy-start.7 = (s32[1,128,2]{1,2,0:T(2,128)S(1)}, s32[1,128,2]{1,2,0:T(2,128)}, u32[]{:S(2)}) copy-start(s32[1,128,2]{1,2,0:T(2,128)} %param.10) | copy-start | bytes 3076
  549.6 9.0 %copy-start.10 = (s32[256]{0:T(256)S(1)}, s32[256]{0:T(256)}, u32[]{:S(2)}) copy-start(s32[256]{0:T(256)} %copy-done.9) | copy-start | bytes 3076
  549.6 9.4 %copy-start.2 = (f32[128,16]{0,1:T(8,128)S(1)}, f32[128,16]{0,1:T(8,128)}, u32[]{:S(2)}) copy-start(f32[128,16]{0,1:T(8,128)} %fusion.32) | copy-start | bytes 24580
  554.0 24.1 %all-to-all-start.1 = ((bf16[4,80,1152]{2,1,0:T(8,128)(2,1)}), bf16[4,80,1152]{2,1,0:T(8,128)(2,1)S(1)}, u32[]{:S(2)}, u32[]{:S(2)}) async-start(bf16[4,80,1152]{2,1,0:T(8,128)(2,1)} %copy.67), calls=%async_computation.1 | async-start | bytes 1474560 | tf_op jit(solution)/shard_map/all_to_all | solution.py:129
  559.0 20.9 %copy-start.4 = (bf16[1,128,1152]{2,1,0:T(8,128)(2,1)S(1)}, bf16[1,128,1152]{2,1,0:T(8,128)(2,1)}, u32[]{:S(2)}) copy-start(bf16[1,128,1152]{2,1,0:T(8,128)(2,1)} %param.9) | copy-start | bytes 884740
  559.0 20.9 %copy-start.5 = (f32[1152]{0:T(1024)S(1)}, f32[1152]{0:T(1024)}, u32[]{:S(2)}) copy-start(f32[1152]{0:T(1024)} %get-tuple-element.6) | copy-start | bytes 13828
  559.0 22.0 %copy-start.1 = (bf16[1152,16]{0,1:T(8,128)(2,1)S(1)}, bf16[1152,16]{0,1:T(8,128)(2,1)}, u32[]{:S(2)}) copy-start(bf16[1152,16]{0,1:T(8,128)(2,1)} %param.12) | copy-start | bytes 110596
Sparse Core Ops, SparseCore 0:
  8.9 255.5 all-gather.2
  266.1 252.9 all-gather.4
where the time goes:
time: 588 us
  waiting for transfers between devices  517 us (88%)
  matrix products  31.7 us (5%)
  between operations  13.7 us (2%)
  starting transfers between devices  11 us (2%)
  local copies, waits for them, and re-layouts  10.3 us (2%)
    all_gather x1, waiting for transfers between devices, expert_compute(): lax.all_gather(w_out, 'fs', axis=1, tiled=True)  255 us
    all_gather x1, waiting for transfers between devices, expert_compute(): lax.all_gather(w_in, 'fs', axis=1, tiled=True)  223 us
    dot_general x1, matrix products, expert_compute(): jnp.einsum('urf,ufd->urd', columns, lax.all_gather(w_out, 'fs', axis=1, t...  30.4 us
    all_to_all x1, waiting for transfers between devices, local(): lax.all_to_all(sending, 'ep', split_axis=0, concat_axis=1, tiled=True)  21.3 us
    all_to_all x1, waiting for transfers between devices, local(): lax.all_to_all(reply, 'ep', split_axis=0, concat_axis=0, tiled=True)  16.7 us
  transfers between devices with their start and end apart: 4, of which 4 were waited for; matrix products, arithmetic and copies ran while one was open for 1% of the time, Pallas kernels for 0%

commit v1 on v0

--- a/solution.py
+++ b/solution.py
@@ -1,6 +1,10 @@
+import functools
+
 import jax
 import jax.numpy as jnp
 from jax import lax
+from jax.experimental import pallas as pl
+from jax.experimental.pallas import tpu as pltpu
 from jax.sharding import PartitionSpec as P
 
 EXPERTS = 16
@@ -78,7 +82,9 @@
     return produced.astype(jnp.bfloat16)
 
 
-def local(hidden_states, expert_ids, modulation, router_weight, w_in, b_in, w_out):
+def gathered_weights(
+    hidden_states, expert_ids, modulation, router_weight, w_in, b_in, w_out
+):
     token_count = hidden_states.shape[1]
     width = hidden_states.shape[2]
     tokens = hidden_states.reshape(token_count, width)
@@ -140,6 +146,184 @@
     return result.reshape(1, token_count, width)
 
 
+def expert_kernel(
+    place_ref, x_ref, own_ref, near_ref, far0_ref, far1_ref, cross_ref, b_ref, out_w_ref,
+    keep_ref, send_ref, weight, total,
+):
+    step = pl.program_id(0)
+    here, core = place_ref[0], place_ref[2]
+    depth, columns = own_ref.shape[1], own_ref.shape[2]
+
+    def rows(device):
+        return pl.ds(pl.multiple_of(device * depth, depth), depth)
+
+    weight[rows(here), :] = own_ref[0]
+    weight[rows(here ^ 1), :] = near_ref[0]
+    weight[rows(here ^ 3), :] = cross_ref[0]
+    for number, far_ref in enumerate((far0_ref, far1_ref)):
+        for half in range(2):
+
+            @pl.when((step == number) & (core == half))
+            def _(far_ref=far_ref, half=half):
+                weight[rows(here ^ 2), :] = far_ref[0, :, half * columns : (half + 1) * columns]
+
+    x = x_ref[...].reshape(-1, x_ref.shape[-1])
+    pre = jnp.dot(x, weight[...], preferred_element_type=jnp.float32) + b_ref[0]
+    hidden = jax.nn.gelu(pre, approximate=True).astype(jnp.bfloat16)
+    piece = jnp.dot(hidden, out_w_ref[0], preferred_element_type=jnp.float32)
+    half_rows = piece.shape[0] // 2
+
+    @pl.when(step == 0)
+    def _():
+        total[...] = piece
+
+    @pl.when(step == 1)
+    def _():
+        keep_ref[...] = total[:half_rows, :] + piece[:half_rows, :]
+        send_ref[...] = (total[half_rows:, :] + piece[half_rows:, :]).astype(jnp.bfloat16)
+
+
+def expert_call(expert, place, x, own, near, far0, far1, cross, b, w_out):
+    images, _, rows, width = x.shape
+    _, depth, columns = own.shape
+    all_rows = images * rows
+
+    def unit(step, place):
+        return SPLIT * expert + (step ^ place[1])
+
+    return pl.pallas_call(
+        expert_kernel,
+        grid_spec=pltpu.PrefetchScalarGridSpec(
+            num_scalar_prefetch=1,
+            grid=(SPLIT,),
+            in_specs=[
+                pl.BlockSpec((images, 1, rows, width), lambda s, p: (0, expert, 0, 0)),
+                pl.BlockSpec((1, depth, columns), lambda s, p: (unit(s, p), 0, 0)),
+                pl.BlockSpec((1, depth, columns), lambda s, p: (unit(s, p), 0, 0)),
+                pl.BlockSpec((1, depth, 2 * columns), lambda s, p: (0, 0, 0)),
+                pl.BlockSpec((1, depth, 2 * columns), lambda s, p: (0, 0, 0)),
+                pl.BlockSpec((1, depth, columns), lambda s, p: (s, 0, 0)),
+                pl.BlockSpec((1, 1, columns), lambda s, p: (unit(s, p), 0, 0)),
+                pl.BlockSpec((1, columns, width), lambda s, p: (unit(s, p), 0, 0)),
+            ],
+            out_specs=[
+                pl.BlockSpec((all_rows // 2, width), lambda s, p: (0, 0)),
+                pl.BlockSpec((all_rows // 2, width), lambda s, p: (0, 0)),
+            ],
+            scratch_shapes=[
+                pltpu.VMEM((width, columns), jnp.bfloat16),
+                pltpu.VMEM((all_rows, width), jnp.float32),
+            ],
+        ),
+        out_shape=[
+            jax.ShapeDtypeStruct((all_rows // 2, width), jnp.float32),
+            jax.ShapeDtypeStruct((all_rows // 2, width), jnp.bfloat16),
+        ],
+        compiler_params=pltpu.CompilerParams(vmem_limit_bytes=40 << 20),
+        cost_estimate=pl.CostEstimate(
+            flops=2 * SPLIT * 2 * all_rows * width * columns,
+            bytes_accessed=2 * SPLIT * 2 * width * columns + 8 * all_rows * width,
+            transcendentals=SPLIT * all_rows * columns,
+        ),
+        name="expert",
+    )(place, x, own, near, far0, far1, cross, b, w_out)
+
+
+def recut_weights(hidden_states, expert_ids, modulation, router_weight, w_in, b_in, w_out):
+    token_count, width = hidden_states.shape[1:]
+    units, depth, _ = w_in.shape
+    columns = w_out.shape[1]
+    experts = units // SPLIT
+    members = lax.axis_size("ep")
+    here, part = lax.axis_index("fs"), lax.axis_index("parts")
+    core, chip = here & 1, here >> 1
+    place = jnp.stack([here, part, core]).astype(jnp.int32)
+
+    far = []
+    for expert in range(experts):
+        block = lax.dynamic_slice(
+            w_in,
+            (SPLIT * expert + part, 0, (1 - chip) * 2 * columns),
+            (1, depth, 2 * columns),
+        )
+        far.append(swapped(block, "fs", 1))
+    near = swapped(
+        lax.dynamic_slice(w_in, (0, 0, (here ^ 1) * columns), (units, depth, columns)), "fs", 0
+    )
+    own = lax.dynamic_slice(w_in, (0, 0, here * columns), (units, depth, columns))
+    other = [swapped(block, "parts", 0) for block in far]
+    cross = [
+        swapped(
+            lax.dynamic_slice(
+                jnp.concatenate([far[e], other[e]]),
+                (0, 0, (1 - core) * columns),
+                (SPLIT, depth, columns),
+            ),
+            "fs",
+            0,
+        )
+        for e in range(experts)
+    ]
+    own_b = lax.dynamic_slice(b_in, (0, here * columns), (units, columns))[:, None, :]
+
+    tokens = hidden_states.reshape(token_count, width)
+    block_ids = expert_ids.reshape(token_count, 2)
+    settings = modulation[0]
+    normed = modulate(tokens, settings[0][None, :], settings[1][None, :])
+    flat_index = slot_index(block_ids)
+    listed = lax.all_gather(flat_index.T, ("fs", "ep"), axis=0, tiled=False)
+    listed = listed.reshape(-1, members, 2, token_count)
+    order = here ^ jnp.array([0, 2, 1, 3], jnp.int32)
+    listed = jnp.take(listed, order, axis=0).transpose(0, 2, 1, 3).reshape(4, 2, 1, -1)
+    opposite = swapped(normed, "fs", 1)
+    mine = lax.all_gather(normed, "ep", axis=0, tiled=True)
+    theirs = lax.all_gather(opposite, "ep", axis=0, tiled=True)
+    same_core = jnp.stack([mine, theirs])
+    other_core = swapped(same_core, "fs", 0)
+    everyone = jnp.concatenate([same_core, other_core])
+    target = jnp.arange(experts * members * CAP, dtype=jnp.int32)[:, None]
+    owner = lax.axis_index("ep") * experts + target // (members * CAP)
+    wanted = owner * CAP + target % CAP
+    block_of = jnp.arange(members * token_count, dtype=jnp.int32)[None, :] // token_count
+    in_block = (target // CAP) % members == block_of
+    select = ((listed[:, 0] == wanted) | (listed[:, 1] == wanted)) & in_block
+    x = jnp.einsum(
+        "irt,itd->ird",
+        select.astype(jnp.bfloat16),
+        everyone,
+        preferred_element_type=jnp.float32,
+    ).astype(jnp.bfloat16)
+    x = x.reshape(4, experts, members * CAP, width)
+
+    returned = []
+    for e in range(experts):
+        keep, send = expert_call(
+            e, place, x, own, near, far[e], other[e], cross[e], own_b, w_out
+        )
+        half = keep + swapped(send, "fs", 0).astype(jnp.float32)
+        rows = members * CAP
+        across = swapped(half[rows:].astype(jnp.bfloat16), "fs", 1)
+        whole = (half[:rows] + across.astype(jnp.float32)).astype(jnp.bfloat16)
+        returned.append(
+            lax.all_to_all(
+                whole.reshape(members, CAP, width), "ep", split_axis=0, concat_axis=0, tiled=True
+            )
+        )
+    expert_out = jnp.stack(returned, axis=1).reshape(EXPERTS * CAP, width)
+    result = combine(
+        tokens, normed, settings[2], router_weight, block_ids, flat_index, expert_out
+    )
+    return result.reshape(1, token_count, width)
+
+
+def local(*arrays):
+    w_in = arrays[4]
+    recut = (
+        lax.axis_size("fs") == 4 and lax.axis_size("parts") == 2 and w_in.shape[0] % SPLIT == 0
+    )
+    return (recut_weights if recut else gathered_weights)(*arrays)
+
+
 def solution(mesh):
     placed = (
         P(("parts", "fs"), "ep", None),

time: 588 us -> 235 us (0.40)
  waiting for transfers between devices: 517 us -> 86.4 us
  blocking collectives: 0 us -> 31.9 us
  matrix products: 31.7 us -> 3.79 us
  Pallas kernels: 0 us -> 24.9 us
  starting transfers between devices: 11 us -> 33.5 us
  other arithmetic: 3.77 us -> 17.9 us
  local copies, waits for them, and re-layouts: 10.3 us -> 22 us
    all_gather x2, waiting for transfers between devices: 478 us -> 4.18 us  [the longest x1 4.18 us: recut_weights(): theirs = lax.all_gather(opposite, 'ep', axis=0, tiled=True)]
    ppermute x0 -> x23, waiting for transfers between devices: none -> 59.9 us  [swapped(): return lax.ppermute(block, axis, route)]
    all_gather x0 -> x1, blocking collectives: none -> 31.9 us  [recut_weights(): listed = lax.all_gather(flat_index.T, ('fs', 'ep'), axis=0, tiled=False)]
    dot_general x2 -> x1, matrix products: 30.8 us -> 3.63 us  [recut_weights(): jnp.einsum('irt,itd->ird', select.astype(jnp.bfloat16), everyone, preferr...]
    pallas_call x0 -> x4, Pallas kernels: none -> 24.9 us  [expert_call(): pl.pallas_call(expert_kernel, grid_spec=pltpu.PrefetchScalarGridSpec(num_...]
    ppermute x0 -> x23, starting transfers between devices: none -> 19.9 us  [swapped(): return lax.ppermute(block, axis, route)]
    all_to_all x2 -> x4, waiting for transfers between devices: 38 us -> 22.3 us  [recut_weights(): lax.all_to_all(whole.reshape(members, CAP, width), 'ep', split_axis=0, co...]
    dynamic_slice x0 -> x3, local copies, waits for them, and re-layouts: none -> 11.7 us  [the longest x1 8.33 us: recut_weights(): lax.dynamic_slice(w_in, (0, 0, (here ^ 1) * columns), (units, depth, colu...]
  transfers between devices with their start and end apart: 4 -> 29, of which waited for: 4 -> 12; matrix products, arithmetic and copies ran while one was open for 1% -> 15% of each run, Pallas kernels for 0% -> 11%
where the time goes in v1:
time: 235 us; the launch traced here: 234 us
  waiting for transfers between devices  86.4 us (37%)
  starting transfers between devices  33.5 us (14%)
  blocking collectives  31.9 us (14%)
  Pallas kernels  24.9 us (11%)
  local copies, waits for them, and re-layouts  22 us (9%)
  other arithmetic  17.9 us (8%)
  between operations  13.8 us (6%)
  matrix products  3.79 us (2%)
    ppermute x23, waiting for transfers between devices, swapped(): return lax.ppermute(block, axis, route)  59.9 us
    all_gather x1, blocking collectives, recut_weights(): listed = lax.all_gather(flat_index.T, ('fs', 'ep'), axis=0, tiled=False)  31.9 us
    pallas_call x4, Pallas kernels, expert_call(): pl.pallas_call(expert_kernel, grid_spec=pltpu.PrefetchScalarGridSpec(num_...  24.9 us
    all_to_all x4, waiting for transfers between devices, recut_weights(): lax.all_to_all(whole.reshape(members, CAP, width), 'ep', split_axis=0, co...  22.3 us
    ppermute x23, starting transfers between devices, swapped(): return lax.ppermute(block, axis, route)  19.9 us
    all_to_all x4, starting transfers between devices, recut_weights(): lax.all_to_all(whole.reshape(members, CAP, width), 'ep', split_axis=0, co...  13.5 us
    dynamic_slice x1, local copies, waits for them, and re-layouts, recut_weights(): lax.dynamic_slice(w_in, (0, 0, (here ^ 1) * columns), (units, depth, colu...  8.33 us
    concatenate x4, other arithmetic, recut_weights(): jnp.concatenate([far[e], other[e]])  5.75 us
  transfers between devices with their start and end apart: 29, of which 12 were waited for; matrix products, arithmetic and copies ran while one was open for 15% of the time, Pallas kernels for 11%

profile of v1, /device:TPU:0, one launch (start us, length us, event | category | flops | bytes accessed | tf_op | source)
XLA Modules:
  0.0 234.2 jit_solution(713699030417492621)
XLA Ops:
  11.6 3.0 %collective-permute-start = (bf16[128,1152]{1,0:T(8,128)(2,1)}, bf16[128,1152]{1,0:T(8,128)(2,1)S(1)}, u32[]{:S(2)}, u32[]{:S(2)}) collective-permute-start(bf16[128,1152]{1,0:T(8,128)(2,1)} %fusion.28), channel_id=1, source_target_pairs={{0,2},{2,0},{1,3},{3,1},{4,6},{6,4},{5,7},{7,5},{8,10},{10,8},{9,1... | collective-permute-start | bytes 884744 | tf_op jit(solution)/shard_map/ppermute | solution.py:25
  14.6 7.2 %collective-permute-done = bf16[128,1152]{1,0:T(8,128)(2,1)S(1)} collective-permute-done((bf16[128,1152]{1,0:T(8,128)(2,1)}, bf16[128,1152]{1,0:T(8,128)(2,1)S(1)}, u32[]{:S(2)}, u32[]{:S(2)}) %collective-permute-start) | collective-permute-done | bytes 294944 | tf_op jit(solution)/shard_map/ppermute | solution.py:25
  22.6 8.3 %constant_dynamic-slice_fusion.5 = (bf16[8,288,576]{2,1,0:T(8,128)(2,1)}, bf16[8,288,576]{2,1,0:T(8,128)(2,1)S(1)}) fusion(bf16[8,288,2304]{2,1,0:T(8,128)(2,1)} %param.14, s32[]{:T(128)S(6)} %select_n.133, s32[]{:T(128)S(6)} %select_n.132), kind=kLoop, calls=%fused_computation.93 | loop fusion | bytes 10616840 | tf_op jit(solution)/shard_map/dynamic_slice | solution.py:251
  30.9 3.3 %constant_dynamic-slice_fusion.4 = (bf16[1,288,1152]{2,1,0:T(8,128)(2,1)}, bf16[1,288,1152]{2,1,0:T(8,128)(2,1)}, bf16[1,288,1152]{2,1,0:T(8,128)(2,1)}, bf16[1,288,1152]{2,1,0:T(8,128)(2,1)}) fusion(bf16[8,288,2304]{2,1,0:T(8,128)(2,1)} %param.14, s32[]{:T(128)S(6)} %select_n.134, s32[]{:T(128)S(6)} %select_n.135, s32[]{:T(128)S(6)} %select_n.137, ...), kind=kLoop, calls=%fused_computation.92 | loop fusion | bytes 5308436 | tf_op jit(solution)/shard_map/dynamic_slice | solution.py:244
  39.4 31.9 %all-gather.1 = s32[16,2,128]{2,1,0:T(2,128)S(1)} all-gather(s32[1,2,128]{2,1,0:T(2,128)S(1)} %bitcast.97), channel_id=2, replica_groups=mesh['parts'=2,'ep'=4,'fs'=4] {'fs','ep'}, dimensions={0}, use_global_device_ids=true | all-gather | bytes 17408 | tf_op jit(solution)/shard_map/all_gather | solution.py:274
  72.1 4.2 %all-gather.7.cloned.1.call-done = bf16[512,1152]{1,0:T(8,128)(2,1)} async-done(((bf16[128,1152]{1,0:T(8,128)(2,1)}), bf16[512,1152]{1,0:T(8,128)(2,1)}) %all-gather.7.cloned.1.call-update) | async-done | bytes 1179664 | tf_op jit(solution)/shard_map/all_gather | solution.py:280
  76.3 3.4 %pad_maximum_fusion = bf16[2,512,1152]{2,1,0:T(8,128)(2,1)} fusion(bf16[1,512,1152]{2,1,0:T(8,128)(2,1)} %bitcast.90, bf16[1,512,1152]{2,1,0:T(8,128)(2,1)} %bitcast.88), kind=kLoop, calls=%fused_computation.15 | loop fusion | flops 1179648 | bytes 4718592 | tf_op jit(solution)/shard_map/stack | solution.py:281
  85.9 13.9 %collective-permute-done.3.far0_ref = bf16[1,288,1152]{2,1,0:T(8,128)(2,1)} collective-permute-done((bf16[1,288,1152]{2,1,0:T(8,128)(2,1)}, bf16[1,288,1152]{2,1,0:T(8,128)(2,1)}, u32[]{:S(2)}, u32[]{:S(2)}) %collective-permute-start.3) | collective-permute-done | bytes 663584 | tf_op jit(solution)/shard_map/ppermute | solution.py:25
  105.0 11.0 %collective-permute-done.14.far1_ref = bf16[1,288,1152]{2,1,0:T(8,128)(2,1)} collective-permute-done((bf16[1,288,1152]{2,1,0:T(8,128)(2,1)}, bf16[1,288,1152]{2,1,0:T(8,128)(2,1)}, u32[]{:S(2)}, u32[]{:S(2)}) %collective-permute-start.14) | collective-permute-done | bytes 663584 | tf_op jit(solution)/shard_map/ppermute | solution.py:25
  117.5 12.8 %collective-permute-done.9.far1_ref = bf16[1,288,1152]{2,1,0:T(8,128)(2,1)} collective-permute-done((bf16[1,288,1152]{2,1,0:T(8,128)(2,1)}, bf16[1,288,1152]{2,1,0:T(8,128)(2,1)}, u32[]{:S(2)}, u32[]{:S(2)}) %collective-permute-start.9) | collective-permute-done | bytes 663584 | tf_op jit(solution)/shard_map/ppermute | solution.py:25
  131.7 12.1 %collective-permute-done.4.far1_ref = bf16[1,288,1152]{2,1,0:T(8,128)(2,1)} collective-permute-done((bf16[1,288,1152]{2,1,0:T(8,128)(2,1)}, bf16[1,288,1152]{2,1,0:T(8,128)(2,1)}, u32[]{:S(2)}, u32[]{:S(2)}) %collective-permute-start.4) | collective-permute-done | bytes 663584 | tf_op jit(solution)/shard_map/ppermute | solution.py:25
  145.9 3.6 %fusion.6 = bf16[4,320,1152]{2,1,0:T(8,128)(2,1)S(1)} fusion(bf16[2,512,1152]{2,1,0:T(8,128)(2,1)} %collective-permute-done.1, bf16[1,512,1152]{2,1,0:T(8,128)(2,1)S(1)} %bitcast.91, bf16[1,512,1152]{2,1,0:T(8,128)(2,1)S(1)} %bitcast.89, s32[4,512]{1,0:T(4,128)S(1)} %get-tuple-element.45, s32[4,512]{1,0:T(4,128)S(1)} %get-tuple-element.46, ...), kind=kOutput, calls=%fused_computation.10 | convolution fusion | flops 1518764032 | bytes 7849216 | tf_op jit(solution)/shard_map/irt,itd->ird/dot_general | solution.py:290
  149.6 6.2 %expert.7 = (f32[160,1152]{1,0:T(8,128)S(1)}, bf16[160,1152]{1,0:T(8,128)(2,1)S(1)}) custom-call(s32[3]{0:T(128)S(1)} %pad_add_fusion.place_ref, bf16[4,4,80,1152]{3,2,1,0:T(8,128)(2,1)S(1)} %bitcast.84, bf16[8,288,576]{2,1,0:T(8,128)(2,1)S(1)} %get-tuple-element.36.own_ref, bf16[8,288,576]{2,1,0:T(8,128)(2,1)} %collective-permute-done.2.near_ref, ...), custom_call_target="tpu_custom_call" | custom-call | flops 1698693120 | bytes 8257536 | tf_op jit(solution)/shard_map/expert/pallas_call | solution.py:194
  156.1 6.2 %expert.6 = (f32[160,1152]{1,0:T(8,128)S(1)}, bf16[160,1152]{1,0:T(8,128)(2,1)S(1)}) custom-call(s32[3]{0:T(128)S(1)} %pad_add_fusion.place_ref, bf16[4,4,80,1152]{3,2,1,0:T(8,128)(2,1)S(1)} %bitcast.85, bf16[8,288,576]{2,1,0:T(8,128)(2,1)S(1)} %get-tuple-element.36.own_ref, bf16[8,288,576]{2,1,0:T(8,128)(2,1)} %collective-permute-done.2.near_ref, ...), custom_call_target="tpu_custom_call" | custom-call | flops 1698693120 | bytes 8257536 | tf_op jit(solution)/shard_map/expert/pallas_call | solution.py:194
  162.9 6.2 %expert.5 = (f32[160,1152]{1,0:T(8,128)S(1)}, bf16[160,1152]{1,0:T(8,128)(2,1)S(1)}) custom-call(s32[3]{0:T(128)S(1)} %pad_add_fusion.place_ref, bf16[4,4,80,1152]{3,2,1,0:T(8,128)(2,1)S(1)} %bitcast.86, bf16[8,288,576]{2,1,0:T(8,128)(2,1)S(1)} %get-tuple-element.36.own_ref, bf16[8,288,576]{2,1,0:T(8,128)(2,1)} %collective-permute-done.2.near_ref, ...), custom_call_target="tpu_custom_call" | custom-call | flops 1698693120 | bytes 8257536 | tf_op jit(solution)/shard_map/expert/pallas_call | solution.py:194
  169.5 6.4 %expert.4 = (f32[160,1152]{1,0:T(8,128)S(1)}, bf16[160,1152]{1,0:T(8,128)(2,1)S(1)}) custom-call(s32[3]{0:T(128)S(1)} %pad_add_fusion.place_ref, bf16[4,4,80,1152]{3,2,1,0:T(8,128)(2,1)S(1)} %bitcast.87, bf16[8,288,576]{2,1,0:T(8,128)(2,1)S(1)} %get-tuple-element.36.own_ref, bf16[8,288,576]{2,1,0:T(8,128)(2,1)} %collective-permute-done.2.near_ref, ...), custom_call_target="tpu_custom_call" | custom-call | flops 1698693120 | bytes 8257536 | tf_op jit(solution)/shard_map/expert/pallas_call | solution.py:194
  184.9 3.4 %all-to-all-start.3 = ((bf16[4,20,1152]{2,1,0:T(8,128)(2,1)}), bf16[4,20,1152]{2,1,0:T(8,128)(2,1)S(1)}, u32[]{:S(2)}, u32[]{:S(2)}) async-start(bf16[4,20,1152]{2,1,0:T(8,128)(2,1)} %reshape.283), calls=%async_computation.3 | async-start | bytes 442368 | tf_op jit(solution)/shard_map/all_to_all | solution.py:308
  189.9 4.7 %all-to-all-done.3 = bf16[4,20,1152]{2,1,0:T(8,128)(2,1)S(1)} async-done(((bf16[4,20,1152]{2,1,0:T(8,128)(2,1)}), bf16[4,20,1152]{2,1,0:T(8,128)(2,1)S(1)}, u32[]{:S(2)}, u32[]{:S(2)}) %all-to-all-start.3) | async-done | bytes 184352 | tf_op jit(solution)/shard_map/all_to_all | solution.py:308
  194.7 3.4 %all-to-all-start.2 = ((bf16[4,20,1152]{2,1,0:T(8,128)(2,1)}), bf16[4,20,1152]{2,1,0:T(8,128)(2,1)S(1)}, u32[]{:S(2)}, u32[]{:S(2)}) async-start(bf16[4,20,1152]{2,1,0:T(8,128)(2,1)} %reshape.282), calls=%async_computation.2 | async-start | bytes 442368 | tf_op jit(solution)/shard_map/all_to_all | solution.py:308
  198.8 5.6 %all-to-all-done.2 = bf16[4,20,1152]{2,1,0:T(8,128)(2,1)S(1)} async-done(((bf16[4,20,1152]{2,1,0:T(8,128)(2,1)}), bf16[4,20,1152]{2,1,0:T(8,128)(2,1)S(1)}, u32[]{:S(2)}, u32[]{:S(2)}) %all-to-all-start.2) | async-done | bytes 184352 | tf_op jit(solution)/shard_map/all_to_all | solution.py:308
  204.5 3.4 %all-to-all-start.1 = ((bf16[4,20,1152]{2,1,0:T(8,128)(2,1)}), bf16[4,20,1152]{2,1,0:T(8,128)(2,1)S(1)}, u32[]{:S(2)}, u32[]{:S(2)}) async-start(bf16[4,20,1152]{2,1,0:T(8,128)(2,1)} %reshape.281), calls=%async_computation.1 | async-start | bytes 442368 | tf_op jit(solution)/shard_map/all_to_all | solution.py:308
  208.6 5.6 %all-to-all-done.1 = bf16[4,20,1152]{2,1,0:T(8,128)(2,1)S(1)} async-done(((bf16[4,20,1152]{2,1,0:T(8,128)(2,1)}), bf16[4,20,1152]{2,1,0:T(8,128)(2,1)S(1)}, u32[]{:S(2)}, u32[]{:S(2)}) %all-to-all-start.1) | async-done | bytes 184352 | tf_op jit(solution)/shard_map/all_to_all | solution.py:308
  214.3 3.4 %all-to-all-start = ((bf16[4,20,1152]{2,1,0:T(8,128)(2,1)}), bf16[4,20,1152]{2,1,0:T(8,128)(2,1)S(1)}, u32[]{:S(2)}, u32[]{:S(2)}) async-start(bf16[4,20,1152]{2,1,0:T(8,128)(2,1)} %reshape.280), calls=%async_computation | async-start | bytes 442368 | tf_op jit(solution)/shard_map/all_to_all | solution.py:308
  217.7 6.4 %all-to-all-done = bf16[4,20,1152]{2,1,0:T(8,128)(2,1)S(1)} async-done(((bf16[4,20,1152]{2,1,0:T(8,128)(2,1)}), bf16[4,20,1152]{2,1,0:T(8,128)(2,1)S(1)}, u32[]{:S(2)}, u32[]{:S(2)}) %all-to-all-start) | async-done | bytes 184352 | tf_op jit(solution)/shard_map/all_to_all | solution.py:308
  (134 shorter events, 44.8 us)
Async XLA Ops:
  6.5 65.5 %all-gather.5.cloned.1.call-start = ((), (), s32[]{:S(2)}) async-start(), calls=%async_computation.4 | async-start | bytes 1474560 | tf_op jit(solution)/shard_map/all_gather | solution.py:279
  11.6 64.7 %all-gather.7.cloned.1.call-start = ((), (), s32[]{:S(2)}) async-start(), calls=%async_computation.5 | async-start | bytes 1474560 | tf_op jit(solution)/shard_map/all_gather | solution.py:280
  11.6 10.2 %collective-permute-start = (bf16[128,1152]{1,0:T(8,128)(2,1)}, bf16[128,1152]{1,0:T(8,128)(2,1)S(1)}, u32[]{:S(2)}, u32[]{:S(2)}) collective-permute-start(bf16[128,1152]{1,0:T(8,128)(2,1)} %fusion.28), channel_id=1, source_target_pairs={{0,2},{2,0},{1,3},{3,1},{4,6},{6,4},{5,7},{7,5},{8,10},{10,8},{9,1... | collective-permute-start | bytes 884744 | tf_op jit(solution)/shard_map/ppermute | solution.py:25
  30.9 118.6 %collective-permute-start.2 = (bf16[8,288,576]{2,1,0:T(8,128)(2,1)}, bf16[8,288,576]{2,1,0:T(8,128)(2,1)}, u32[]{:S(2)}, u32[]{:S(2)}) collective-permute-start(bf16[8,288,576]{2,1,0:T(8,128)(2,1)} %get-tuple-element.35), channel_id=1, source_target_pairs={{0,1},{1,0},{2,3},{3,2},{4,5},{5,4},{6,7},{7,6},{8,9},{9,8},{10,11... | collective-permute-start | bytes 7962632 | tf_op jit(solution)/shard_map/ppermute | solution.py:25
  34.3 47.9 %collective-permute-start.18 = (bf16[1,288,1152]{2,1,0:T(8,128)(2,1)}, bf16[1,288,1152]{2,1,0:T(8,128)(2,1)}, u32[]{:S(2)}, u32[]{:S(2)}) collective-permute-start(bf16[1,288,1152]{2,1,0:T(8,128)(2,1)} %get-tuple-element.33), channel_id=1, source_target_pairs={{0,2},{2,0},{1,3},{3,1},{4,6},{6,4},{5,7},{7,5},{8,10},{10,8},{9,1... | collective-permute-start | bytes 1990664 | tf_op jit(solution)/shard_map/ppermute | solution.py:25
  35.8 48.0 %collective-permute-start.13 = (bf16[1,288,1152]{2,1,0:T(8,128)(2,1)}, bf16[1,288,1152]{2,1,0:T(8,128)(2,1)}, u32[]{:S(2)}, u32[]{:S(2)}) collective-permute-start(bf16[1,288,1152]{2,1,0:T(8,128)(2,1)} %get-tuple-element.34), channel_id=1, source_target_pairs={{0,2},{2,0},{1,3},{3,1},{4,6},{6,4},{5,7},{7,5},{8,10},{10,8},{9,1... | collective-permute-start | bytes 1990664 | tf_op jit(solution)/shard_map/ppermute | solution.py:25
  36.3 49.0 %collective-permute-start.8 = (bf16[1,288,1152]{2,1,0:T(8,128)(2,1)}, bf16[1,288,1152]{2,1,0:T(8,128)(2,1)}, u32[]{:S(2)}, u32[]{:S(2)}) collective-permute-start(bf16[1,288,1152]{2,1,0:T(8,128)(2,1)} %get-tuple-element.32), channel_id=1, source_target_pairs={{0,2},{2,0},{1,3},{3,1},{4,6},{6,4},{5,7},{7,5},{8,10},{10,8},{9,1... | collective-permute-start | bytes 1990664 | tf_op jit(solution)/shard_map/ppermute | solution.py:25
  79.6 65.7 %collective-permute-start.1 = (bf16[2,512,1152]{2,1,0:T(8,128)(2,1)}, bf16[2,512,1152]{2,1,0:T(8,128)(2,1)}, u32[]{:S(2)}, u32[]{:S(2)}) collective-permute-start(bf16[2,512,1152]{2,1,0:T(8,128)(2,1)} %pad_maximum_fusion), channel_id=1, source_target_pairs={{0,1},{1,0},{2,3},{3,2},{4,5},{5,4},{6,7},{7,6},{8,9},{9,8},{10,11... | collective-permute-start | bytes 7077896 | tf_op jit(solution)/shard_map/ppermute | solution.py:25
  82.2 17.7 %collective-permute-start.3 = (bf16[1,288,1152]{2,1,0:T(8,128)(2,1)}, bf16[1,288,1152]{2,1,0:T(8,128)(2,1)}, u32[]{:S(2)}, u32[]{:S(2)}) collective-permute-start(bf16[1,288,1152]{2,1,0:T(8,128)(2,1)} %get-tuple-element.31), channel_id=1, source_target_pairs={{0,2},{2,0},{1,3},{3,1},{4,6},{6,4},{5,7},{7,5},{8,10},{10,8},{9,1... | collective-permute-start | bytes 1990664 | tf_op jit(solution)/shard_map/ppermute | solution.py:25
  83.8 18.1 %collective-permute-start.19 = (bf16[1,288,1152]{2,1,0:T(8,128)(2,1)}, bf16[1,288,1152]{2,1,0:T(8,128)(2,1)}, u32[]{:S(2)}, u32[]{:S(2)}) collective-permute-start(bf16[1,288,1152]{2,1,0:T(8,128)(2,1)} %collective-permute-done.18.far0_ref), channel_id=1, source_target_pairs={{0,16},{16,0},{1,17},{17,1},{2,18},{18,2},{3,19},{19,3},{4,20},{20... | collective-permute-start | bytes 1990664 | tf_op jit(solution)/shard_map/ppermute | solution.py:25
  85.3 30.8 %collective-permute-start.14 = (bf16[1,288,1152]{2,1,0:T(8,128)(2,1)}, bf16[1,288,1152]{2,1,0:T(8,128)(2,1)}, u32[]{:S(2)}, u32[]{:S(2)}) collective-permute-start(bf16[1,288,1152]{2,1,0:T(8,128)(2,1)} %collective-permute-done.13.far0_ref), channel_id=1, source_target_pairs={{0,16},{16,0},{1,17},{17,1},{2,18},{18,2},{3,19},{19,3},{4,20},{20... | collective-permute-start | bytes 1990664 | tf_op jit(solution)/shard_map/ppermute | solution.py:25
  99.9 30.4 %collective-permute-start.9 = (bf16[1,288,1152]{2,1,0:T(8,128)(2,1)}, bf16[1,288,1152]{2,1,0:T(8,128)(2,1)}, u32[]{:S(2)}, u32[]{:S(2)}) collective-permute-start(bf16[1,288,1152]{2,1,0:T(8,128)(2,1)} %collective-permute-done.8.far0_ref), channel_id=1, source_target_pairs={{0,16},{16,0},{1,17},{17,1},{2,18},{18,2},{3,19},{19,3},{4,20},{20... | collective-permute-start | bytes 1990664 | tf_op jit(solution)/shard_map/ppermute | solution.py:25
  101.9 42.0 %collective-permute-start.4 = (bf16[1,288,1152]{2,1,0:T(8,128)(2,1)}, bf16[1,288,1152]{2,1,0:T(8,128)(2,1)}, u32[]{:S(2)}, u32[]{:S(2)}) collective-permute-start(bf16[1,288,1152]{2,1,0:T(8,128)(2,1)} %collective-permute-done.3.far0_ref), channel_id=1, source_target_pairs={{0,16},{16,0},{1,17},{17,1},{2,18},{18,2},{3,19},{19,3},{4,20},{20... | collective-permute-start | bytes 1990664 | tf_op jit(solution)/shard_map/ppermute | solution.py:25
  116.1 33.5 %collective-permute-start.20 = (bf16[2,288,576]{2,1,0:T(8,128)(2,1)S(1)}, bf16[2,288,576]{2,1,0:T(8,128)(2,1)S(1)}, u32[]{:S(2)}, u32[]{:S(2)}) collective-permute-start(bf16[2,288,576]{2,1,0:T(8,128)(2,1)S(1)} %fusion.17), channel_id=1, source_target_pairs={{0,1},{1,0},{2,3},{3,2},{4,5},{5,4},{6,7},{7,6},{8,9},{9,8},{10,11... | collective-permute-start | bytes 1990664 | tf_op jit(solution)/shard_map/ppermute | solution.py:25
  130.3 25.8 %collective-permute-start.15 = (bf16[2,288,576]{2,1,0:T(8,128)(2,1)S(1)}, bf16[2,288,576]{2,1,0:T(8,128)(2,1)S(1)}, u32[]{:S(2)}, u32[]{:S(2)}) collective-permute-start(bf16[2,288,576]{2,1,0:T(8,128)(2,1)S(1)} %fusion.18), channel_id=1, source_target_pairs={{0,1},{1,0},{2,3},{3,2},{4,5},{5,4},{6,7},{7,6},{8,9},{9,8},{10,11... | collective-permute-start | bytes 1990664 | tf_op jit(solution)/shard_map/ppermute | solution.py:25
  143.8 19.1 %collective-permute-start.10 = (bf16[2,288,576]{2,1,0:T(8,128)(2,1)S(1)}, bf16[2,288,576]{2,1,0:T(8,128)(2,1)S(1)}, u32[]{:S(2)}, u32[]{:S(2)}) collective-permute-start(bf16[2,288,576]{2,1,0:T(8,128)(2,1)S(1)} %fusion.19), channel_id=1, source_target_pairs={{0,1},{1,0},{2,3},{3,2},{4,5},{5,4},{6,7},{7,6},{8,9},{9,8},{10,11... | collective-permute-start | bytes 1990664 | tf_op jit(solution)/shard_map/ppermute | solution.py:25
  145.3 24.2 %collective-permute-start.5 = (bf16[2,288,576]{2,1,0:T(8,128)(2,1)S(1)}, bf16[2,288,576]{2,1,0:T(8,128)(2,1)S(1)}, u32[]{:S(2)}, u32[]{:S(2)}) collective-permute-start(bf16[2,288,576]{2,1,0:T(8,128)(2,1)S(1)} %fusion.20), channel_id=1, source_target_pairs={{0,1},{1,0},{2,3},{3,2},{4,5},{5,4},{6,7},{7,6},{8,9},{9,8},{10,11... | collective-permute-start | bytes 1990664 | tf_op jit(solution)/shard_map/ppermute | solution.py:25
  155.7 20.7 %collective-permute-start.21 = (bf16[160,1152]{1,0:T(8,128)(2,1)S(1)}, bf16[160,1152]{1,0:T(8,128)(2,1)S(1)}, u32[]{:S(2)}, u32[]{:S(2)}) collective-permute-start(bf16[160,1152]{1,0:T(8,128)(2,1)S(1)} %get-tuple-element.21), channel_id=1, source_target_pairs={{0,1},{1,0},{2,3},{3,2},{4,5},{5,4},{6,7},{7,6},{8,9},{9,8},{10,11... | collective-permute-start | bytes 1105928 | tf_op jit(solution)/shard_map/ppermute | solution.py:25
  162.3 14.8 %collective-permute-start.16 = (bf16[160,1152]{1,0:T(8,128)(2,1)S(1)}, bf16[160,1152]{1,0:T(8,128)(2,1)S(1)}, u32[]{:S(2)}, u32[]{:S(2)}) collective-permute-start(bf16[160,1152]{1,0:T(8,128)(2,1)S(1)} %get-tuple-element.19), channel_id=1, source_target_pairs={{0,1},{1,0},{2,3},{3,2},{4,5},{5,4},{6,7},{7,6},{8,9},{9,8},{10,11... | collective-permute-start | bytes 1105928 | tf_op jit(solution)/shard_map/ppermute | solution.py:25
  169.1 10.3 %collective-permute-start.11 = (bf16[160,1152]{1,0:T(8,128)(2,1)S(1)}, bf16[160,1152]{1,0:T(8,128)(2,1)S(1)}, u32[]{:S(2)}, u32[]{:S(2)}) collective-permute-start(bf16[160,1152]{1,0:T(8,128)(2,1)S(1)} %get-tuple-element.17), channel_id=1, source_target_pairs={{0,1},{1,0},{2,3},{3,2},{4,5},{5,4},{6,7},{7,6},{8,9},{9,8},{10,11... | collective-permute-start | bytes 1105928 | tf_op jit(solution)/shard_map/ppermute | solution.py:25
  177.9 10.3 %collective-permute-start.17 = (bf16[80,1152]{1,0:T(8,128)(2,1)}, bf16[80,1152]{1,0:T(8,128)(2,1)}, u32[]{:S(2)}, u32[]{:S(2)}) collective-permute-start(bf16[80,1152]{1,0:T(8,128)(2,1)} %slice.135), channel_id=1, source_target_pairs={{0,2},{2,0},{1,3},{3,1},{4,6},{6,4},{5,7},{7,5},{8,10},{10,8},{9,1... | collective-permute-start | bytes 552968 | tf_op jit(solution)/shard_map/ppermute | solution.py:25
  179.5 18.5 %collective-permute-start.12 = (bf16[80,1152]{1,0:T(8,128)(2,1)S(1)}, bf16[80,1152]{1,0:T(8,128)(2,1)S(1)}, u32[]{:S(2)}, u32[]{:S(2)}) collective-permute-start(bf16[80,1152]{1,0:T(8,128)(2,1)S(1)} %slice.136), channel_id=1, source_target_pairs={{0,2},{2,0},{1,3},{3,1},{4,6},{6,4},{5,7},{7,5},{8,10},{10,8},{9,1... | collective-permute-start | bytes 552968 | tf_op jit(solution)/shard_map/ppermute | solution.py:25
  180.3 27.6 %collective-permute-start.7 = (bf16[80,1152]{1,0:T(8,128)(2,1)S(1)}, bf16[80,1152]{1,0:T(8,128)(2,1)S(1)}, u32[]{:S(2)}, u32[]{:S(2)}) collective-permute-start(bf16[80,1152]{1,0:T(8,128)(2,1)S(1)} %slice.137), channel_id=1, source_target_pairs={{0,2},{2,0},{1,3},{3,1},{4,6},{6,4},{5,7},{7,5},{8,10},{10,8},{9,1... | collective-permute-start | bytes 552968 | tf_op jit(solution)/shard_map/ppermute | solution.py:25
  204.5 9.8 %all-to-all-start.1 = ((bf16[4,20,1152]{2,1,0:T(8,128)(2,1)}), bf16[4,20,1152]{2,1,0:T(8,128)(2,1)S(1)}, u32[]{:S(2)}, u32[]{:S(2)}) async-start(bf16[4,20,1152]{2,1,0:T(8,128)(2,1)} %reshape.281), calls=%async_computation.1 | async-start | bytes 442368 | tf_op jit(solution)/shard_map/all_to_all | solution.py:308
  (15 other events, 309.9 us)
Sparse Core Ops, SparseCore 0:
  11.7 33.1 all-gather.4
  46.4 29.7 all-gather.6

commit v2 on v0

--- a/solution.py
+++ b/solution.py
@@ -1,6 +1,10 @@
+import functools
+
 import jax
 import jax.numpy as jnp
 from jax import lax
+from jax.experimental import pallas as pl
+from jax.experimental.pallas import tpu as pltpu
 from jax.sharding import PartitionSpec as P
 
 EXPERTS = 16
@@ -78,7 +82,9 @@
     return produced.astype(jnp.bfloat16)
 
 
-def local(hidden_states, expert_ids, modulation, router_weight, w_in, b_in, w_out):
+def gathered_weights(
+    hidden_states, expert_ids, modulation, router_weight, w_in, b_in, w_out
+):
     token_count = hidden_states.shape[1]
     width = hidden_states.shape[2]
     tokens = hidden_states.reshape(token_count, width)
@@ -140,6 +146,501 @@
     return result.reshape(1, token_count, width)
 
 
+def crossed(block, axis, mask):
+    count = lax.axis_size(axis)
+    return lax.ppermute(block, axis, [(i, i ^ mask) for i in range(count)])
+
+
+def after(value, *events):
+    return lax.optimization_barrier((value, *events))[0] if events else value
+
+
+def slot_rows(ids, experts_count):
+    tokens = ids[0].shape[1]
+    experts = lax.broadcasted_iota(jnp.int32, (experts_count, tokens), 0).astype(jnp.float32)
+    chosen = [jnp.where(experts == row, 1.0, 0.0) for row in ids]
+    earlier = jnp.where(
+        lax.broadcasted_iota(jnp.int32, (tokens, tokens), 0)
+        < lax.broadcasted_iota(jnp.int32, (tokens, tokens), 1),
+        1.0,
+        0.0,
+    )
+    before = jnp.dot(
+        (chosen[0] + chosen[1]).astype(jnp.bfloat16),
+        earlier.astype(jnp.bfloat16),
+        preferred_element_type=jnp.float32,
+    )
+    return [jnp.sum(before * one, axis=0, keepdims=True) for one in chosen]
+
+
+def prepare_kernel(tokens_ref, ids_ref, settings_ref, out_ref):
+    count, width = tokens_ref.shape[1:]
+    out_ref[:count, :] = modulate(
+        tokens_ref[0], settings_ref[0, 0:1, :], settings_ref[0, 1:2, :]
+    )
+    lanes = lax.broadcasted_iota(jnp.int32, (count, count), 1)
+    columns = ids_ref[0].astype(jnp.float32)
+    spread = jnp.where(lanes == 0, columns[:, 0:1], columns[:, 1:2]).T
+    ids = [spread[0:1, :], spread[1:2, :]]
+    listed = [*ids, *slot_rows(ids, EXPERTS), jnp.zeros((1, width - 4 * count), jnp.float32)]
+    row = jnp.concatenate(listed, axis=1)
+    first = lax.broadcasted_iota(jnp.int32, (16, width), 0) == 0
+    out_ref[count:, :] = jnp.where(first, row, 0.0).astype(jnp.bfloat16)
+
+
+def prepare_call(hidden_states, expert_ids, modulation):
+    count, width = hidden_states.shape[1:]
+    return pl.pallas_call(
+        prepare_kernel,
+        out_shape=jax.ShapeDtypeStruct((count + 16, width), jnp.bfloat16),
+        name="prepare",
+    )(hidden_states, expert_ids, modulation)
+
+
+def route_kernel(block_ref, ids_ref, router_ref, out_ref):
+    count = out_ref.shape[0]
+    listed = block_ref[count:, :].astype(jnp.float32)[0:1, :]
+    rows = [listed[:, k * count : (k + 1) * count] for k in range(4)]
+    place = lax.broadcasted_iota(jnp.int32, (count, count), 0)
+    spread = jnp.zeros((count, count), jnp.float32)
+    for k, row in enumerate(rows):
+        spread = jnp.where(place == k, row, spread)
+    columns = spread.T
+    logits = jnp.dot(block_ref[:count, :], router_ref[...], preferred_element_type=jnp.float32)
+    ids = ids_ref[0]
+    experts = lax.broadcasted_iota(jnp.int32, logits.shape, 1)
+    picked = [
+        jnp.sum(jnp.where(experts == ids[:, k : k + 1], logits, 0.0), axis=1, keepdims=True)
+        for k in range(2)
+    ]
+    gap = picked[0] - picked[1]
+    lanes = lax.broadcasted_iota(jnp.int32, (count, count), 1)
+    columns = jnp.where(lanes == 4, jax.nn.sigmoid(gap), columns)
+    out_ref[...] = jnp.where(lanes == 5, jax.nn.sigmoid(-gap), columns)
+
+
+def route_call(block, expert_ids, router_weight):
+    count = expert_ids.shape[1]
+    return pl.pallas_call(
+        route_kernel,
+        out_shape=jax.ShapeDtypeStruct((count, count), jnp.float32),
+        name="route",
+    )(block, expert_ids, router_weight)
+
+
+def dispatch_kernel(wanted_ref, *refs):
+    images = wanted_ref.shape[1]
+    blocks, outs = refs[:images], refs[images:]
+    rows = outs[0].shape[0]
+    count = blocks[0].shape[0] - 16
+    choices = []
+    for image, block in enumerate(blocks):
+        listed = block[count:, :].astype(jnp.float32)[0:1, :]
+        wanted = wanted_ref[:, image : image + 1]
+        chosen = None
+        for k in range(2):
+            ids = listed[:, k * count : (k + 1) * count]
+            slots = listed[:, (2 + k) * count : (3 + k) * count]
+            match = wanted == ids * CAP + slots
+            chosen = match if chosen is None else chosen | match
+        choices.append(jnp.where(chosen, 1.0, 0.0).astype(jnp.bfloat16))
+    select = jnp.concatenate(choices, axis=1)
+    tokens = jnp.concatenate([block[:count, :] for block in blocks], axis=0)
+    for number, out_ref in enumerate(outs):
+        out_ref[...] = jnp.dot(
+            select[number * rows : (number + 1) * rows, :],
+            tokens,
+            preferred_element_type=jnp.float32,
+        ).astype(jnp.bfloat16)
+
+
+def dispatch_call(wanted, blocks, members):
+    rows = wanted.shape[0] // members
+    width = blocks[0].shape[1]
+    return pl.pallas_call(
+        dispatch_kernel,
+        out_shape=[jax.ShapeDtypeStruct((rows, width), jnp.bfloat16)] * members,
+        name="dispatch",
+    )(wanted, *blocks)
+
+
+def cut_kernel(plan, place_ref, w_in_ref, *refs):
+    outs, (held, sems) = refs[:-2], refs[-2:]
+    width = held.shape[2]
+    chip = place_ref[0] >> 1
+    arriving, leaving = [], []
+    for number, (unit, offset, rows, far) in enumerate(plan):
+        first = pl.multiple_of((1 - chip if far else chip) * width, 128)
+        count = outs[number].shape[0]
+        for at in range(count):
+            slot = len(arriving)
+            source = w_in_ref.at[
+                unit + (place_ref[1] if far else at), pl.ds(offset, rows), pl.ds(first, width)
+            ]
+            staged = held.at[slot, pl.ds(0, rows), :]
+            arriving.append(pltpu.make_async_copy(source, staged, sems.at[0, slot]))
+            leaving.append(pltpu.make_async_copy(staged, outs[number].at[at], sems.at[1, slot]))
+    for copy in arriving:
+        copy.start()
+    for copy, onward in zip(arriving, leaving, strict=True):
+        copy.wait()
+        onward.start()
+    for copy in leaving:
+        copy.wait()
+
+
+def cut_call(plan, width, place, w_in):
+    anywhere = pl.BlockSpec(memory_space=pl.ANY)
+    slots = sum(1 if far else SPLIT for *_, far in plan)
+    return pl.pallas_call(
+        functools.partial(cut_kernel, plan),
+        in_specs=[pl.BlockSpec(memory_space=pltpu.SMEM), anywhere],
+        out_specs=[anywhere] * len(plan),
+        out_shape=[
+            jax.ShapeDtypeStruct((1 if far else SPLIT, rows, width), jnp.bfloat16)
+            for _, _, rows, far in plan
+        ],
+        scratch_shapes=[
+            pltpu.VMEM((slots, w_in.shape[1], width), jnp.bfloat16),
+            pltpu.SemaphoreType.DMA((2, slots)),
+        ],
+        compiler_params=pltpu.CompilerParams(vmem_limit_bytes=60 << 20),
+        name="cut",
+    )(place, w_in)
+
+
+def expert_kernel(
+    expert, groups, sources, place_ref, own_ref, b_ref, out_w_ref, *refs
+):
+    x_refs, refs = refs[:sources], refs[sources:]
+    arrays, refs = refs[:-10], refs[-10:]
+    near_ref, keep_ref, keep_far_ref, send_ref, *refs = refs
+    x_pairs, x_held, weight, out_weight, total, sems = refs
+    step = pl.program_id(0)
+    here, part, core = place_ref[0], place_ref[1], place_ref[2]
+    depth = own_ref.shape[1]
+    columns, width = out_w_ref.shape[1:]
+    slab = weight.shape[2]
+    skip = slab - columns
+    wide = 2 * columns
+    first = pl.multiple_of(core * (wide - slab), 128)
+    chip_first = pl.multiple_of((here >> 1) * wide + core * (wide - slab), 128)
+    half_rows = x_held.shape[0] // 2
+    per = x_pairs.shape[1] // 2
+
+    def copies(number):
+        unit = SPLIT * expert + (number ^ part)
+        made = []
+
+        def add(source, target):
+            made.append(pltpu.make_async_copy(source, target, sems.at[number, len(made)]))
+
+        def rows(device, offset, size):
+            return weight.at[number, pl.ds(pl.multiple_of(device * depth + offset, 16), size), :]
+
+        add(own_ref.at[unit, :, pl.ds(chip_first, slab)], rows(here, 0, depth))
+        add(near_ref.at[number ^ part, :, pl.ds(first, slab)], rows(here ^ 1, 0, depth))
+        for relative, at, offset, size in groups[number]:
+            add(
+                arrays[at].at[0, :, pl.ds(first, slab)],
+                rows(here ^ relative, offset, size),
+            )
+        add(
+            out_w_ref.at[unit],
+            out_weight.at[number, pl.ds(pl.multiple_of(core * skip, 16), columns), :],
+        )
+        return made
+
+    spare_sem = sems.shape[1] - sources
+    x_copies = [
+        pltpu.make_async_copy(
+            x_ref.at[pl.ds(2 * per * (expert // 2), 2 * per), :],
+            x_pairs.at[at],
+            sems.at[0, spare_sem + at],
+        )
+        for at, x_ref in enumerate(x_refs)
+    ]
+
+    @pl.when(step == 0)
+    def _():
+        for copy in x_copies:
+            copy.start()
+        for number in range(SPLIT):
+            for copy in copies(number):
+                copy.start()
+        for number in range(SPLIT):
+            spare = pl.ds(pl.multiple_of((1 - core) * columns, 16), skip)
+            out_weight[number, spare, :] = jnp.zeros((skip, width), out_weight.dtype)
+        for at, copy in enumerate(x_copies):
+            copy.wait()
+            pair = x_pairs[at].astype(jnp.float32)
+            own_rows = pair[per * (expert % 2) : per * (expert % 2 + 1), :]
+            total[per * at : per * (at + 1), :] = own_rows
+        x_held[...] = total[...].astype(jnp.bfloat16)
+
+    for number in range(SPLIT):
+
+        @pl.when(step == number)
+        def _(number=number):
+            for copy in copies(number):
+                copy.wait()
+
+    pre = jnp.dot(x_held[...], weight[step], preferred_element_type=jnp.float32) + b_ref[0]
+    hidden = jax.nn.gelu(pre, approximate=True).astype(jnp.bfloat16)
+    piece = jnp.dot(hidden, out_weight[step], preferred_element_type=jnp.float32)
+
+    @pl.when(step == 0)
+    def _():
+        total[...] = piece
+
+    @pl.when(step == 1)
+    def _():
+        total[...] += piece
+        members = half_rows // (2 * CAP)
+        for member in range(members):
+            at = 2 * CAP * member
+            keep_ref[CAP * member : CAP * (member + 1), :] = total[at : at + CAP, :]
+            keep_far_ref[CAP * member : CAP * (member + 1), :] = total[at + CAP : at + 2 * CAP, :]
+        given = [
+            total[at : at + CAP, :]
+            for image in range(2)
+            for at in range(half_rows + CAP * image, 2 * half_rows, 2 * CAP)
+        ]
+        for number, rows in enumerate(given):
+            total[CAP * number : CAP * (number + 1), :] = rows
+        send_ref[...] = total[:half_rows, :].astype(jnp.bfloat16)
+
+
+def expert_call(expert, place, xs, own, b, w_out, near, pieces):
+    width = w_out.shape[2]
+    per = 2 * CAP
+    half_rows = per * len(xs) // 2
+    columns = w_out.shape[1]
+    slab = b.shape[2]
+    arrays, groups = [], [[] for _ in range(SPLIT)]
+    for number, relative, array, offset in pieces:
+        groups[number].append((relative, len(arrays), offset, array.shape[1]))
+        arrays.append(array)
+    anywhere = pl.BlockSpec(memory_space=pl.ANY)
+    kept = pl.BlockSpec((half_rows // 2, width), lambda s, p: (0, 0))
+
+    return pl.pallas_call(
+        functools.partial(expert_kernel, expert, groups, len(xs)),
+        grid_spec=pltpu.PrefetchScalarGridSpec(
+            num_scalar_prefetch=1,
+            grid=(SPLIT,),
+            in_specs=[
+                anywhere,
+                pl.BlockSpec((1, 1, slab), lambda s, p: (SPLIT * expert + (s ^ p[1]), 0, 0)),
+                anywhere,
+                *([anywhere] * (len(xs) + len(arrays) + 1)),
+            ],
+            out_specs=[kept, kept, pl.BlockSpec((half_rows, width), lambda s, p: (0, 0))],
+            scratch_shapes=[
+                pltpu.VMEM((len(xs), 2 * per, width), jnp.bfloat16),
+                pltpu.VMEM((2 * half_rows, width), jnp.bfloat16),
+                pltpu.VMEM((SPLIT, width, slab), jnp.bfloat16),
+                pltpu.VMEM((SPLIT, slab, width), jnp.bfloat16),
+                pltpu.VMEM((2 * half_rows, width), jnp.float32),
+                pltpu.SemaphoreType.DMA((SPLIT, 3 + max(map(len, groups)) + len(xs))),
+            ],
+        ),
+        out_shape=[
+            jax.ShapeDtypeStruct((half_rows // 2, width), jnp.float32),
+            jax.ShapeDtypeStruct((half_rows // 2, width), jnp.float32),
+            jax.ShapeDtypeStruct((half_rows, width), jnp.bfloat16),
+        ],
+        compiler_params=pltpu.CompilerParams(vmem_limit_bytes=60 << 20),
+        cost_estimate=pl.CostEstimate(
+            flops=2 * SPLIT * 2 * 2 * half_rows * width * columns,
+            bytes_accessed=2 * SPLIT * 3 * width * columns + 16 * half_rows * width,
+            transcendentals=SPLIT * 2 * half_rows * columns,
+        ),
+        name="expert",
+    )(place, own, b, w_out, *xs, *arrays, near)
+
+
+def combine_kernel(experts, groups, place_ref, route_ref, tokens_ref, settings_ref, *refs):
+    out_ref, held = refs[-2:]
+    replies = refs[:-2]
+    count = route_ref.shape[0]
+    members = len(replies) // len(groups)
+    at = 0
+    for reply in replies:
+        rows = reply.shape[0]
+        held[at : at + rows, :] = reply[...].astype(jnp.float32)
+        at += rows
+    rows_held = held[...].astype(jnp.bfloat16)
+    place = lax.broadcasted_iota(jnp.int32, (count, at), 1)
+    branch = None
+    for k in range(2):
+        expert = route_ref[:, k : k + 1].astype(jnp.int32)
+        slot = route_ref[:, 2 + k : 3 + k].astype(jnp.int32)
+        owner = jnp.zeros_like(expert)
+        for member in range(1, members):
+            owner += jnp.where(expert >= member * experts, 1, 0)
+        local_expert = expert - owner * experts
+        ring = owner ^ place_ref[3]
+        position = jnp.zeros_like(expert)
+        first = 0
+        for group in groups:
+            size = len(group) * CAP
+            inside = (local_expert >= group[0]) & (local_expert <= group[-1])
+            here = first + ring * size + (local_expert - group[0]) * CAP + slot
+            position = jnp.where(inside, here, position)
+            first += members * size
+        select = jnp.where(place == position, 1.0, 0.0).astype(jnp.bfloat16)
+        term = route_ref[:, 4 + k : 5 + k] * jnp.dot(
+            select, rows_held, preferred_element_type=jnp.float32
+        )
+        branch = term if branch is None else branch + term
+    out_ref[0] = (
+        tokens_ref[0].astype(jnp.float32) + settings_ref[0, 2:3, :] * branch
+    ).astype(out_ref.dtype)
+
+
+def combine_call(experts, groups, place, route, hidden_states, modulation, replies):
+    rows = sum(reply.shape[0] for reply in replies)
+    whole = pl.BlockSpec(memory_space=pltpu.VMEM)
+    return pl.pallas_call(
+        functools.partial(combine_kernel, experts, groups),
+        in_specs=[pl.BlockSpec(memory_space=pltpu.SMEM), *([whole] * (3 + len(replies)))],
+        out_shape=jax.ShapeDtypeStruct(hidden_states.shape, hidden_states.dtype),
+        scratch_shapes=[pltpu.VMEM((rows, hidden_states.shape[2]), jnp.float32)],
+        name="combine",
+    )(place, route, hidden_states, modulation, *replies)
+
+
+def recut_weights(hidden_states, expert_ids, modulation, router_weight, w_in, b_in, w_out):
+    units, depth, _ = w_in.shape
+    columns = w_out.shape[1]
+    wide = 2 * columns
+    experts = units // SPLIT
+    members = lax.axis_size("ep")
+    here, part, row = lax.axis_index("fs"), lax.axis_index("parts"), lax.axis_index("ep")
+    core, chip = here & 1, here >> 1
+    place = jnp.stack([here, part, core, row]).astype(jnp.int32)
+
+    plan = []
+    for expert in range(experts):
+        pieces = 2 if expert == experts - 1 else 1
+        plan += [(expert, piece * (depth // pieces), depth // pieces) for piece in range(pieces)]
+
+    def over(held, gate):
+        return crossed(after(held, gate), "fs", 1)
+
+    def beside(held, gate):
+        return crossed(after(held, gate), "parts", 1)
+
+    slab = -(-columns // 128) * 128
+    own_b = lax.dynamic_slice(
+        b_in, (0, chip * wide + core * (wide - slab)), (units, slab)
+    )[:, None, :]
+    per = 2 * CAP
+    shape = (members, experts, 2, CAP)
+    number = [jnp.broadcast_to(jnp.arange(size, dtype=jnp.int32).reshape(
+        [-1 if axis == at else 1 for axis in range(4)]), shape).reshape(-1)
+        for at, size in enumerate(shape)]
+    wanted = ((row ^ number[0]) * experts + number[1]) * CAP + number[3]
+    wanted = jnp.stack([jnp.where(number[2] == image, wanted, -1) for image in range(2)], axis=1)
+
+    block = prepare_call(hidden_states, expert_ids, modulation)
+    gate = after(place, block)
+    cuts = cut_call(
+        tuple((SPLIT * e, offset, rows, True) for e, offset, rows in plan)
+        + tuple((SPLIT * e, 0, depth, False) for e in range(experts)),
+        wide,
+        place,
+        w_in,
+    )
+    leaving, nearby = cuts[: len(plan)], cuts[len(plan) :]
+
+    def fetch(number, gate):
+        return crossed(after(leaving[number], gate), "fs", 2)
+
+    opposite = crossed(after(block, gate), "fs", 2)
+    gate = after(gate, opposite, leaving[0])
+    far = [fetch(0, gate), fetch(1, gate)]
+    sending = dispatch_call(wanted.astype(jnp.float32), [block, opposite], members)
+    arrived = [sending[0]] + [crossed(sending[d], "ep", d) for d in range(1, members - 1)]
+    across = [over(sending[0], gate)]
+    gate = after(gate, far[0], across[0], *arrived[1:])
+
+    far.append(fetch(2, gate))
+    arrived.append(crossed(after(sending[-1], gate), "ep", members - 1))
+    other = [beside(far[0], gate)]
+    cross = [over(far[0], gate)]
+    across += [over(held, gate) for held in arrived[1:-1]]
+    near = [over(nearby[0], gate)]
+    gate = after(gate, far[1], arrived[-1], other[0], cross[0], *across[1:])
+
+    far.append(fetch(3, gate))
+    other.append(beside(far[1], gate))
+    cross.append(over(far[1], gate))
+    cross_other = [over(other[0], gate)]
+    across.append(over(arrived[-1], gate))
+    near.append(over(nearby[1], gate))
+    gate = after(gate, far[2], other[1], cross[1], cross_other[0], across[-1])
+
+    far.append(fetch(4, gate))
+    other.append(beside(far[2], gate))
+    cross.append(over(far[2], gate))
+    cross_other.append(over(other[1], gate))
+    near.append(over(nearby[2], gate))
+
+    def run(expert):
+        pieces = []
+        for at, (of, offset, _) in enumerate(plan):
+            if of == expert:
+                pieces += [(0, 2, far[at], offset), (0, 3, cross[at], offset)]
+                pieces += [(1, 2, other[at], offset), (1, 3, cross_other[at], offset)]
+        return expert_call(
+            expert, place, arrived + across, w_in, own_b, w_out, near[expert], pieces
+        )
+
+    outs = [run(0)]
+    gate = after(gate, far[3], cross[2], cross_other[1], outs[0][0])
+    other.append(beside(far[3], gate))
+    cross.append(over(far[3], gate))
+    near.append(over(nearby[3], gate))
+    cross_other.append(over(other[2], gate))
+    outs.append(run(1))
+    gate = after(gate, far[4], cross[3], cross_other[2], outs[1][0])
+    other.append(beside(far[4], gate))
+    cross.append(over(far[4], gate))
+    cross_other.append(over(other[3], gate))
+    outs.append(run(2))
+    gate = after(gate, outs[2][0])
+    cross_other.append(over(other[4], gate))
+    outs.append(run(3))
+
+    route = route_call(block, expert_ids, router_weight)
+    half_rows = members * CAP
+    sent = [crossed(send, "fs", 1) for _, _, send in outs]
+    wholes = []
+    for e in range(experts):
+        keep, keep_far, _ = outs[e]
+        given = (keep_far + sent[e][half_rows:].astype(jnp.float32)).astype(jnp.bfloat16)
+        given = crossed(after(given, *[out[0] for out in outs[e + 1 : e + 2]]), "fs", 2)
+        half = keep + sent[e][:half_rows].astype(jnp.float32)
+        wholes.append((half + given.astype(jnp.float32)).astype(jnp.bfloat16))
+    groups = ((0, 1), (2, 3))
+    replies = []
+    for group in groups:
+        for d in range(members):
+            reply = jnp.concatenate([wholes[e][d * CAP : (d + 1) * CAP] for e in group])
+            reply = crossed(after(reply, outs[-1][0]), "ep", d) if d else reply
+            replies.append(reply)
+    return combine_call(experts, groups, place, route, hidden_states, modulation, replies)
+
+
+def local(*arrays):
+    w_in = arrays[4]
+    recut = lax.axis_size("fs") == lax.axis_size("ep") == 4 and lax.axis_size("parts") == 2
+    recut = recut and w_in.shape[0] == 4 * SPLIT
+    return (recut_weights if recut else gathered_weights)(*arrays)
+
+
 def solution(mesh):
     placed = (
         P(("parts", "fs"), "ep", None),

time: 588 us -> 171 us (0.29)
  waiting for transfers between devices: 517 us -> 58 us
  Pallas kernels: 0 us -> 50.9 us
  matrix products: 31.7 us -> 0 us
  starting transfers between devices: 11 us -> 42.5 us
  between operations: 13.7 us -> 0.52 us
    all_gather x2 -> x0, waiting for transfers between devices: 478 us -> none  [the longest x1 255 us: expert_compute(): lax.all_gather(w_out, 'fs', axis=1, tiled=True)]
    ppermute x0 -> x46, waiting for transfers between devices: none -> 58 us  [crossed(): return lax.ppermute(block, axis, [(i, i ^ mask) for i in range(count)])]
    pallas_call x0 -> x9, Pallas kernels: none -> 50.9 us  [the longest x4 34.5 us: expert_call(): pl.pallas_call(functools.partial(expert_kernel, expert, groups, len(xs)),...]
    ppermute x0 -> x46, starting transfers between devices: none -> 42.5 us  [crossed(): return lax.ppermute(block, axis, [(i, i ^ mask) for i in range(count)])]
    all_to_all x2 -> x0, waiting for transfers between devices: 38 us -> none  [the longest x1 21.3 us: local(): lax.all_to_all(sending, 'ep', split_axis=0, concat_axis=1, tiled=True)]
    dot_general x3 -> x0, matrix products: 31.7 us -> none  [the longest x1 30.4 us: expert_compute(): jnp.einsum('urf,ufd->urd', columns, lax.all_gather(w_out, 'fs', axis=1, t...]
    all_to_all x2 -> x0, starting transfers between devices: 10.9 us -> none  [the longest x1 6.32 us: local(): lax.all_to_all(sending, 'ep', split_axis=0, concat_axis=1, tiled=True)]
    unnamed x25 -> x75, local copies, waits for them, and re-layouts: 0.17 us -> 8.57 us
  transfers between devices with their start and end apart: 4 -> 46, of which waited for: 4 -> 17; matrix products, arithmetic and copies ran while one was open for 1% -> 6% of each run, Pallas kernels for 0% -> 22%
where the time goes in v2:
time: 171 us
  waiting for transfers between devices  58 us (34%)
  Pallas kernels  50.9 us (30%)
  starting transfers between devices  42.5 us (25%)
  local copies, waits for them, and re-layouts  10.5 us (6%)
  other arithmetic  8.41 us (5%)
    ppermute x46, waiting for transfers between devices, crossed(): return lax.ppermute(block, axis, [(i, i ^ mask) for i in range(count)])  58 us
    ppermute x46, starting transfers between devices, crossed(): return lax.ppermute(block, axis, [(i, i ^ mask) for i in range(count)])  42.5 us
    pallas_call x4, Pallas kernels, expert_call(): pl.pallas_call(functools.partial(expert_kernel, expert, groups, len(xs)),...  34.5 us
    unnamed x75, local copies, waits for them, and re-layouts  8.57 us
    pallas_call x1, Pallas kernels, cut_call(): pl.pallas_call(functools.partial(cut_kernel, plan), in_specs=[pl.BlockSpe...  6.93 us
    convert_element_type x4, other arithmetic, recut_weights(): (keep_far + sent[e][half_rows:].astype(jnp.float32)).astype(jnp.bfloat16)  3.59 us
  transfers between devices with their start and end apart: 46, of which 17 were waited for; matrix products, arithmetic and copies ran while one was open for 6% of the time, Pallas kernels for 22%

profile of v2, /device:TPU:0, one launch (start us, length us, event | category | flops | bytes accessed | tf_op | source)
XLA Modules:
  0.0 170.8 jit_solution(4560070170521723395)
XLA Ops:
  2.8 2.1 %prepare.1.block_ref.refs_0_ = bf16[144,1152]{1,0:T(8,128)(2,1)} custom-call(bf16[1,128,1152]{2,1,0:T(8,128)(2,1)} %tokens_ref.3, s32[1,128,2]{2,1,0:T(8,128)} %copy.26.ids_ref, f32[1,3,1152]{2,1,0:T(4,128)} %copy.27.settings_ref), custom_call_target="tpu_custom_call" | custom-call | tf_op jit(solution)/shard_map/prepare/pallas_call | solution.py:193
  5.4 2.9 %collective-permute-start = (bf16[144,1152]{1,0:T(8,128)(2,1)}, bf16[144,1152]{1,0:T(8,128)(2,1)S(1)}, u32[]{:S(2)}, u32[]{:S(2)}) collective-permute-start(bf16[144,1152]{1,0:T(8,128)(2,1)} %prepare.1.block_ref.refs_0_), channel_id=1, source_target_pairs={{0,2},{1,3},{2,0},{3,1},{4,6},{5,7},{6,4},{7,5},{8,10},{9,11},{10,... | collective-permute-start | bytes 995336 | tf_op jit(solution)/shard_map/ppermute | solution.py:151
  8.3 6.9 %cut.1 = (bf16[1,288,1152]{2,1,0:T(8,128)(2,1)}, bf16[1,288,1152]{2,1,0:T(8,128)(2,1)}, bf16[1,288,1152]{2,1,0:T(8,128)(2,1)}, bf16[1,144,1152]{2,1,0:T(8,128)(2...) custom-call(s32[4]{0:T(128)} %pad_add_fusion.place_ref, ...), custom_call_target="tpu_custom_call" | custom-call | tf_op jit(solution)/shard_map/cut/pallas_call | solution.py:295
  19.3 2.6 %dispatch.1 = (bf16[160,1152]{1,0:T(8,128)(2,1)}, bf16[160,1152]{1,0:T(8,128)(2,1)}, bf16[160,1152]{1,0:T(8,128)(2,1)}, bf16[160,1152]{1,0:T(8,128)(2,1)}) custom-call(f32[640,2]{1,0:T(8,128)} %copy.30.wanted_ref, bf16[144,1152]{1,0:T(8,128)(2,1)} %prepare.1.block_ref.refs_0_, bf16[144,1152]{1,0:T(8,128)(2,1)} %copy-done.22), custom_call_target="tpu_custom_call" | custom-call | tf_op jit(solution)/shard_map/dispatch/pallas_call | solution.py:260
  23.5 2.6 %collective-permute-start.2 = (bf16[160,1152]{1,0:T(8,128)(2,1)}, bf16[160,1152]{1,0:T(8,128)(2,1)S(1)}, u32[]{:S(2)}, u32[]{:S(2)}) collective-permute-start(bf16[160,1152]{1,0:T(8,128)(2,1)} %get-tuple-element.74), channel_id=1, source_target_pairs={{0,8},{4,12},{8,0},{12,4},{1,9},{5,13},{9,1},{13,5},{2,10},{6,14},... | collective-permute-start | bytes 1105928 | tf_op jit(solution)/shard_map/ppermute | solution.py:151
  26.6 14.3 %collective-permute-done.1.refs_1_ = bf16[160,1152]{1,0:T(8,128)(2,1)S(1)} collective-permute-done((bf16[160,1152]{1,0:T(8,128)(2,1)}, bf16[160,1152]{1,0:T(8,128)(2,1)S(1)}, u32[]{:S(2)}, u32[]{:S(2)}) %collective-permute-start.1) | collective-permute-done | bytes 368672 | tf_op jit(solution)/shard_map/ppermute | solution.py:151
  40.9 2.4 %collective-permute-done.2.refs_2_ = bf16[160,1152]{1,0:T(8,128)(2,1)S(1)} collective-permute-done((bf16[160,1152]{1,0:T(8,128)(2,1)}, bf16[160,1152]{1,0:T(8,128)(2,1)S(1)}, u32[]{:S(2)}, u32[]{:S(2)}) %collective-permute-start.2) | collective-permute-done | bytes 368672 | tf_op jit(solution)/shard_map/ppermute | solution.py:151
  47.0 3.6 %collective-permute-start.5 = (bf16[160,1152]{1,0:T(8,128)(2,1)}, bf16[160,1152]{1,0:T(8,128)(2,1)S(1)}, u32[]{:S(2)}, u32[]{:S(2)}) collective-permute-start(bf16[160,1152]{1,0:T(8,128)(2,1)} %get-tuple-element.81), channel_id=1, source_target_pairs={{0,12},{4,8},{8,4},{12,0},{1,13},{5,9},{9,5},{13,1},{2,14},{6,10},... | collective-permute-start | bytes 1105928 | tf_op jit(solution)/shard_map/ppermute | solution.py:151
  50.6 9.5 %collective-permute-done.5.refs_3_ = bf16[160,1152]{1,0:T(8,128)(2,1)S(1)} collective-permute-done((bf16[160,1152]{1,0:T(8,128)(2,1)}, bf16[160,1152]{1,0:T(8,128)(2,1)S(1)}, u32[]{:S(2)}, u32[]{:S(2)}) %collective-permute-start.5) | collective-permute-done | bytes 368672 | tf_op jit(solution)/shard_map/ppermute | solution.py:151
  65.7 8.7 %expert.4 = (f32[80,1152]{1,0:T(8,128)}, f32[80,1152]{1,0:T(8,128)}, bf16[160,1152]{1,0:T(8,128)(2,1)}) custom-call(s32[4]{0:T(128)} %pad_add_fusion.place_ref, bf16[8,288,2304]{2,1,0:T(8,128)(2,1)} %own_ref.7, f32[8,1,640]{2,1,0:T(1,128)} %broadcast_in_dim.30.b_ref, bf16[8,576,1152]{2,1,0:T(8,128)(2,1)} %out_w_ref.7, ...), custom_call_target="tpu_custom_call" | custom-call | flops 1698693120 | bytes 10911744 | tf_op jit(solution)/shard_map/expert/pallas_call | solution.py:427
  75.0 3.8 %collective-permute-done.17.refs_8_ = bf16[1,288,1152]{2,1,0:T(8,128)(2,1)S(1)} collective-permute-done((bf16[1,288,1152]{2,1,0:T(8,128)(2,1)}, bf16[1,288,1152]{2,1,0:T(8,128)(2,1)S(1)}, u32[]{:S(2)}, u32[]{:S(2)}) %collective-permute-start.17) | collective-permute-done | bytes 663584 | tf_op jit(solution)/shard_map/ppermute | solution.py:151
  78.9 1.9 %collective-permute-done.16.refs_10_ = bf16[1,288,1152]{2,1,0:T(8,128)(2,1)} collective-permute-done((bf16[1,288,1152]{2,1,0:T(8,128)(2,1)}, bf16[1,288,1152]{2,1,0:T(8,128)(2,1)}, u32[]{:S(2)}, u32[]{:S(2)}) %collective-permute-start.16) | collective-permute-done | bytes 663584 | tf_op jit(solution)/shard_map/ppermute | solution.py:151
  85.5 8.6 %expert.5 = (f32[80,1152]{1,0:T(8,128)}, f32[80,1152]{1,0:T(8,128)}, bf16[160,1152]{1,0:T(8,128)(2,1)}) custom-call(s32[4]{0:T(128)} %pad_add_fusion.place_ref, bf16[8,288,2304]{2,1,0:T(8,128)(2,1)} %own_ref.7, f32[8,1,640]{2,1,0:T(1,128)} %broadcast_in_dim.30.b_ref, bf16[8,576,1152]{2,1,0:T(8,128)(2,1)} %out_w_ref.7, ...), custom_call_target="tpu_custom_call" | custom-call | flops 1698693120 | bytes 10911744 | tf_op jit(solution)/shard_map/expert/pallas_call | solution.py:427
  96.3 2.1 %route.1.route_ref = f32[128,128]{1,0:T(8,128)} custom-call(bf16[144,1152]{1,0:T(8,128)(2,1)} %prepare.1.block_ref.refs_0_, s32[1,128,2]{2,1,0:T(8,128)} %copy.26.ids_ref, bf16[1152,16]{1,0:T(8,128)(2,1)} %copy.29.router_ref), custom_call_target="tpu_custom_call" | custom-call | tf_op jit(solution)/shard_map/route/pallas_call | solution.py:224
  108.0 8.6 %expert.6 = (f32[80,1152]{1,0:T(8,128)}, f32[80,1152]{1,0:T(8,128)}, bf16[160,1152]{1,0:T(8,128)(2,1)}) custom-call(s32[4]{0:T(128)} %pad_add_fusion.place_ref, bf16[8,288,2304]{2,1,0:T(8,128)(2,1)} %own_ref.7, f32[8,1,640]{2,1,0:T(1,128)} %broadcast_in_dim.30.b_ref, bf16[8,576,1152]{2,1,0:T(8,128)(2,1)} %out_w_ref.7, ...), custom_call_target="tpu_custom_call" | custom-call | flops 1698693120 | bytes 10911744 | tf_op jit(solution)/shard_map/expert/pallas_call | solution.py:427
  119.5 3.7 %collective-permute-done.27 = bf16[80,1152]{1,0:T(8,128)(2,1)S(1)} collective-permute-done((bf16[80,1152]{1,0:T(8,128)(2,1)}, bf16[80,1152]{1,0:T(8,128)(2,1)S(1)}, u32[]{:S(2)}, u32[]{:S(2)}) %collective-permute-start.27) | collective-permute-done | bytes 184352 | tf_op jit(solution)/shard_map/ppermute | solution.py:151
  130.3 8.6 %expert.7 = (f32[80,1152]{1,0:T(8,128)}, f32[80,1152]{1,0:T(8,128)}, bf16[160,1152]{1,0:T(8,128)(2,1)}) custom-call(s32[4]{0:T(128)} %pad_add_fusion.place_ref, bf16[8,288,2304]{2,1,0:T(8,128)(2,1)} %own_ref.7, f32[8,1,640]{2,1,0:T(1,128)} %broadcast_in_dim.30.b_ref, bf16[8,576,1152]{2,1,0:T(8,128)(2,1)} %out_w_ref.7, ...), custom_call_target="tpu_custom_call" | custom-call | flops 1698693120 | bytes 10911744 | tf_op jit(solution)/shard_map/expert/pallas_call | solution.py:427
  141.0 2.7 %collective-permute-start.38 = (bf16[40,1152]{1,0:T(8,128)(2,1)S(1)}, bf16[40,1152]{1,0:T(8,128)(2,1)S(1)}, u32[]{:S(2)}, u32[]{:S(2)}) collective-permute-start(bf16[40,1152]{1,0:T(8,128)(2,1)S(1)} %copy-done.27), channel_id=1, source_target_pairs={{0,12},{4,8},{8,4},{12,0},{1,13},{5,9},{9,5},{13,1},{2,14},{6,10},... | collective-permute-start | bytes 276488 | tf_op jit(solution)/shard_map/ppermute | solution.py:151
  143.7 5.4 %collective-permute-start.37 = (bf16[40,1152]{1,0:T(8,128)(2,1)S(1)}, bf16[40,1152]{1,0:T(8,128)(2,1)S(1)}, u32[]{:S(2)}, u32[]{:S(2)}) collective-permute-start(bf16[40,1152]{1,0:T(8,128)(2,1)S(1)} %pad_maximum_fusion.2), channel_id=1, source_target_pairs={{0,8},{4,12},{8,0},{12,4},{1,9},{5,13},{9,1},{13,5},{2,10},{6,14},... | collective-permute-start | bytes 276488 | tf_op jit(solution)/shard_map/ppermute | solution.py:151
  150.2 5.8 %collective-permute-done.42 = bf16[80,1152]{1,0:T(8,128)(2,1)S(1)} collective-permute-done((bf16[80,1152]{1,0:T(8,128)(2,1)S(1)}, bf16[80,1152]{1,0:T(8,128)(2,1)S(1)}, u32[]{:S(2)}, u32[]{:S(2)}) %collective-permute-start.42) | collective-permute-done | bytes 184352 | tf_op jit(solution)/shard_map/ppermute | solution.py:151
  156.1 2.4 %collective-permute-start.45 = (bf16[40,1152]{1,0:T(8,128)(2,1)S(1)}, bf16[40,1152]{1,0:T(8,128)(2,1)S(1)}, u32[]{:S(2)}, u32[]{:S(2)}) collective-permute-start(bf16[40,1152]{1,0:T(8,128)(2,1)S(1)} %pad_maximum_fusion.7), channel_id=1, source_target_pairs={{0,12},{4,8},{8,4},{12,0},{1,13},{5,9},{9,5},{13,1},{2,14},{6,10},... | collective-permute-start | bytes 276488 | tf_op jit(solution)/shard_map/ppermute | solution.py:151
  161.4 2.1 %collective-permute-done.45.refs_7_ = bf16[40,1152]{1,0:T(8,128)(2,1)S(1)} collective-permute-done((bf16[40,1152]{1,0:T(8,128)(2,1)S(1)}, bf16[40,1152]{1,0:T(8,128)(2,1)S(1)}, u32[]{:S(2)}, u32[]{:S(2)}) %collective-permute-start.45) | collective-permute-done | bytes 92192 | tf_op jit(solution)/shard_map/ppermute | solution.py:151
  163.5 3.4 %collective-permute-done.44.refs_6_ = bf16[40,1152]{1,0:T(8,128)(2,1)S(1)} collective-permute-done((bf16[40,1152]{1,0:T(8,128)(2,1)S(1)}, bf16[40,1152]{1,0:T(8,128)(2,1)S(1)}, u32[]{:S(2)}, u32[]{:S(2)}) %collective-permute-start.44) | collective-permute-done | bytes 92192 | tf_op jit(solution)/shard_map/ppermute | solution.py:151
  168.2 2.6 %combine.1 = bf16[1,128,1152]{2,1,0:T(8,128)(2,1)} custom-call(s32[4]{0:T(128)} %pad_add_fusion.place_ref, f32[128,128]{1,0:T(8,128)} %route.1.route_ref, bf16[1,128,1152]{2,1,0:T(8,128)(2,1)} %tokens_ref.3, f32[1,3,1152]{2,1,0:T(4,128)} %copy.27.settings_ref, bf16[40,1152]{1,0:T(8,128)(2,1)} %pad_maximum_fusion.refs_0_, bf16[40,1152]{1,0:T(8,128)(2,1)} %copy-done.30, ...), custom_call_target="tpu_custom_call" | custom-call | tf_op jit(solution)/shard_map/combine/pallas_call | solution.py:505
  (180 shorter events, 52.8 us)
Async XLA Ops:
  5.4 10.9 %collective-permute-start = (bf16[144,1152]{1,0:T(8,128)(2,1)}, bf16[144,1152]{1,0:T(8,128)(2,1)S(1)}, u32[]{:S(2)}, u32[]{:S(2)}) collective-permute-start(bf16[144,1152]{1,0:T(8,128)(2,1)} %prepare.1.block_ref.refs_0_), channel_id=1, source_target_pairs={{0,2},{1,3},{2,0},{3,1},{4,6},{5,7},{6,4},{7,5},{8,10},{9,11},{10,... | collective-permute-start | bytes 995336 | tf_op jit(solution)/shard_map/ppermute | solution.py:151
  16.4 26.9 %collective-permute-start.3 = (bf16[1,288,1152]{2,1,0:T(8,128)(2,1)}, bf16[1,288,1152]{2,1,0:T(8,128)(2,1)S(1)}, u32[]{:S(2)}, u32[]{:S(2)}) collective-permute-start(bf16[1,288,1152]{2,1,0:T(8,128)(2,1)} %get-tuple-element.78), channel_id=1, source_target_pairs={{0,2},{1,3},{2,0},{3,1},{4,6},{5,7},{6,4},{7,5},{8,10},{9,11},{10,... | collective-permute-start | bytes 1990664 | tf_op jit(solution)/shard_map/ppermute | solution.py:151
  21.9 19.0 %collective-permute-start.1 = (bf16[160,1152]{1,0:T(8,128)(2,1)}, bf16[160,1152]{1,0:T(8,128)(2,1)S(1)}, u32[]{:S(2)}, u32[]{:S(2)}) collective-permute-start(bf16[160,1152]{1,0:T(8,128)(2,1)} %get-tuple-element.73), channel_id=1, source_target_pairs={{0,4},{4,0},{8,12},{12,8},{1,5},{5,1},{9,13},{13,9},{2,6},{6,2},{1... | collective-permute-start | bytes 1105928 | tf_op jit(solution)/shard_map/ppermute | solution.py:151
  23.5 19.8 %collective-permute-start.2 = (bf16[160,1152]{1,0:T(8,128)(2,1)}, bf16[160,1152]{1,0:T(8,128)(2,1)S(1)}, u32[]{:S(2)}, u32[]{:S(2)}) collective-permute-start(bf16[160,1152]{1,0:T(8,128)(2,1)} %get-tuple-element.74), channel_id=1, source_target_pairs={{0,8},{4,12},{8,0},{12,4},{1,9},{5,13},{9,1},{13,5},{2,10},{6,14},... | collective-permute-start | bytes 1105928 | tf_op jit(solution)/shard_map/ppermute | solution.py:151
  26.1 20.9 %collective-permute-start.8 = (bf16[1,288,1152]{2,1,0:T(8,128)(2,1)S(1)}, bf16[1,288,1152]{2,1,0:T(8,128)(2,1)}, u32[]{:S(2)}, u32[]{:S(2)}) collective-permute-start(bf16[1,288,1152]{2,1,0:T(8,128)(2,1)S(1)} %copy-done.35), channel_id=1, source_target_pairs={{0,2},{1,3},{2,0},{3,1},{4,6},{5,7},{6,4},{7,5},{8,10},{9,11},{10,... | collective-permute-start | bytes 1990664 | tf_op jit(solution)/shard_map/ppermute | solution.py:151
  43.3 21.7 %collective-permute-start.13 = (bf16[2,288,1152]{2,1,0:T(8,128)(2,1)}, bf16[2,288,1152]{2,1,0:T(8,128)(2,1)}, u32[]{:S(2)}, u32[]{:S(2)}) collective-permute-start(bf16[2,288,1152]{2,1,0:T(8,128)(2,1)} %get-tuple-element.91), channel_id=1, source_target_pairs={{0,1},{1,0},{2,3},{3,2},{4,5},{5,4},{6,7},{7,6},{8,9},{9,8},{10,11... | collective-permute-start | bytes 3981320 | tf_op jit(solution)/shard_map/ppermute | solution.py:151
  43.9 16.3 %collective-permute-start.10 = (bf16[1,288,1152]{2,1,0:T(8,128)(2,1)S(1)}, bf16[1,288,1152]{2,1,0:T(8,128)(2,1)S(1)}, u32[]{:S(2)}, u32[]{:S(2)}) collective-permute-start(bf16[1,288,1152]{2,1,0:T(8,128)(2,1)S(1)} %collective-permute-done.3.refs_8_), channel_id=1, source_target_pairs={{0,1},{1,0},{2,3},{3,2},{4,5},{5,4},{6,7},{7,6},{8,9},{9,8},{10,11... | collective-permute-start | bytes 1990664 | tf_op jit(solution)/shard_map/ppermute | solution.py:151
  43.9 17.4 %collective-permute-start.9 = (bf16[1,288,1152]{2,1,0:T(8,128)(2,1)S(1)}, bf16[1,288,1152]{2,1,0:T(8,128)(2,1)}, u32[]{:S(2)}, u32[]{:S(2)}) collective-permute-start(bf16[1,288,1152]{2,1,0:T(8,128)(2,1)S(1)} %collective-permute-done.3.refs_8_), channel_id=1, source_target_pairs={{0,16},{16,0},{1,17},{17,1},{2,18},{18,2},{3,19},{19,3},{4,20},{20... | collective-permute-start | bytes 1990664 | tf_op jit(solution)/shard_map/ppermute | solution.py:151
  47.0 13.1 %collective-permute-start.5 = (bf16[160,1152]{1,0:T(8,128)(2,1)}, bf16[160,1152]{1,0:T(8,128)(2,1)S(1)}, u32[]{:S(2)}, u32[]{:S(2)}) collective-permute-start(bf16[160,1152]{1,0:T(8,128)(2,1)} %get-tuple-element.81), channel_id=1, source_target_pairs={{0,12},{4,8},{8,4},{12,0},{1,13},{5,9},{9,5},{13,1},{2,14},{6,10},... | collective-permute-start | bytes 1105928 | tf_op jit(solution)/shard_map/ppermute | solution.py:151
  61.8 17.0 %collective-permute-start.17 = (bf16[1,288,1152]{2,1,0:T(8,128)(2,1)}, bf16[1,288,1152]{2,1,0:T(8,128)(2,1)S(1)}, u32[]{:S(2)}, u32[]{:S(2)}) collective-permute-start(bf16[1,288,1152]{2,1,0:T(8,128)(2,1)} %get-tuple-element.97), channel_id=1, source_target_pairs={{0,2},{1,3},{2,0},{3,1},{4,6},{5,7},{6,4},{7,5},{8,10},{9,11},{10,... | collective-permute-start | bytes 1990664 | tf_op jit(solution)/shard_map/ppermute | solution.py:151
  62.4 16.5 %collective-permute-start.15 = (bf16[1,288,1152]{2,1,0:T(8,128)(2,1)}, bf16[1,288,1152]{2,1,0:T(8,128)(2,1)}, u32[]{:S(2)}, u32[]{:S(2)}) collective-permute-start(bf16[1,288,1152]{2,1,0:T(8,128)(2,1)} %collective-permute-done.8.refs_8_), channel_id=1, source_target_pairs={{0,1},{1,0},{2,3},{3,2},{4,5},{5,4},{6,7},{7,6},{8,9},{9,8},{10,11... | collective-permute-start | bytes 1990664 | tf_op jit(solution)/shard_map/ppermute | solution.py:151
  63.5 17.3 %collective-permute-start.16 = (bf16[1,288,1152]{2,1,0:T(8,128)(2,1)}, bf16[1,288,1152]{2,1,0:T(8,128)(2,1)}, u32[]{:S(2)}, u32[]{:S(2)}) collective-permute-start(bf16[1,288,1152]{2,1,0:T(8,128)(2,1)} %collective-permute-done.8.refs_8_), channel_id=1, source_target_pairs={{0,16},{16,0},{1,17},{17,1},{2,18},{18,2},{3,19},{19,3},{4,20},{20... | collective-permute-start | bytes 1990664 | tf_op jit(solution)/shard_map/ppermute | solution.py:151
  65.0 20.5 %collective-permute-start.19 = (bf16[2,288,1152]{2,1,0:T(8,128)(2,1)}, bf16[2,288,1152]{2,1,0:T(8,128)(2,1)}, u32[]{:S(2)}, u32[]{:S(2)}) collective-permute-start(bf16[2,288,1152]{2,1,0:T(8,128)(2,1)} %get-tuple-element.101), channel_id=1, source_target_pairs={{0,1},{1,0},{2,3},{3,2},{4,5},{5,4},{6,7},{7,6},{8,9},{9,8},{10,11... | collective-permute-start | bytes 3981320 | tf_op jit(solution)/shard_map/ppermute | solution.py:151
  80.8 18.5 %collective-permute-start.22 = (bf16[1,288,1152]{2,1,0:T(8,128)(2,1)S(1)}, bf16[1,288,1152]{2,1,0:T(8,128)(2,1)S(1)}, u32[]{:S(2)}, u32[]{:S(2)}) collective-permute-start(bf16[1,288,1152]{2,1,0:T(8,128)(2,1)S(1)} %collective-permute-done.17.refs_8_), channel_id=1, source_target_pairs={{0,1},{1,0},{2,3},{3,2},{4,5},{5,4},{6,7},{7,6},{8,9},{9,8},{10,11... | collective-permute-start | bytes 1990664 | tf_op jit(solution)/shard_map/ppermute | solution.py:151
  81.3 18.0 %collective-permute-start.23 = (bf16[1,288,1152]{2,1,0:T(8,128)(2,1)S(1)}, bf16[1,288,1152]{2,1,0:T(8,128)(2,1)}, u32[]{:S(2)}, u32[]{:S(2)}) collective-permute-start(bf16[1,288,1152]{2,1,0:T(8,128)(2,1)S(1)} %collective-permute-done.17.refs_8_), channel_id=1, source_target_pairs={{0,16},{16,0},{1,17},{17,1},{2,18},{18,2},{3,19},{19,3},{4,20},{20... | collective-permute-start | bytes 1990664 | tf_op jit(solution)/shard_map/ppermute | solution.py:151
  82.8 23.2 %collective-permute-start.26 = (bf16[2,288,1152]{2,1,0:T(8,128)(2,1)}, bf16[2,288,1152]{2,1,0:T(8,128)(2,1)S(1)}, u32[]{:S(2)}, u32[]{:S(2)}) collective-permute-start(bf16[2,288,1152]{2,1,0:T(8,128)(2,1)} %get-tuple-element.112), channel_id=1, source_target_pairs={{0,1},{1,0},{2,3},{3,2},{4,5},{5,4},{6,7},{7,6},{8,9},{9,8},{10,11... | collective-permute-start | bytes 3981320 | tf_op jit(solution)/shard_map/ppermute | solution.py:151
  84.6 13.8 %collective-permute-start.24 = (bf16[1,144,1152]{2,1,0:T(8,128)(2,1)}, bf16[1,144,1152]{2,1,0:T(8,128)(2,1)}, u32[]{:S(2)}, u32[]{:S(2)}) collective-permute-start(bf16[1,144,1152]{2,1,0:T(8,128)(2,1)} %get-tuple-element.108), channel_id=1, source_target_pairs={{0,2},{1,3},{2,0},{3,1},{4,6},{5,7},{6,4},{7,5},{8,10},{9,11},{10,... | collective-permute-start | bytes 995336 | tf_op jit(solution)/shard_map/ppermute | solution.py:151
  98.4 18.9 %collective-permute-start.30 = (bf16[1,144,1152]{2,1,0:T(8,128)(2,1)}, bf16[1,144,1152]{2,1,0:T(8,128)(2,1)}, u32[]{:S(2)}, u32[]{:S(2)}) collective-permute-start(bf16[1,144,1152]{2,1,0:T(8,128)(2,1)} %get-tuple-element.117), channel_id=1, source_target_pairs={{0,2},{1,3},{2,0},{3,1},{4,6},{5,7},{6,4},{7,5},{8,10},{9,11},{10,... | collective-permute-start | bytes 995336 | tf_op jit(solution)/shard_map/ppermute | solution.py:151
  99.3 18.0 %collective-permute-start.28 = (bf16[1,144,1152]{2,1,0:T(8,128)(2,1)}, bf16[1,144,1152]{2,1,0:T(8,128)(2,1)}, u32[]{:S(2)}, u32[]{:S(2)}) collective-permute-start(bf16[1,144,1152]{2,1,0:T(8,128)(2,1)} %collective-permute-done.24.refs_8_), channel_id=1, source_target_pairs={{0,1},{1,0},{2,3},{3,2},{4,5},{5,4},{6,7},{7,6},{8,9},{9,8},{10,11... | collective-permute-start | bytes 995336 | tf_op jit(solution)/shard_map/ppermute | solution.py:151
  103.6 15.3 %collective-permute-start.29 = (bf16[1,144,1152]{2,1,0:T(8,128)(2,1)}, bf16[1,144,1152]{2,1,0:T(8,128)(2,1)}, u32[]{:S(2)}, u32[]{:S(2)}) collective-permute-start(bf16[1,144,1152]{2,1,0:T(8,128)(2,1)} %collective-permute-done.24.refs_8_), channel_id=1, source_target_pairs={{0,16},{16,0},{1,17},{17,1},{2,18},{18,2},{3,19},{19,3},{4,20},{20... | collective-permute-start | bytes 995336 | tf_op jit(solution)/shard_map/ppermute | solution.py:151
  106.0 22.5 %collective-permute-start.35 = (bf16[2,288,1152]{2,1,0:T(8,128)(2,1)}, bf16[2,288,1152]{2,1,0:T(8,128)(2,1)S(1)}, u32[]{:S(2)}, u32[]{:S(2)}) collective-permute-start(bf16[2,288,1152]{2,1,0:T(8,128)(2,1)} %get-tuple-element.122), channel_id=1, source_target_pairs={{0,1},{1,0},{2,3},{3,2},{4,5},{5,4},{6,7},{7,6},{8,9},{9,8},{10,11... | collective-permute-start | bytes 3981320 | tf_op jit(solution)/shard_map/ppermute | solution.py:151
  141.0 19.2 %collective-permute-start.38 = (bf16[40,1152]{1,0:T(8,128)(2,1)S(1)}, bf16[40,1152]{1,0:T(8,128)(2,1)S(1)}, u32[]{:S(2)}, u32[]{:S(2)}) collective-permute-start(bf16[40,1152]{1,0:T(8,128)(2,1)S(1)} %copy-done.27), channel_id=1, source_target_pairs={{0,12},{4,8},{8,4},{12,0},{1,13},{5,9},{9,5},{13,1},{2,14},{6,10},... | collective-permute-start | bytes 276488 | tf_op jit(solution)/shard_map/ppermute | solution.py:151
  143.7 17.7 %collective-permute-start.37 = (bf16[40,1152]{1,0:T(8,128)(2,1)S(1)}, bf16[40,1152]{1,0:T(8,128)(2,1)S(1)}, u32[]{:S(2)}, u32[]{:S(2)}) collective-permute-start(bf16[40,1152]{1,0:T(8,128)(2,1)S(1)} %pad_maximum_fusion.2), channel_id=1, source_target_pairs={{0,8},{4,12},{8,0},{12,4},{1,9},{5,13},{9,1},{13,5},{2,10},{6,14},... | collective-permute-start | bytes 276488 | tf_op jit(solution)/shard_map/ppermute | solution.py:151
  149.1 12.3 %collective-permute-start.36 = (bf16[40,1152]{1,0:T(8,128)(2,1)S(1)}, bf16[40,1152]{1,0:T(8,128)(2,1)S(1)}, u32[]{:S(2)}, u32[]{:S(2)}) collective-permute-start(bf16[40,1152]{1,0:T(8,128)(2,1)S(1)} %pad_maximum_fusion.1), channel_id=1, source_target_pairs={{0,4},{4,0},{8,12},{12,8},{1,5},{5,1},{9,13},{13,9},{2,6},{6,2},{1... | collective-permute-start | bytes 276488 | tf_op jit(solution)/shard_map/ppermute | solution.py:151
  (58 other events, 522.5 us)

commit v3 on v0

--- a/solution.py
+++ b/solution.py
@@ -1,6 +1,11 @@
+import functools
+
 import jax
 import jax.numpy as jnp
+import numpy as np
 from jax import lax
+from jax.experimental import pallas as pl
+from jax.experimental.pallas import tpu as pltpu
 from jax.sharding import PartitionSpec as P
 
 EXPERTS = 16
@@ -78,7 +83,9 @@
     return produced.astype(jnp.bfloat16)
 
 
-def local(hidden_states, expert_ids, modulation, router_weight, w_in, b_in, w_out):
+def gathered_weights(
+    hidden_states, expert_ids, modulation, router_weight, w_in, b_in, w_out
+):
     token_count = hidden_states.shape[1]
     width = hidden_states.shape[2]
     tokens = hidden_states.reshape(token_count, width)
@@ -140,6 +147,523 @@
     return result.reshape(1, token_count, width)
 
 
+def crossed(block, axis, mask):
+    count = lax.axis_size(axis)
+    return lax.ppermute(block, axis, [(i, i ^ mask) for i in range(count)])
+
+
+def after(value, *events):
+    return lax.optimization_barrier((value, *events))[0] if events else value
+
+
+def slot_rows(ids, experts_count):
+    tokens = ids[0].shape[1]
+    experts = lax.broadcasted_iota(jnp.int32, (experts_count, tokens), 0).astype(jnp.float32)
+    chosen = [jnp.where(experts == row, 1.0, 0.0) for row in ids]
+    earlier = jnp.where(
+        lax.broadcasted_iota(jnp.int32, (tokens, tokens), 0)
+        < lax.broadcasted_iota(jnp.int32, (tokens, tokens), 1),
+        1.0,
+        0.0,
+    )
+    before = jnp.dot(
+        (chosen[0] + chosen[1]).astype(jnp.bfloat16),
+        earlier.astype(jnp.bfloat16),
+        preferred_element_type=jnp.float32,
+    )
+    return [jnp.sum(before * one, axis=0, keepdims=True) for one in chosen]
+
+
+def prepare_kernel(tokens_ref, ids_ref, settings_ref, out_ref):
+    count, width = tokens_ref.shape[1:]
+    out_ref[:count, :] = modulate(tokens_ref[0], settings_ref[0:1, :], settings_ref[1:2, :])
+    ids = [ids_ref[0:1, :], ids_ref[1:2, :]]
+    listed = [*ids, *slot_rows(ids, EXPERTS), jnp.zeros((1, width - 4 * count), jnp.float32)]
+    row = jnp.concatenate(listed, axis=1)
+    first = lax.broadcasted_iota(jnp.int32, (16, width), 0) == 0
+    out_ref[count:, :] = jnp.where(first, row, 0.0).astype(jnp.bfloat16)
+
+
+def prepare_call(hidden_states, ids, settings):
+    count, width = hidden_states.shape[1:]
+    return pl.pallas_call(
+        prepare_kernel,
+        out_shape=jax.ShapeDtypeStruct((count + 16, width), jnp.bfloat16),
+        name="prepare",
+    )(hidden_states, ids, settings)
+
+
+def route_kernel(block_ref, router_ref, out_ref):
+    count = out_ref.shape[0]
+    listed = block_ref[count:, :].astype(jnp.float32)[0:1, :]
+    place = lax.broadcasted_iota(jnp.int32, (count, count), 0)
+    spread = jnp.zeros((count, count), jnp.float32)
+    for k in range(4):
+        spread = jnp.where(place == k, listed[:, k * count : (k + 1) * count], spread)
+    columns = spread.T
+    logits = jnp.dot(block_ref[:count, :], router_ref[...], preferred_element_type=jnp.float32)
+    experts = lax.broadcasted_iota(jnp.int32, logits.shape, 1).astype(jnp.float32)
+    picked = [
+        jnp.sum(jnp.where(experts == columns[:, k : k + 1], logits, 0.0), axis=1, keepdims=True)
+        for k in range(2)
+    ]
+    gap = picked[0] - picked[1]
+    lanes = lax.broadcasted_iota(jnp.int32, (count, count), 1)
+    columns = jnp.where(lanes == 4, jax.nn.sigmoid(gap), columns)
+    out_ref[...] = jnp.where(lanes == 5, jax.nn.sigmoid(-gap), columns)
+
+
+def route_call(block, router_weight):
+    count = block.shape[0] - 16
+    return pl.pallas_call(
+        route_kernel,
+        out_shape=jax.ShapeDtypeStruct((count, count), jnp.float32),
+        name="route",
+    )(block, router_weight)
+
+
+def dispatch_kernel(wanted_ref, *refs):
+    rows, images = wanted_ref.shape
+    blocks, outs = refs[:images], refs[images:]
+    count = blocks[0].shape[0] - 16
+    places = []
+    for block in blocks:
+        listed = block[count:, :].astype(jnp.float32)[0:1, :]
+        parts = [listed[:, k * count : (k + 1) * count] for k in range(4)]
+        places.append([parts[k] * CAP + parts[2 + k] for k in range(2)])
+    tokens = jnp.concatenate([block[:count, :] for block in blocks], axis=0)
+    owner = lax.axis_index("ep")
+    for number, out_ref in enumerate(outs):
+        first = (owner ^ number) * (rows // images)
+        choices = []
+        for image in range(images):
+            wanted = wanted_ref[:, image : image + 1] + first.astype(jnp.float32)
+            match = (wanted == places[image][0]) | (wanted == places[image][1])
+            choices.append(jnp.where(match, 1.0, 0.0).astype(jnp.bfloat16))
+        out_ref[...] = jnp.dot(
+            jnp.concatenate(choices, axis=1), tokens, preferred_element_type=jnp.float32
+        ).astype(jnp.bfloat16)
+
+
+def dispatch_call(wanted, blocks, members):
+    rows = wanted.shape[0]
+    width = blocks[0].shape[1]
+    return pl.pallas_call(
+        dispatch_kernel,
+        out_shape=[jax.ShapeDtypeStruct((rows, width), jnp.bfloat16)] * members,
+        cost_estimate=pl.CostEstimate(
+            flops=2 * members * rows * len(blocks) * blocks[0].shape[0] * width,
+            bytes_accessed=4 * members * rows * width,
+            transcendentals=0,
+        ),
+        name="dispatch",
+    )(wanted, *blocks)
+
+
+def halves_turned(tile):
+    half = tile.shape[1] // 2
+    return pltpu.roll(tile.astype(jnp.float32), half, 1).astype(tile.dtype)
+
+
+def where_am_i():
+    here, part = lax.axis_index("fs"), lax.axis_index("parts")
+    return here, part, here & 1
+
+
+def cut_kernel(groups, w_in_ref, *refs):
+    outs, (held, tiles, sems) = refs[:-3], refs[-3:]
+    experts, depth, lanes = tiles.shape
+    upper = depth // 2
+    slots = [(g, at) for g, group in enumerate(groups) for at in range(len(group))]
+    wide = held.shape[2]
+    main = (wide - lanes) // 2
+    here, part, core = where_am_i()
+    chip = here >> 1
+    first = (1 - chip) * wide
+    rest = [
+        pltpu.make_async_copy(
+            w_in_ref.at[SPLIT * e + part, :, pl.ds(pl.multiple_of(first + main, 128), lanes)],
+            tiles.at[e],
+            sems.at[0, e],
+        )
+        for e in range(experts)
+    ]
+    arriving, leaving = [], []
+    for number in range(2 * experts):
+        e, target = number // 2, core ^ (number % 2)
+        group, at = slots[e]
+        out = outs[2 * group + number % 2].at[pl.ds(at * upper, upper), :]
+        columns = pl.ds(pl.multiple_of(first + target * (main + lanes), 128), main)
+        arriving.append(
+            [
+                pltpu.make_async_copy(
+                    w_in_ref.at[SPLIT * e + part, pl.ds(half * upper, upper), columns],
+                    held.at[number, :, pl.ds(half * main, main)],
+                    sems.at[1 + half, number],
+                )
+                for half in range(2)
+            ]
+        )
+        leaving.append(pltpu.make_async_copy(held.at[number], out, sems.at[3, number]))
+    for copy in rest:
+        copy.start()
+    for halves in arriving:
+        for copy in halves:
+            copy.start()
+    left = lax.broadcasted_iota(jnp.int32, (upper, lanes), 1) < lanes // 2
+    for number, halves in enumerate(arriving):
+        e, target = number // 2, core ^ (number % 2)
+        if number % 2 == 0:
+            rest[e].wait()
+        top, bottom = tiles[e, :upper, :], tiles[e, upper:, :]
+        low = jnp.where(left, top, halves_turned(bottom))
+        high = jnp.where(left, halves_turned(top), bottom)
+        held[number, :, 2 * main :] = jnp.where(target == 0, low, high)
+        for copy in halves:
+            copy.wait()
+        leaving[number].start()
+    for copy in leaving:
+        copy.wait()
+
+
+def cut_call(w_in, wide, groups):
+    units, depth, _ = w_in.shape
+    experts = units // SPLIT
+    anywhere = pl.BlockSpec(memory_space=pl.ANY)
+    blocks = 2 * experts
+    return pl.pallas_call(
+        functools.partial(cut_kernel, groups),
+        in_specs=[anywhere],
+        out_specs=[anywhere] * (2 * len(groups)),
+        out_shape=[
+            jax.ShapeDtypeStruct((len(group) * (depth // 2), wide), jnp.bfloat16)
+            for group in groups
+            for _ in range(2)
+        ],
+        scratch_shapes=[
+            pltpu.VMEM((blocks, depth // 2, wide), jnp.bfloat16),
+            pltpu.VMEM((experts, depth, 128), jnp.bfloat16),
+            pltpu.SemaphoreType.DMA((4, blocks)),
+        ],
+        compiler_params=pltpu.CompilerParams(vmem_limit_bytes=60 << 20),
+        cost_estimate=pl.CostEstimate(
+            flops=0, bytes_accessed=4 * blocks * (depth // 2) * wide, transcendentals=0
+        ),
+        name="cut",
+    )(w_in)
+
+
+def expert_kernel(expert, sources, offsets, events, own_ref, b_ref, out_w_ref, *refs):
+    x_refs, refs = refs[:sources], refs[sources:]
+    near_ref, moved_refs, refs = refs[0], refs[1:5], refs[5 + events :]
+    keep_ref, keep_far_ref, send_ref, *refs = refs
+    x_pairs, x_held, weight, rest, bias, out_weight, total, sems = refs
+    here, part, core = where_am_i()
+    depth = own_ref.shape[1]
+    columns, width = out_w_ref.shape[1:]
+    upper, lanes = rest.shape[2:]
+    slab = weight.shape[2]
+    skip = slab - columns
+    wide = 2 * columns
+    main = slab - lanes
+    chip_first = pl.multiple_of((here >> 1) * wide + core * (wide - slab), 128)
+    half_rows = x_held.shape[0] // 2
+    per = x_pairs.shape[1] // 2
+
+    def rows(device, offset, size):
+        return pl.ds(pl.multiple_of(device * depth + offset, 16), size)
+
+    made = [[] for _ in range(SPLIT)]
+    for number in range(SPLIT):
+        unit = SPLIT * expert + (number ^ part)
+
+        def add(source, target, number=number):
+            copy = pltpu.make_async_copy(source, target, sems.at[number, len(made[number])])
+            made[number].append(copy)
+
+        for ref, device in ((own_ref, here), (near_ref, here ^ 1)):
+            add(
+                ref.at[unit, :, pl.ds(chip_first, slab)],
+                weight.at[number, rows(device, 0, depth), :],
+            )
+        for at in range(2):
+            moved = moved_refs[2 * number + at]
+            moved_rows = pl.ds(offsets[2 * number + at], upper)
+            for half in range(2):
+                add(
+                    moved.at[moved_rows, pl.ds(half * main, main)],
+                    weight.at[
+                        number,
+                        rows(here ^ (2 + at), half * upper, upper),
+                        pl.ds(pl.multiple_of(core * lanes, 128), main),
+                    ],
+                )
+            add(moved.at[moved_rows, pl.ds(2 * main, lanes)], rest.at[number, at])
+        add(b_ref.at[unit], bias.at[number])
+        add(
+            out_w_ref.at[unit],
+            out_weight.at[number, pl.ds(pl.multiple_of(core * skip, 16), columns), :],
+        )
+
+    spare_sem = sems.shape[1] - sources
+    x_copies = [
+        pltpu.make_async_copy(
+            x_ref.at[pl.ds(2 * per * (expert // 2), 2 * per), :],
+            x_pairs.at[at],
+            sems.at[0, spare_sem + at],
+        )
+        for at, x_ref in enumerate(x_refs)
+    ]
+    for copy in x_copies + made[0] + made[1]:
+        copy.start()
+    for number in range(SPLIT):
+        spare = pl.ds(pl.multiple_of((1 - core) * columns, 16), skip)
+        out_weight[number, spare, :] = jnp.zeros((skip, width), out_weight.dtype)
+    for at, copy in enumerate(x_copies):
+        copy.wait()
+        pair = x_pairs[at].astype(jnp.float32)
+        own_rows = pair[per * (expert % 2) : per * (expert % 2 + 1), :]
+        total[per * at : per * (at + 1), :] = own_rows
+    x_held[...] = total[...].astype(jnp.bfloat16)
+
+    for number in range(SPLIT):
+        for copy in made[number][:-1]:
+            copy.wait()
+        for at in range(2):
+            tile = rest[number, at]
+            turned = halves_turned(tile)
+            for half in range(2):
+                at_rows = rows(here ^ (2 + at), half * upper, upper)
+                value = jnp.where(core == half, tile, turned)
+                tail = pl.ds(pl.multiple_of((1 - core) * main, 128), lanes)
+                weight[number, at_rows, tail] = value
+        pre = jnp.dot(x_held[...], weight[number], preferred_element_type=jnp.float32)
+        hidden = jax.nn.gelu(pre + bias[number], approximate=True).astype(jnp.bfloat16)
+        made[number][-1].wait()
+        piece = jnp.dot(hidden, out_weight[number], preferred_element_type=jnp.float32)
+        total[...] = piece if number == 0 else total[...] + piece
+
+    members = half_rows // (2 * CAP)
+    for member in range(members):
+        at = 2 * CAP * member
+        keep_ref[CAP * member : CAP * (member + 1), :] = total[at : at + CAP, :]
+        keep_far_ref[CAP * member : CAP * (member + 1), :] = total[at + CAP : at + 2 * CAP, :]
+    given = [
+        total[at : at + CAP, :]
+        for image in range(2)
+        for at in range(half_rows + CAP * image, 2 * half_rows, 2 * CAP)
+    ]
+    for number, rows_of in enumerate(given):
+        total[CAP * number : CAP * (number + 1), :] = rows_of
+    send_ref[...] = total[:half_rows, :].astype(jnp.bfloat16)
+
+
+def expert_call(expert, xs, own, b, w_out, near, moved, events):
+    width = w_out.shape[2]
+    per = 2 * CAP
+    half_rows = per * len(xs) // 2
+    depth = own.shape[1]
+    columns = w_out.shape[1]
+    slab = b.shape[2]
+    anywhere = pl.BlockSpec(memory_space=pl.ANY)
+
+    return pl.pallas_call(
+        functools.partial(
+            expert_kernel, expert, len(xs), [offset for _, offset in moved], len(events)
+        ),
+        in_specs=[anywhere] * (4 + len(xs) + len(moved) + len(events)),
+        out_specs=[pl.BlockSpec(memory_space=pltpu.VMEM)] * 3,
+        scratch_shapes=[
+            pltpu.VMEM((len(xs), 2 * per, width), jnp.bfloat16),
+            pltpu.VMEM((2 * half_rows, width), jnp.bfloat16),
+            pltpu.VMEM((SPLIT, width, slab), jnp.bfloat16),
+            pltpu.VMEM((SPLIT, 2, depth // 2, 128), jnp.bfloat16),
+            pltpu.VMEM((SPLIT, 1, slab), jnp.float32),
+            pltpu.VMEM((SPLIT, slab, width), jnp.bfloat16),
+            pltpu.VMEM((2 * half_rows, width), jnp.float32),
+            pltpu.SemaphoreType.DMA((SPLIT, 10 + len(xs))),
+        ],
+        out_shape=[
+            jax.ShapeDtypeStruct((half_rows // 2, width), jnp.float32),
+            jax.ShapeDtypeStruct((half_rows // 2, width), jnp.float32),
+            jax.ShapeDtypeStruct((half_rows, width), jnp.bfloat16),
+        ],
+        compiler_params=pltpu.CompilerParams(vmem_limit_bytes=54 << 20),
+        cost_estimate=pl.CostEstimate(
+            flops=2 * SPLIT * 2 * 2 * half_rows * width * columns,
+            bytes_accessed=3 * (2 * SPLIT * 2 * width * columns + 16 * half_rows * width),
+            transcendentals=SPLIT * 2 * half_rows * columns,
+        ),
+        name="expert",
+    )(own, b, w_out, *xs, near, *[held for held, _ in moved], *events)
+
+
+def combine_kernel(experts, group, last, route_ref, *refs):
+    refs, held = refs[:-1], refs[-1]
+    refs, out_ref = refs[:-1], refs[-1]
+    before_ref = None
+    if last:
+        (before_ref, tokens_ref, settings_ref), refs = refs[:3], refs[3:]
+    count = route_ref.shape[0]
+    members = len(refs)
+    size = len(group) * CAP
+    for at, reply in enumerate(refs):
+        held[at * size : (at + 1) * size, :] = reply[...].astype(jnp.float32)
+    rows = held[...].astype(jnp.bfloat16)
+    place = lax.broadcasted_iota(jnp.int32, (count, members * size), 1).astype(jnp.float32)
+    row = lax.axis_index("ep")
+    branch = before_ref[...] if last else None
+    for k in range(2):
+        expert, slot = route_ref[:, k : k + 1], route_ref[:, 2 + k : 3 + k]
+        at = jnp.full_like(expert, -1.0)
+        for ring in range(members):
+            first = (row ^ ring) * experts + group[0]
+            local = expert - first.astype(jnp.float32)
+            inside = (local >= 0) & (local < len(group))
+            at = jnp.where(inside, ring * size + local * CAP + slot, at)
+        select = jnp.where(place == at, 1.0, 0.0).astype(jnp.bfloat16)
+        term = route_ref[:, 4 + k : 5 + k] * jnp.dot(
+            select, rows, preferred_element_type=jnp.float32
+        )
+        branch = term if branch is None else branch + term
+    if last:
+        tokens = tokens_ref[0].astype(jnp.float32)
+        out_ref[0] = (tokens + settings_ref[2:3, :] * branch).astype(out_ref.dtype)
+    else:
+        out_ref[...] = branch
+
+
+def combine_call(experts, group, route, replies, final=None):
+    width = replies[0].shape[1]
+    out = jax.ShapeDtypeStruct((route.shape[0], width), jnp.float32)
+    if final:
+        out = jax.ShapeDtypeStruct(final[1].shape, final[1].dtype)
+    return pl.pallas_call(
+        functools.partial(combine_kernel, experts, group, bool(final)),
+        out_shape=out,
+        scratch_shapes=[pltpu.VMEM((len(replies) * len(group) * CAP, width), jnp.float32)],
+        name="combine",
+    )(route, *(final or ()), *replies)
+
+
+def recut_weights(hidden_states, expert_ids, modulation, router_weight, w_in, b_in, w_out):
+    units, depth, _ = w_in.shape
+    columns = w_out.shape[1]
+    wide = 2 * columns
+    experts = units // SPLIT
+    members = lax.axis_size("ep")
+    here = lax.axis_index("fs")
+    core, chip = here & 1, here >> 1
+    settings = modulation[0]
+
+    def over(held, *events):
+        return crossed(after(held, *events), "fs", 1)
+
+    def beside(held, *events):
+        return crossed(after(held, *events), "parts", 1)
+
+    slab = -(-columns // 128) * 128
+    own_b = lax.dynamic_slice(
+        b_in, (0, chip * wide + core * (wide - slab)), (units, slab)
+    )[:, None, :]
+    place = np.arange(experts * 2 * CAP)
+    image = place // CAP % 2
+    wanted = np.where(
+        image[:, None] == np.arange(2), (place // (2 * CAP) * CAP + place % CAP)[:, None], -np.inf
+    ).astype(np.float32)
+
+    ids = expert_ids[0].T.astype(jnp.float32)
+    block = prepare_call(hidden_states, ids, settings)
+    gate = after(here, block)
+    near = over(w_in)
+    opposite = crossed(after(block, gate), "fs", 2)
+    upper = depth // 2
+    fetched = ((0,), tuple(range(1, experts - 1)), (experts - 1,))
+    cuts = cut_call(after(w_in, gate), wide, fetched)
+
+    def fetch(number, *events):
+        return crossed(after(cuts[number], *events), "fs", 2 + number % 2)
+
+    def exchange(number, gate):
+        size = len(fetched[number // 2])
+        blocks = [far[number][at * upper : (at + 1) * upper] for at in range(size)]
+        return [beside(held, gate) for held in blocks]
+
+    def run(expert, *events):
+        group = [expert in held for held in fetched].index(True)
+        at = fetched[group].index(expert)
+        moved = [(far[2 * group + k], at * upper) for k in range(2)]
+        moved += [(other[2 * group + k][at], 0) for k in range(2)]
+        return expert_call(expert, arrived + across, w_in, own_b, w_out, near, moved, events)
+
+    far, other, outs = [fetch(0), fetch(1)], [], []
+    opposite, near = lax.optimization_barrier((opposite, near))
+    sending = dispatch_call(jnp.asarray(wanted), [block, opposite], members)
+    arrived = [sending[0], crossed(sending[1], "ep", 1), crossed(sending[2], "ep", 2)]
+    far.append(fetch(2, opposite))
+    gate = after(gate, far[0], far[1], near)
+
+    far.append(fetch(3, gate))
+    other += [exchange(0, gate), exchange(1, gate)]
+    gate = after(gate, far[2], *other[0], *other[1], arrived[1], arrived[2])
+
+    far.append(fetch(4, gate))
+    other.append(exchange(2, gate))
+    arrived.append(crossed(after(sending[3], gate), "ep", 3))
+    gate = after(gate, far[3], *other[2])
+
+    far.append(fetch(5, gate))
+    other.append(exchange(3, gate))
+    gate = after(gate, far[4], arrived[3])
+
+    other.append(exchange(4, gate))
+    across = [over(held, gate) for held in arrived]
+    route = route_call(block, router_weight)
+    outs.append(run(0, route))
+    gate = after(gate, far[5], *other[3])
+    other.append(exchange(5, gate))
+    half_rows = members * CAP
+
+    def give(expert):
+        held = outs[expert][1] + sent[expert][half_rows:].astype(jnp.float32)
+        return crossed(held.astype(jnp.bfloat16), "fs", 2)
+
+    sent = [over(outs[0][2])]
+    outs.append(run(1, outs[0][0]))
+    sent.append(over(outs[1][2]))
+    given = [give(0), give(1)]
+    outs.append(run(2, *sent))
+    sent.append(over(outs[2][2]))
+    given.append(give(2))
+    outs.append(run(3, *given[:2]))
+    sent.append(over(outs[3][2]))
+    given.append(give(3))
+
+    branch = None
+    for group in (tuple(range(experts // 2)), tuple(range(experts // 2, experts))):
+        wholes = []
+        for e in group:
+            half = outs[e][0] + sent[e][:half_rows].astype(jnp.float32)
+            wholes.append((half + given[e].astype(jnp.float32)).astype(jnp.bfloat16))
+        replies = []
+        for d in range(members):
+            reply = jnp.concatenate([held[d * CAP : (d + 1) * CAP] for held in wholes])
+            replies.append(crossed(after(reply, sent[3]), "ep", d) if d else reply)
+        if not group[0]:
+            branch = combine_call(experts, group, route, replies)
+        else:
+            final = (branch, hidden_states, settings)
+            branch = combine_call(experts, group, route, replies, final)
+    return branch
+
+
+def local(*arrays):
+    w_in = arrays[4]
+    recut = lax.axis_size("fs") == lax.axis_size("ep") == 4 and lax.axis_size("parts") == 2
+    recut = recut and w_in.shape[0] == 4 * SPLIT and arrays[6].shape[1] % 128 == 64
+    return (recut_weights if recut else gathered_weights)(*arrays)
+
+
 def solution(mesh):
     placed = (
         P(("parts", "fs"), "ep", None),

time: 588 us -> 157 us (0.27)
  waiting for transfers between devices: 517 us -> 51.6 us
  Pallas kernels: 0 us -> 43.3 us
  starting transfers between devices: 11 us -> 42.8 us
  matrix products: 31.7 us -> 0 us
  between operations: 13.7 us -> 0.53 us
    all_gather x2 -> x0, waiting for transfers between devices: 478 us -> none  [the longest x1 255 us: expert_compute(): lax.all_gather(w_out, 'fs', axis=1, tiled=True)]
    ppermute x0 -> x37, waiting for transfers between devices: none -> 51.6 us  [crossed(): return lax.ppermute(block, axis, [(i, i ^ mask) for i in range(count)])]
    pallas_call x0 -> x10, Pallas kernels: none -> 43.3 us  [the longest x4 28.9 us: expert_call(): pl.pallas_call(functools.partial(expert_kernel, expert, len(xs), [offset...]
    ppermute x0 -> x37, starting transfers between devices: none -> 42.8 us  [crossed(): return lax.ppermute(block, axis, [(i, i ^ mask) for i in range(count)])]
    all_to_all x2 -> x0, waiting for transfers between devices: 38 us -> none  [the longest x1 21.3 us: local(): lax.all_to_all(sending, 'ep', split_axis=0, concat_axis=1, tiled=True)]
    dot_general x3 -> x0, matrix products: 31.7 us -> none  [the longest x1 30.4 us: expert_compute(): jnp.einsum('urf,ufd->urd', columns, lax.all_gather(w_out, 'fs', axis=1, t...]
    all_to_all x2 -> x0, starting transfers between devices: 10.9 us -> none  [the longest x1 6.32 us: local(): lax.all_to_all(sending, 'ep', split_axis=0, concat_axis=1, tiled=True)]
    unnamed x25 -> x80, local copies, waits for them, and re-layouts: 0.17 us -> 8.09 us
  transfers between devices with their start and end apart: 4 -> 37, of which waited for: 4 -> 12; matrix products, arithmetic and copies ran while one was open for 1% -> 7% of each run, Pallas kernels for 0% -> 21%
where the time goes in v3:
time: 157 us; the launch traced here: 156 us
  waiting for transfers between devices  51.6 us (33%)
  Pallas kernels  43.3 us (28%)
  starting transfers between devices  42.8 us (27%)
  local copies, waits for them, and re-layouts  9.78 us (6%)
  other arithmetic  8.21 us (5%)
    ppermute x37, waiting for transfers between devices, crossed(): return lax.ppermute(block, axis, [(i, i ^ mask) for i in range(count)])  51.6 us
    ppermute x37, starting transfers between devices, crossed(): return lax.ppermute(block, axis, [(i, i ^ mask) for i in range(count)])  42.8 us
    pallas_call x4, Pallas kernels, expert_call(): pl.pallas_call(functools.partial(expert_kernel, expert, len(xs), [offset...  28.9 us
    unnamed x80, local copies, waits for them, and re-layouts  8.09 us
    pallas_call x2, Pallas kernels, combine_call(): pl.pallas_call(functools.partial(combine_kernel, experts, group, bool(fin...  4.84 us
    convert_element_type x4, other arithmetic, recut_weights(): wholes.append((half + given[e].astype(jnp.float32)).astype(jnp.bfloat16))  3.24 us
  transfers between devices with their start and end apart: 37, of which 12 were waited for; matrix products, arithmetic and copies ran while one was open for 7% of the time, Pallas kernels for 21%

profile of v3, /device:TPU:0, one launch (start us, length us, event | category | flops | bytes accessed | tf_op | source)
XLA Modules:
  0.0 156.2 jit_solution(3437718992797039882)
XLA Ops:
  5.0 2.5 %collective-permute-start = (bf16[144,1152]{1,0:T(8,128)(2,1)}, bf16[144,1152]{1,0:T(8,128)(2,1)S(1)}, u32[]{:S(2)}, u32[]{:S(2)}) collective-permute-start(bf16[144,1152]{1,0:T(8,128)(2,1)} %prepare.1.block_ref.refs_0_), channel_id=1, source_target_pairs={{0,2},{1,3},{2,0},{3,1},{4,6},{5,7},{6,4},{7,5},{8,10},{9,11},{10,... | collective-permute-start | bytes 995336 | tf_op jit(solution)/shard_map/ppermute | solution.py:152
  7.5 3.0 %cut.1 = (bf16[144,1152]{1,0:T(8,128)(2,1)}, bf16[144,1152]{1,0:T(8,128)(2,1)}, bf16[288,1152]{1,0:T(8,128)(2,1)}, bf16[288,1152]{1,0:T(8,128)(2,1)}, bf16[144,1...) custom-call(bf16[8,288,2304]{2,1,0:T(8,128)(2,1)} %own_ref.7), custom_call_target="tpu_custom_call" | custom-call | bytes 5308416 | tf_op jit(solution)/shard_map/cut/pallas_call | solution.py:334
  12.1 4.3 %collective-permute-done.refs_1_ = bf16[144,1152]{1,0:T(8,128)(2,1)S(1)} collective-permute-done((bf16[144,1152]{1,0:T(8,128)(2,1)}, bf16[144,1152]{1,0:T(8,128)(2,1)S(1)}, u32[]{:S(2)}, u32[]{:S(2)}) %collective-permute-start) | collective-permute-done | bytes 331808 | tf_op jit(solution)/shard_map/ppermute | solution.py:152
  16.8 2.9 %collective-permute-start.6 = (bf16[288,1152]{1,0:T(8,128)(2,1)}, bf16[288,1152]{1,0:T(8,128)(2,1)S(1)}, u32[]{:S(2)}, u32[]{:S(2)}) collective-permute-start(bf16[288,1152]{1,0:T(8,128)(2,1)} %get-tuple-element.71), channel_id=1, source_target_pairs={{0,2},{1,3},{2,0},{3,1},{4,6},{5,7},{6,4},{7,5},{8,10},{9,11},{10,... | collective-permute-start | bytes 1990664 | tf_op jit(solution)/shard_map/ppermute | solution.py:152
  19.6 2.6 %dispatch.1 = (bf16[160,1152]{1,0:T(8,128)(2,1)}, bf16[160,1152]{1,0:T(8,128)(2,1)}, bf16[160,1152]{1,0:T(8,128)(2,1)}, bf16[160,1152]{1,0:T(8,128)(2,1)}) custom-call(f32[160,2]{1,0:T(8,128)} %constant.16.clone.wanted_ref, bf16[144,1152]{1,0:T(8,128)(2,1)} %prepare.1.block_ref.refs_0_, bf16[144,1152]{1,0:T(8,128)(2,1)} %copy-done.38), custom_call_target="tpu_custom_call" | custom-call | flops 424673280 | bytes 2949120 | tf_op jit(solution)/shard_map/dispatch/pallas_call | solution.py:251
  23.8 2.6 %collective-permute-start.3 = (bf16[160,1152]{1,0:T(8,128)(2,1)}, bf16[160,1152]{1,0:T(8,128)(2,1)S(1)}, u32[]{:S(2)}, u32[]{:S(2)}) collective-permute-start(bf16[160,1152]{1,0:T(8,128)(2,1)} %get-tuple-element.63), channel_id=1, source_target_pairs={{0,8},{4,12},{8,0},{12,4},{1,9},{5,13},{9,1},{13,5},{2,10},{6,14},... | collective-permute-start | bytes 1105928 | tf_op jit(solution)/shard_map/ppermute | solution.py:152
  26.4 3.8 %collective-permute-done.5.refs_10_ = bf16[144,1152]{1,0:T(8,128)(2,1)S(1)} collective-permute-done((bf16[144,1152]{1,0:T(8,128)(2,1)}, bf16[144,1152]{1,0:T(8,128)(2,1)S(1)}, u32[]{:S(2)}, u32[]{:S(2)}) %collective-permute-start.5) | collective-permute-done | bytes 331808 | tf_op jit(solution)/shard_map/ppermute | solution.py:152
  32.2 8.7 %collective-permute-done.7.refs_11_ = bf16[144,1152]{1,0:T(8,128)(2,1)} collective-permute-done((bf16[144,1152]{1,0:T(8,128)(2,1)S(1)}, bf16[144,1152]{1,0:T(8,128)(2,1)}, u32[]{:S(2)}, u32[]{:S(2)}) %collective-permute-start.7) | collective-permute-done | bytes 331808 | tf_op jit(solution)/shard_map/ppermute | solution.py:152
  42.2 5.6 %collective-permute-done.8.refs_12_ = bf16[144,1152]{1,0:T(8,128)(2,1)S(1)} collective-permute-done((bf16[144,1152]{1,0:T(8,128)(2,1)S(1)}, bf16[144,1152]{1,0:T(8,128)(2,1)S(1)}, u32[]{:S(2)}, u32[]{:S(2)}) %collective-permute-start.8) | collective-permute-done | bytes 331808 | tf_op jit(solution)/shard_map/ppermute | solution.py:152
  48.5 3.8 %collective-permute-start.9 = (bf16[160,1152]{1,0:T(8,128)(2,1)}, bf16[160,1152]{1,0:T(8,128)(2,1)S(1)}, u32[]{:S(2)}, u32[]{:S(2)}) collective-permute-start(bf16[160,1152]{1,0:T(8,128)(2,1)} %get-tuple-element.75), channel_id=1, source_target_pairs={{0,12},{4,8},{8,4},{12,0},{1,13},{5,9},{9,5},{13,1},{2,14},{6,10},... | collective-permute-start | bytes 1105928 | tf_op jit(solution)/shard_map/ppermute | solution.py:152
  55.9 2.7 %collective-permute-done.10.refs_10_ = bf16[288,1152]{1,0:T(8,128)(2,1)S(1)} collective-permute-done((bf16[288,1152]{1,0:T(8,128)(2,1)}, bf16[288,1152]{1,0:T(8,128)(2,1)S(1)}, u32[]{:S(2)}, u32[]{:S(2)}) %collective-permute-start.10) | collective-permute-done | bytes 663584 | tf_op jit(solution)/shard_map/ppermute | solution.py:152
  58.6 4.5 %collective-permute-done.11.refs_11_ = bf16[144,1152]{1,0:T(8,128)(2,1)S(1)} collective-permute-done((bf16[144,1152]{1,0:T(8,128)(2,1)S(1)}, bf16[144,1152]{1,0:T(8,128)(2,1)S(1)}, u32[]{:S(2)}, u32[]{:S(2)}) %collective-permute-start.11) | collective-permute-done | bytes 331808 | tf_op jit(solution)/shard_map/ppermute | solution.py:152
  63.1 6.0 %collective-permute-done.12.refs_11_ = bf16[144,1152]{1,0:T(8,128)(2,1)S(1)} collective-permute-done((bf16[144,1152]{1,0:T(8,128)(2,1)S(1)}, bf16[144,1152]{1,0:T(8,128)(2,1)S(1)}, u32[]{:S(2)}, u32[]{:S(2)}) %collective-permute-start.12) | collective-permute-done | bytes 331808 | tf_op jit(solution)/shard_map/ppermute | solution.py:152
  73.7 2.0 %route.1.refs_13_.route_ref = f32[128,128]{1,0:T(8,128)} custom-call(bf16[144,1152]{1,0:T(8,128)(2,1)} %prepare.1.block_ref.refs_0_, bf16[1152,16]{1,0:T(8,128)(2,1)} %copy.9.router_ref), custom_call_target="tpu_custom_call" | custom-call | tf_op jit(solution)/shard_map/route/pallas_call | solution.py:218
  77.2 7.1 %expert.4 = (f32[80,1152]{1,0:T(8,128)}, f32[80,1152]{1,0:T(8,128)}, bf16[160,1152]{1,0:T(8,128)(2,1)}) custom-call(bf16[8,288,2304]{2,1,0:T(8,128)(2,1)} %own_ref.7, f32[8,1,640]{2,1,0:T(1,128)} %broadcast_in_dim.3.b_ref, bf16[8,576,1152]{2,1,0:T(8,128)(2,1)} %out_w_ref.7, bf16[160,1152]{1,0:T(8,128)(2,1)} %get-tuple-element.84.refs_0_, ...), custom_call_target="tpu_custom_call" | custom-call | flops 1698693120 | bytes 24772608 | tf_op jit(solution)/shard_map/expert/pallas_call | solution.py:470
  84.4 7.3 %expert.5 = (f32[80,1152]{1,0:T(8,128)}, f32[80,1152]{1,0:T(8,128)}, bf16[160,1152]{1,0:T(8,128)(2,1)}) custom-call(bf16[8,288,2304]{2,1,0:T(8,128)(2,1)} %own_ref.7, f32[8,1,640]{2,1,0:T(1,128)} %broadcast_in_dim.3.b_ref, bf16[8,576,1152]{2,1,0:T(8,128)(2,1)} %out_w_ref.7, bf16[160,1152]{1,0:T(8,128)(2,1)} %get-tuple-element.84.refs_0_, ...), custom_call_target="tpu_custom_call" | custom-call | flops 1698693120 | bytes 24772608 | tf_op jit(solution)/shard_map/expert/pallas_call | solution.py:470
  95.4 6.0 %collective-permute-done.23.refs_10_ = bf16[144,1152]{1,0:T(8,128)(2,1)S(1)} collective-permute-done((bf16[144,1152]{1,0:T(8,128)(2,1)S(1)}, bf16[144,1152]{1,0:T(8,128)(2,1)S(1)}, u32[]{:S(2)}, u32[]{:S(2)}) %collective-permute-start.23) | collective-permute-done | bytes 331808 | tf_op jit(solution)/shard_map/ppermute | solution.py:152
  106.5 7.3 %expert.7 = (f32[80,1152]{1,0:T(8,128)}, f32[80,1152]{1,0:T(8,128)}, bf16[160,1152]{1,0:T(8,128)(2,1)}) custom-call(bf16[8,288,2304]{2,1,0:T(8,128)(2,1)} %own_ref.7, f32[8,1,640]{2,1,0:T(1,128)} %broadcast_in_dim.3.b_ref, bf16[8,576,1152]{2,1,0:T(8,128)(2,1)} %out_w_ref.7, bf16[160,1152]{1,0:T(8,128)(2,1)} %get-tuple-element.84.refs_0_, ...), custom_call_target="tpu_custom_call" | custom-call | flops 1698693120 | bytes 24772608 | tf_op jit(solution)/shard_map/expert/pallas_call | solution.py:470
  118.1 7.1 %expert.6 = (f32[80,1152]{1,0:T(8,128)}, f32[80,1152]{1,0:T(8,128)}, bf16[160,1152]{1,0:T(8,128)(2,1)}) custom-call(bf16[8,288,2304]{2,1,0:T(8,128)(2,1)} %own_ref.7, f32[8,1,640]{2,1,0:T(1,128)} %broadcast_in_dim.3.b_ref, bf16[8,576,1152]{2,1,0:T(8,128)(2,1)} %out_w_ref.7, bf16[160,1152]{1,0:T(8,128)(2,1)} %get-tuple-element.84.refs_0_, ...), custom_call_target="tpu_custom_call" | custom-call | flops 1698693120 | bytes 24772608 | tf_op jit(solution)/shard_map/expert/pallas_call | solution.py:470
  128.8 3.3 %collective-permute-start.29 = (bf16[40,1152]{1,0:T(8,128)(2,1)S(1)}, bf16[40,1152]{1,0:T(8,128)(2,1)S(1)}, u32[]{:S(2)}, u32[]{:S(2)}) collective-permute-start(bf16[40,1152]{1,0:T(8,128)(2,1)S(1)} %pad_maximum_fusion.3), channel_id=1, source_target_pairs={{0,12},{4,8},{8,4},{12,0},{1,13},{5,9},{9,5},{13,1},{2,14},{6,10},... | collective-permute-start | bytes 276488 | tf_op jit(solution)/shard_map/ppermute | solution.py:152
  134.0 3.9 %collective-permute-done.28.refs_2_ = bf16[40,1152]{1,0:T(8,128)(2,1)S(1)} collective-permute-done((bf16[40,1152]{1,0:T(8,128)(2,1)S(1)}, bf16[40,1152]{1,0:T(8,128)(2,1)S(1)}, u32[]{:S(2)}, u32[]{:S(2)}) %collective-permute-start.28) | collective-permute-done | bytes 92192 | tf_op jit(solution)/shard_map/ppermute | solution.py:152
  139.1 2.4 %combine.2.refs_0_ = f32[128,1152]{1,0:T(8,128)} custom-call(f32[128,128]{1,0:T(8,128)} %route.1.refs_13_.route_ref, bf16[40,1152]{1,0:T(8,128)(2,1)} %pad_maximum_fusion.refs_0_, bf16[40,1152]{1,0:T(8,128)(2,1)} %copy-done.32, bf16[40,1152]{1,0:T(8,128)(2,1)} %copy-done.33, bf16[40,1152]{1,0:T(8,128)(2,1)} %copy-done.34), custom_call_target="tpu_custom_call" | custom-call | tf_op jit(solution)/shard_map/combine/pallas_call | solution.py:541
  147.9 4.6 %collective-permute-done.35.refs_5_ = bf16[40,1152]{1,0:T(8,128)(2,1)S(1)} collective-permute-done((bf16[40,1152]{1,0:T(8,128)(2,1)S(1)}, bf16[40,1152]{1,0:T(8,128)(2,1)S(1)}, u32[]{:S(2)}, u32[]{:S(2)}) %collective-permute-start.35) | collective-permute-done | bytes 92192 | tf_op jit(solution)/shard_map/ppermute | solution.py:152
  153.7 2.5 %combine.3 = bf16[1,128,1152]{2,1,0:T(8,128)(2,1)} custom-call(f32[128,128]{1,0:T(8,128)} %route.1.refs_13_.route_ref, f32[128,1152]{1,0:T(8,128)} %combine.2.refs_0_, bf16[1,128,1152]{2,1,0:T(8,128)(2,1)} %refs_1_.1, f32[3,1152]{1,0:T(4,128)} %bitcast.8, bf16[40,1152]{1,0:T(8,128)(2,1)} %pad_maximum_fusion.4.refs_3_, bf16[40,1152]{1,0:T(8,128)(2,1)} %copy-done.29, ...), custom_call_target="tpu_custom_call" | custom-call | tf_op jit(solution)/shard_map/combine/pallas_call | solution.py:541
  (163 shorter events, 49.3 us)
Async XLA Ops:
  0.0 16.8 %collective-permute-start.1 = (bf16[8,288,2304]{2,1,0:T(8,128)(2,1)}, bf16[8,288,2304]{2,1,0:T(8,128)(2,1)}, u32[]{:S(2)}, u32[]{:S(2)}) collective-permute-start(bf16[8,288,2304]{2,1,0:T(8,128)(2,1)} %own_ref.7), channel_id=1, source_target_pairs={{0,1},{1,0},{2,3},{3,2},{4,5},{5,4},{6,7},{7,6},{8,9},{9,8},{10,11... | collective-permute-start | bytes 31850504 | tf_op jit(solution)/shard_map/ppermute | solution.py:152
  5.0 11.4 %collective-permute-start = (bf16[144,1152]{1,0:T(8,128)(2,1)}, bf16[144,1152]{1,0:T(8,128)(2,1)S(1)}, u32[]{:S(2)}, u32[]{:S(2)}) collective-permute-start(bf16[144,1152]{1,0:T(8,128)(2,1)} %prepare.1.block_ref.refs_0_), channel_id=1, source_target_pairs={{0,2},{1,3},{2,0},{3,1},{4,6},{5,7},{6,4},{7,5},{8,10},{9,11},{10,... | collective-permute-start | bytes 995336 | tf_op jit(solution)/shard_map/ppermute | solution.py:152
  10.5 15.9 %collective-permute-start.4 = (bf16[144,1152]{1,0:T(8,128)(2,1)}, bf16[144,1152]{1,0:T(8,128)(2,1)S(1)}, u32[]{:S(2)}, u32[]{:S(2)}) collective-permute-start(bf16[144,1152]{1,0:T(8,128)(2,1)} %get-tuple-element.66), channel_id=1, source_target_pairs={{0,2},{1,3},{2,0},{3,1},{4,6},{5,7},{6,4},{7,5},{8,10},{9,11},{10,... | collective-permute-start | bytes 995336 | tf_op jit(solution)/shard_map/ppermute | solution.py:152
  10.6 19.6 %collective-permute-start.5 = (bf16[144,1152]{1,0:T(8,128)(2,1)}, bf16[144,1152]{1,0:T(8,128)(2,1)S(1)}, u32[]{:S(2)}, u32[]{:S(2)}) collective-permute-start(bf16[144,1152]{1,0:T(8,128)(2,1)} %get-tuple-element.67), channel_id=1, source_target_pairs={{0,3},{1,2},{2,1},{3,0},{4,7},{5,6},{6,5},{7,4},{8,11},{9,10},{10,... | collective-permute-start | bytes 995336 | tf_op jit(solution)/shard_map/ppermute | solution.py:152
  16.8 31.0 %collective-permute-start.6 = (bf16[288,1152]{1,0:T(8,128)(2,1)}, bf16[288,1152]{1,0:T(8,128)(2,1)S(1)}, u32[]{:S(2)}, u32[]{:S(2)}) collective-permute-start(bf16[288,1152]{1,0:T(8,128)(2,1)} %get-tuple-element.71), channel_id=1, source_target_pairs={{0,2},{1,3},{2,0},{3,1},{4,6},{5,7},{6,4},{7,5},{8,10},{9,11},{10,... | collective-permute-start | bytes 1990664 | tf_op jit(solution)/shard_map/ppermute | solution.py:152
  22.2 25.6 %collective-permute-start.2 = (bf16[160,1152]{1,0:T(8,128)(2,1)}, bf16[160,1152]{1,0:T(8,128)(2,1)S(1)}, u32[]{:S(2)}, u32[]{:S(2)}) collective-permute-start(bf16[160,1152]{1,0:T(8,128)(2,1)} %get-tuple-element.62), channel_id=1, source_target_pairs={{0,4},{4,0},{8,12},{12,8},{1,5},{5,1},{9,13},{13,9},{2,6},{6,2},{1... | collective-permute-start | bytes 1105928 | tf_op jit(solution)/shard_map/ppermute | solution.py:152
  23.8 24.0 %collective-permute-start.3 = (bf16[160,1152]{1,0:T(8,128)(2,1)}, bf16[160,1152]{1,0:T(8,128)(2,1)S(1)}, u32[]{:S(2)}, u32[]{:S(2)}) collective-permute-start(bf16[160,1152]{1,0:T(8,128)(2,1)} %get-tuple-element.63), channel_id=1, source_target_pairs={{0,8},{4,12},{8,0},{12,4},{1,9},{5,13},{9,1},{13,5},{2,10},{6,14},... | collective-permute-start | bytes 1105928 | tf_op jit(solution)/shard_map/ppermute | solution.py:152
  30.2 10.8 %collective-permute-start.7 = (bf16[144,1152]{1,0:T(8,128)(2,1)S(1)}, bf16[144,1152]{1,0:T(8,128)(2,1)}, u32[]{:S(2)}, u32[]{:S(2)}) collective-permute-start(bf16[144,1152]{1,0:T(8,128)(2,1)S(1)} %collective-permute-done.4.refs_9_), channel_id=1, source_target_pairs={{0,16},{16,0},{1,17},{17,1},{2,18},{18,2},{3,19},{19,3},{4,20},{20... | collective-permute-start | bytes 995336 | tf_op jit(solution)/shard_map/ppermute | solution.py:152
  31.7 16.1 %collective-permute-start.8 = (bf16[144,1152]{1,0:T(8,128)(2,1)S(1)}, bf16[144,1152]{1,0:T(8,128)(2,1)S(1)}, u32[]{:S(2)}, u32[]{:S(2)}) collective-permute-start(bf16[144,1152]{1,0:T(8,128)(2,1)S(1)} %collective-permute-done.5.refs_10_), channel_id=1, source_target_pairs={{0,16},{16,0},{1,17},{17,1},{2,18},{18,2},{3,19},{19,3},{4,20},{20... | collective-permute-start | bytes 995336 | tf_op jit(solution)/shard_map/ppermute | solution.py:152
  41.0 17.7 %collective-permute-start.10 = (bf16[288,1152]{1,0:T(8,128)(2,1)}, bf16[288,1152]{1,0:T(8,128)(2,1)S(1)}, u32[]{:S(2)}, u32[]{:S(2)}) collective-permute-start(bf16[288,1152]{1,0:T(8,128)(2,1)} %get-tuple-element.77), channel_id=1, source_target_pairs={{0,3},{1,2},{2,1},{3,0},{4,7},{5,6},{6,5},{7,4},{8,11},{9,10},{10,... | collective-permute-start | bytes 1990664 | tf_op jit(solution)/shard_map/ppermute | solution.py:152
  48.5 20.6 %collective-permute-start.9 = (bf16[160,1152]{1,0:T(8,128)(2,1)}, bf16[160,1152]{1,0:T(8,128)(2,1)S(1)}, u32[]{:S(2)}, u32[]{:S(2)}) collective-permute-start(bf16[160,1152]{1,0:T(8,128)(2,1)} %get-tuple-element.75), channel_id=1, source_target_pairs={{0,12},{4,8},{8,4},{12,0},{1,13},{5,9},{9,5},{13,1},{2,14},{6,10},... | collective-permute-start | bytes 1105928 | tf_op jit(solution)/shard_map/ppermute | solution.py:152
  52.4 10.7 %collective-permute-start.11 = (bf16[144,1152]{1,0:T(8,128)(2,1)S(1)}, bf16[144,1152]{1,0:T(8,128)(2,1)S(1)}, u32[]{:S(2)}, u32[]{:S(2)}) collective-permute-start(bf16[144,1152]{1,0:T(8,128)(2,1)S(1)} %get-tuple-element.78), channel_id=1, source_target_pairs={{0,16},{16,0},{1,17},{17,1},{2,18},{18,2},{3,19},{19,3},{4,20},{20... | collective-permute-start | bytes 995336 | tf_op jit(solution)/shard_map/ppermute | solution.py:152
  53.9 15.2 %collective-permute-start.12 = (bf16[144,1152]{1,0:T(8,128)(2,1)S(1)}, bf16[144,1152]{1,0:T(8,128)(2,1)S(1)}, u32[]{:S(2)}, u32[]{:S(2)}) collective-permute-start(bf16[144,1152]{1,0:T(8,128)(2,1)S(1)} %get-tuple-element.79), channel_id=1, source_target_pairs={{0,16},{16,0},{1,17},{17,1},{2,18},{18,2},{3,19},{19,3},{4,20},{20... | collective-permute-start | bytes 995336 | tf_op jit(solution)/shard_map/ppermute | solution.py:152
  54.5 14.6 %collective-permute-start.13 = (bf16[144,1152]{1,0:T(8,128)(2,1)}, bf16[144,1152]{1,0:T(8,128)(2,1)S(1)}, u32[]{:S(2)}, u32[]{:S(2)}) collective-permute-start(bf16[144,1152]{1,0:T(8,128)(2,1)} %get-tuple-element.82), channel_id=1, source_target_pairs={{0,2},{1,3},{2,0},{3,1},{4,6},{5,7},{6,4},{7,5},{8,10},{9,11},{10,... | collective-permute-start | bytes 995336 | tf_op jit(solution)/shard_map/ppermute | solution.py:152
  71.3 13.1 %collective-permute-start.20 = (bf16[144,1152]{1,0:T(8,128)(2,1)}, bf16[144,1152]{1,0:T(8,128)(2,1)}, u32[]{:S(2)}, u32[]{:S(2)}) collective-permute-start(bf16[144,1152]{1,0:T(8,128)(2,1)} %get-tuple-element.91), channel_id=1, source_target_pairs={{0,16},{16,0},{1,17},{17,1},{2,18},{18,2},{3,19},{19,3},{4,20},{20... | collective-permute-start | bytes 995336 | tf_op jit(solution)/shard_map/ppermute | solution.py:152
  91.7 10.6 %collective-permute-start.21 = (bf16[160,1152]{1,0:T(8,128)(2,1)}, bf16[160,1152]{1,0:T(8,128)(2,1)S(1)}, u32[]{:S(2)}, u32[]{:S(2)}) collective-permute-start(bf16[160,1152]{1,0:T(8,128)(2,1)} %get-tuple-element.93), channel_id=1, source_target_pairs={{0,1},{1,0},{2,3},{3,2},{4,5},{5,4},{6,7},{7,6},{8,9},{9,8},{10,11... | collective-permute-start | bytes 1105928 | tf_op jit(solution)/shard_map/ppermute | solution.py:152
  91.8 9.6 %collective-permute-start.23 = (bf16[144,1152]{1,0:T(8,128)(2,1)S(1)}, bf16[144,1152]{1,0:T(8,128)(2,1)S(1)}, u32[]{:S(2)}, u32[]{:S(2)}) collective-permute-start(bf16[144,1152]{1,0:T(8,128)(2,1)S(1)} %copy-done.37), channel_id=1, source_target_pairs={{0,3},{1,2},{2,1},{3,0},{4,7},{5,6},{6,5},{7,4},{8,11},{9,10},{10,... | collective-permute-start | bytes 995336 | tf_op jit(solution)/shard_map/ppermute | solution.py:152
  93.4 12.3 %collective-permute-start.30 = (bf16[144,1152]{1,0:T(8,128)(2,1)S(1)}, bf16[144,1152]{1,0:T(8,128)(2,1)S(1)}, u32[]{:S(2)}, u32[]{:S(2)}) collective-permute-start(bf16[144,1152]{1,0:T(8,128)(2,1)S(1)} %copy-done.20), channel_id=1, source_target_pairs={{0,16},{16,0},{1,17},{17,1},{2,18},{18,2},{3,19},{19,3},{4,20},{20... | collective-permute-start | bytes 995336 | tf_op jit(solution)/shard_map/ppermute | solution.py:152
  93.9 22.3 %collective-permute-start.24 = (bf16[144,1152]{1,0:T(8,128)(2,1)S(1)}, bf16[144,1152]{1,0:T(8,128)(2,1)S(1)}, u32[]{:S(2)}, u32[]{:S(2)}) collective-permute-start(bf16[144,1152]{1,0:T(8,128)(2,1)S(1)} %copy-done.22), channel_id=1, source_target_pairs={{0,16},{16,0},{1,17},{17,1},{2,18},{18,2},{3,19},{19,3},{4,20},{20... | collective-permute-start | bytes 995336 | tf_op jit(solution)/shard_map/ppermute | solution.py:152
  101.4 16.0 %collective-permute-start.25 = (bf16[144,1152]{1,0:T(8,128)(2,1)S(1)}, bf16[144,1152]{1,0:T(8,128)(2,1)S(1)}, u32[]{:S(2)}, u32[]{:S(2)}) collective-permute-start(bf16[144,1152]{1,0:T(8,128)(2,1)S(1)} %collective-permute-done.23.refs_10_), channel_id=1, source_target_pairs={{0,16},{16,0},{1,17},{17,1},{2,18},{18,2},{3,19},{19,3},{4,20},{20... | collective-permute-start | bytes 995336 | tf_op jit(solution)/shard_map/ppermute | solution.py:152
  103.5 10.5 %collective-permute-start.22 = (bf16[80,1152]{1,0:T(8,128)(2,1)S(1)}, bf16[80,1152]{1,0:T(8,128)(2,1)S(1)}, u32[]{:S(2)}, u32[]{:S(2)}) collective-permute-start(bf16[80,1152]{1,0:T(8,128)(2,1)S(1)} %add_convert_fusion.5), channel_id=1, source_target_pairs={{0,2},{1,3},{2,0},{3,1},{4,6},{5,7},{6,4},{7,5},{8,10},{9,11},{10,... | collective-permute-start | bytes 552968 | tf_op jit(solution)/shard_map/ppermute | solution.py:152
  105.1 10.0 %collective-permute-start.19 = (bf16[80,1152]{1,0:T(8,128)(2,1)S(1)}, bf16[80,1152]{1,0:T(8,128)(2,1)S(1)}, u32[]{:S(2)}, u32[]{:S(2)}) collective-permute-start(bf16[80,1152]{1,0:T(8,128)(2,1)S(1)} %add_convert_fusion.7), channel_id=1, source_target_pairs={{0,2},{1,3},{2,0},{3,1},{4,6},{5,7},{6,4},{7,5},{8,10},{9,11},{10,... | collective-permute-start | bytes 552968 | tf_op jit(solution)/shard_map/ppermute | solution.py:152
  113.9 12.3 %collective-permute-start.31 = (bf16[160,1152]{1,0:T(8,128)(2,1)}, bf16[160,1152]{1,0:T(8,128)(2,1)S(1)}, u32[]{:S(2)}, u32[]{:S(2)}) collective-permute-start(bf16[160,1152]{1,0:T(8,128)(2,1)} %get-tuple-element.104), channel_id=1, source_target_pairs={{0,1},{1,0},{2,3},{3,2},{4,5},{5,4},{6,7},{7,6},{8,9},{9,8},{10,11... | collective-permute-start | bytes 1105928 | tf_op jit(solution)/shard_map/ppermute | solution.py:152
  127.7 10.2 %collective-permute-start.28 = (bf16[40,1152]{1,0:T(8,128)(2,1)S(1)}, bf16[40,1152]{1,0:T(8,128)(2,1)S(1)}, u32[]{:S(2)}, u32[]{:S(2)}) collective-permute-start(bf16[40,1152]{1,0:T(8,128)(2,1)S(1)} %get-tuple-element.100), channel_id=1, source_target_pairs={{0,8},{4,12},{8,0},{12,4},{1,9},{5,13},{9,1},{13,5},{2,10},{6,14},... | collective-permute-start | bytes 276488 | tf_op jit(solution)/shard_map/ppermute | solution.py:152
  (52 other events, 544.6 us)

commit v4 on v3

--- a/solution.py
+++ b/solution.py
@@ -600,6 +600,7 @@
     opposite, near = lax.optimization_barrier((opposite, near))
     sending = dispatch_call(jnp.asarray(wanted), [block, opposite], members)
     arrived = [sending[0], crossed(sending[1], "ep", 1), crossed(sending[2], "ep", 2)]
+    route = route_call(block, router_weight)
     far.append(fetch(2, opposite))
     gate = after(gate, far[0], far[1], near)
 
@@ -609,7 +610,7 @@
 
     far.append(fetch(4, gate))
     other.append(exchange(2, gate))
-    arrived.append(crossed(after(sending[3], gate), "ep", 3))
+    arrived.append(crossed(after(sending[3], gate, route, own_b), "ep", 3))
     gate = after(gate, far[3], *other[2])
 
     far.append(fetch(5, gate))
@@ -618,8 +619,7 @@
 
     other.append(exchange(4, gate))
     across = [over(held, gate) for held in arrived]
-    route = route_call(block, router_weight)
-    outs.append(run(0, route))
+    outs.append(run(0))
     gate = after(gate, far[5], *other[3])
     other.append(exchange(5, gate))
     half_rows = members * CAP
@@ -629,7 +629,7 @@
         return crossed(held.astype(jnp.bfloat16), "fs", 2)
 
     sent = [over(outs[0][2])]
-    outs.append(run(1, outs[0][0]))
+    outs.append(run(1, outs[0][0], far[5], other[3][1]))
     sent.append(over(outs[1][2]))
     given = [give(0), give(1)]
     outs.append(run(2, *sent))

time: 157 us -> 152 us (0.968)
  waiting for transfers between devices: 51.6 us -> 47.8 us
    ppermute x37, waiting for transfers between devices: 51.6 us -> 47.8 us  [crossed(): return lax.ppermute(block, axis, [(i, i ^ mask) for i in range(count)])]
    unnamed x80 -> x82, local copies, waits for them, and re-layouts: 8.09 us -> 7.75 us
  transfers between devices with their start and end apart: 37 -> 37, of which waited for: 12 -> 12; matrix products, arithmetic and copies ran while one was open for 7% -> 7% of each run, Pallas kernels for 21% -> 22%
where the time goes in v4:
time: 152 us
  waiting for transfers between devices  47.8 us (31%)
  Pallas kernels  43.3 us (28%)
  starting transfers between devices  43.2 us (28%)
  local copies, waits for them, and re-layouts  8.61 us (6%)
  other arithmetic  8.24 us (5%)
    ppermute x37, waiting for transfers between devices, crossed(): return lax.ppermute(block, axis, [(i, i ^ mask) for i in range(count)])  47.8 us
    ppermute x37, starting transfers between devices, crossed(): return lax.ppermute(block, axis, [(i, i ^ mask) for i in range(count)])  43.2 us
    pallas_call x4, Pallas kernels, expert_call(): pl.pallas_call(functools.partial(expert_kernel, expert, len(xs), [offset...  28.7 us
    unnamed x82, local copies, waits for them, and re-layouts  7.75 us
    pallas_call x2, Pallas kernels, combine_call(): pl.pallas_call(functools.partial(combine_kernel, experts, group, bool(fin...  4.85 us
    convert_element_type x4, other arithmetic, recut_weights(): wholes.append((half + given[e].astype(jnp.float32)).astype(jnp.bfloat16))  3.24 us
    pallas_call x1, Pallas kernels, cut_call(): pl.pallas_call(functools.partial(cut_kernel, groups), in_specs=[anywhere]...  3.05 us
  transfers between devices with their start and end apart: 37, of which 12 were waited for; matrix products, arithmetic and copies ran while one was open for 7% of the time, Pallas kernels for 22%

profile of v4, /device:TPU:0, one launch (start us, length us, event | category | flops | bytes accessed | tf_op | source)
XLA Modules:
  0.0 151.7 jit_solution(9717266939544643340)
XLA Ops:
  5.0 2.5 %collective-permute-start = (bf16[144,1152]{1,0:T(8,128)(2,1)}, bf16[144,1152]{1,0:T(8,128)(2,1)S(1)}, u32[]{:S(2)}, u32[]{:S(2)}) collective-permute-start(bf16[144,1152]{1,0:T(8,128)(2,1)} %prepare.1.block_ref.refs_0_), channel_id=1, source_target_pairs={{0,2},{1,3},{2,0},{3,1},{4,6},{5,7},{6,4},{7,5},{8,10},{9,11},{10,... | collective-permute-start | bytes 995336 | tf_op jit(solution)/shard_map/ppermute | solution.py:152
  7.5 3.1 %cut.1 = (bf16[144,1152]{1,0:T(8,128)(2,1)}, bf16[144,1152]{1,0:T(8,128)(2,1)}, bf16[288,1152]{1,0:T(8,128)(2,1)}, bf16[288,1152]{1,0:T(8,128)(2,1)}, bf16[144,1...) custom-call(bf16[8,288,2304]{2,1,0:T(8,128)(2,1)} %own_ref.7), custom_call_target="tpu_custom_call" | custom-call | bytes 5308416 | tf_op jit(solution)/shard_map/cut/pallas_call | solution.py:334
  12.2 4.2 %collective-permute-done.refs_1_ = bf16[144,1152]{1,0:T(8,128)(2,1)S(1)} collective-permute-done((bf16[144,1152]{1,0:T(8,128)(2,1)}, bf16[144,1152]{1,0:T(8,128)(2,1)S(1)}, u32[]{:S(2)}, u32[]{:S(2)}) %collective-permute-start) | collective-permute-done | bytes 331808 | tf_op jit(solution)/shard_map/ppermute | solution.py:152
  16.8 2.9 %collective-permute-start.6 = (bf16[288,1152]{1,0:T(8,128)(2,1)}, bf16[288,1152]{1,0:T(8,128)(2,1)S(1)}, u32[]{:S(2)}, u32[]{:S(2)}) collective-permute-start(bf16[288,1152]{1,0:T(8,128)(2,1)} %get-tuple-element.71), channel_id=1, source_target_pairs={{0,2},{1,3},{2,0},{3,1},{4,6},{5,7},{6,4},{7,5},{8,10},{9,11},{10,... | collective-permute-start | bytes 1990664 | tf_op jit(solution)/shard_map/ppermute | solution.py:152
  19.6 2.6 %dispatch.1 = (bf16[160,1152]{1,0:T(8,128)(2,1)}, bf16[160,1152]{1,0:T(8,128)(2,1)}, bf16[160,1152]{1,0:T(8,128)(2,1)}, bf16[160,1152]{1,0:T(8,128)(2,1)}) custom-call(f32[160,2]{1,0:T(8,128)} %constant.16.clone.wanted_ref, bf16[144,1152]{1,0:T(8,128)(2,1)} %prepare.1.block_ref.refs_0_, bf16[144,1152]{1,0:T(8,128)(2,1)} %copy-done.39), custom_call_target="tpu_custom_call" | custom-call | flops 424673280 | bytes 2949120 | tf_op jit(solution)/shard_map/dispatch/pallas_call | solution.py:251
  23.8 2.6 %collective-permute-start.3 = (bf16[160,1152]{1,0:T(8,128)(2,1)}, bf16[160,1152]{1,0:T(8,128)(2,1)S(1)}, u32[]{:S(2)}, u32[]{:S(2)}) collective-permute-start(bf16[160,1152]{1,0:T(8,128)(2,1)} %get-tuple-element.63), channel_id=1, source_target_pairs={{0,8},{4,12},{8,0},{12,4},{1,9},{5,13},{9,1},{13,5},{2,10},{6,14},... | collective-permute-start | bytes 1105928 | tf_op jit(solution)/shard_map/ppermute | solution.py:152
  26.4 3.8 %collective-permute-done.5.refs_10_ = bf16[144,1152]{1,0:T(8,128)(2,1)S(1)} collective-permute-done((bf16[144,1152]{1,0:T(8,128)(2,1)}, bf16[144,1152]{1,0:T(8,128)(2,1)S(1)}, u32[]{:S(2)}, u32[]{:S(2)}) %collective-permute-start.5) | collective-permute-done | bytes 331808 | tf_op jit(solution)/shard_map/ppermute | solution.py:152
  33.1 2.1 %route.1.route_ref = f32[128,128]{1,0:T(8,128)} custom-call(bf16[144,1152]{1,0:T(8,128)(2,1)} %prepare.1.block_ref.refs_0_, bf16[1152,16]{1,0:T(8,128)(2,1)} %copy.9.router_ref), custom_call_target="tpu_custom_call" | custom-call | tf_op jit(solution)/shard_map/route/pallas_call | solution.py:218
  35.8 5.1 %collective-permute-done.7.refs_11_ = bf16[144,1152]{1,0:T(8,128)(2,1)S(1)} collective-permute-done((bf16[144,1152]{1,0:T(8,128)(2,1)S(1)}, bf16[144,1152]{1,0:T(8,128)(2,1)S(1)}, u32[]{:S(2)}, u32[]{:S(2)}) %collective-permute-start.7) | collective-permute-done | bytes 331808 | tf_op jit(solution)/shard_map/ppermute | solution.py:152
  42.1 5.7 %collective-permute-done.8.refs_12_ = bf16[144,1152]{1,0:T(8,128)(2,1)S(1)} collective-permute-done((bf16[144,1152]{1,0:T(8,128)(2,1)S(1)}, bf16[144,1152]{1,0:T(8,128)(2,1)S(1)}, u32[]{:S(2)}, u32[]{:S(2)}) %collective-permute-start.8) | collective-permute-done | bytes 331808 | tf_op jit(solution)/shard_map/ppermute | solution.py:152
  47.8 3.9 %collective-permute-start.9 = (bf16[160,1152]{1,0:T(8,128)(2,1)}, bf16[160,1152]{1,0:T(8,128)(2,1)S(1)}, u32[]{:S(2)}, u32[]{:S(2)}) collective-permute-start(bf16[160,1152]{1,0:T(8,128)(2,1)} %get-tuple-element.75), channel_id=1, source_target_pairs={{0,12},{4,8},{8,4},{12,0},{1,13},{5,9},{9,5},{13,1},{2,14},{6,10},... | collective-permute-start | bytes 1105928 | tf_op jit(solution)/shard_map/ppermute | solution.py:152
  55.3 3.3 %collective-permute-done.10.refs_10_ = bf16[288,1152]{1,0:T(8,128)(2,1)S(1)} collective-permute-done((bf16[288,1152]{1,0:T(8,128)(2,1)}, bf16[288,1152]{1,0:T(8,128)(2,1)S(1)}, u32[]{:S(2)}, u32[]{:S(2)}) %collective-permute-start.10) | collective-permute-done | bytes 663584 | tf_op jit(solution)/shard_map/ppermute | solution.py:152
  58.6 3.8 %collective-permute-done.11.refs_11_ = bf16[144,1152]{1,0:T(8,128)(2,1)S(1)} collective-permute-done((bf16[144,1152]{1,0:T(8,128)(2,1)S(1)}, bf16[144,1152]{1,0:T(8,128)(2,1)S(1)}, u32[]{:S(2)}, u32[]{:S(2)}) %collective-permute-start.11) | collective-permute-done | bytes 331808 | tf_op jit(solution)/shard_map/ppermute | solution.py:152
  62.5 6.0 %collective-permute-done.12.refs_11_ = bf16[144,1152]{1,0:T(8,128)(2,1)S(1)} collective-permute-done((bf16[144,1152]{1,0:T(8,128)(2,1)S(1)}, bf16[144,1152]{1,0:T(8,128)(2,1)S(1)}, u32[]{:S(2)}, u32[]{:S(2)}) %collective-permute-start.12) | collective-permute-done | bytes 331808 | tf_op jit(solution)/shard_map/ppermute | solution.py:152
  74.7 7.1 %expert.4 = (f32[80,1152]{1,0:T(8,128)}, f32[80,1152]{1,0:T(8,128)}, bf16[160,1152]{1,0:T(8,128)(2,1)}) custom-call(bf16[8,288,2304]{2,1,0:T(8,128)(2,1)} %own_ref.7, f32[8,1,640]{2,1,0:T(1,128)} %broadcast_in_dim.3.b_ref, bf16[8,576,1152]{2,1,0:T(8,128)(2,1)} %out_w_ref.7, bf16[160,1152]{1,0:T(8,128)(2,1)} %get-tuple-element.84.refs_0_, ...), custom_call_target="tpu_custom_call" | custom-call | flops 1698693120 | bytes 24772608 | tf_op jit(solution)/shard_map/expert/pallas_call | solution.py:470
  81.9 4.7 %collective-permute-done.22.refs_15_.refs_12_ = bf16[144,1152]{1,0:T(8,128)(2,1)S(1)} collective-permute-done((bf16[144,1152]{1,0:T(8,128)(2,1)S(1)}, bf16[144,1152]{1,0:T(8,128)(2,1)S(1)}, u32[]{:S(2)}, u32[]{:S(2)}) %collective-permute-start.22) | collective-permute-done | bytes 331808 | tf_op jit(solution)/shard_map/ppermute | solution.py:152
  87.3 7.2 %expert.5 = (f32[80,1152]{1,0:T(8,128)}, f32[80,1152]{1,0:T(8,128)}, bf16[160,1152]{1,0:T(8,128)(2,1)}) custom-call(bf16[8,288,2304]{2,1,0:T(8,128)(2,1)} %own_ref.7, f32[8,1,640]{2,1,0:T(1,128)} %broadcast_in_dim.3.b_ref, bf16[8,576,1152]{2,1,0:T(8,128)(2,1)} %out_w_ref.7, bf16[160,1152]{1,0:T(8,128)(2,1)} %get-tuple-element.84.refs_0_, ...), custom_call_target="tpu_custom_call" | custom-call | flops 1698693120 | bytes 24772608 | tf_op jit(solution)/shard_map/expert/pallas_call | solution.py:470
  100.2 7.3 %expert.7 = (f32[80,1152]{1,0:T(8,128)}, f32[80,1152]{1,0:T(8,128)}, bf16[160,1152]{1,0:T(8,128)(2,1)}) custom-call(bf16[8,288,2304]{2,1,0:T(8,128)(2,1)} %own_ref.7, f32[8,1,640]{2,1,0:T(1,128)} %broadcast_in_dim.3.b_ref, bf16[8,576,1152]{2,1,0:T(8,128)(2,1)} %out_w_ref.7, bf16[160,1152]{1,0:T(8,128)(2,1)} %get-tuple-element.84.refs_0_, ...), custom_call_target="tpu_custom_call" | custom-call | flops 1698693120 | bytes 24772608 | tf_op jit(solution)/shard_map/expert/pallas_call | solution.py:470
  112.7 7.1 %expert.6 = (f32[80,1152]{1,0:T(8,128)}, f32[80,1152]{1,0:T(8,128)}, bf16[160,1152]{1,0:T(8,128)(2,1)}) custom-call(bf16[8,288,2304]{2,1,0:T(8,128)(2,1)} %own_ref.7, f32[8,1,640]{2,1,0:T(1,128)} %broadcast_in_dim.3.b_ref, bf16[8,576,1152]{2,1,0:T(8,128)(2,1)} %out_w_ref.7, bf16[160,1152]{1,0:T(8,128)(2,1)} %get-tuple-element.84.refs_0_, ...), custom_call_target="tpu_custom_call" | custom-call | flops 1698693120 | bytes 24772608 | tf_op jit(solution)/shard_map/expert/pallas_call | solution.py:470
  124.1 2.5 %collective-permute-start.30 = (bf16[40,1152]{1,0:T(8,128)(2,1)S(1)}, bf16[40,1152]{1,0:T(8,128)(2,1)S(1)}, u32[]{:S(2)}, u32[]{:S(2)}) collective-permute-start(bf16[40,1152]{1,0:T(8,128)(2,1)S(1)} %pad_maximum_fusion.3), channel_id=1, source_target_pairs={{0,12},{4,8},{8,4},{12,0},{1,13},{5,9},{9,5},{13,1},{2,14},{6,10},... | collective-permute-start | bytes 276488 | tf_op jit(solution)/shard_map/ppermute | solution.py:152
  128.9 3.8 %collective-permute-done.29.refs_2_ = bf16[40,1152]{1,0:T(8,128)(2,1)S(1)} collective-permute-done((bf16[40,1152]{1,0:T(8,128)(2,1)S(1)}, bf16[40,1152]{1,0:T(8,128)(2,1)S(1)}, u32[]{:S(2)}, u32[]{:S(2)}) %collective-permute-start.29) | collective-permute-done | bytes 92192 | tf_op jit(solution)/shard_map/ppermute | solution.py:152
  133.9 2.4 %combine.2.refs_0_ = f32[128,1152]{1,0:T(8,128)} custom-call(f32[128,128]{1,0:T(8,128)} %route.1.route_ref, bf16[40,1152]{1,0:T(8,128)(2,1)} %pad_maximum_fusion.refs_0_, bf16[40,1152]{1,0:T(8,128)(2,1)} %copy-done.34, bf16[40,1152]{1,0:T(8,128)(2,1)} %copy-done.35, bf16[40,1152]{1,0:T(8,128)(2,1)} %copy-done.36), custom_call_target="tpu_custom_call" | custom-call | tf_op jit(solution)/shard_map/combine/pallas_call | solution.py:541
  142.7 5.2 %collective-permute-done.35.refs_5_ = bf16[40,1152]{1,0:T(8,128)(2,1)S(1)} collective-permute-done((bf16[40,1152]{1,0:T(8,128)(2,1)S(1)}, bf16[40,1152]{1,0:T(8,128)(2,1)S(1)}, u32[]{:S(2)}, u32[]{:S(2)}) %collective-permute-start.35) | collective-permute-done | bytes 92192 | tf_op jit(solution)/shard_map/ppermute | solution.py:152
  149.2 2.5 %combine.3 = bf16[1,128,1152]{2,1,0:T(8,128)(2,1)} custom-call(f32[128,128]{1,0:T(8,128)} %route.1.route_ref, f32[128,1152]{1,0:T(8,128)} %combine.2.refs_0_, bf16[1,128,1152]{2,1,0:T(8,128)(2,1)} %refs_1_.1, f32[3,1152]{1,0:T(4,128)} %bitcast.8, bf16[40,1152]{1,0:T(8,128)(2,1)} %pad_maximum_fusion.4.refs_3_, bf16[40,1152]{1,0:T(8,128)(2,1)} %copy-done.31, ...), custom_call_target="tpu_custom_call" | custom-call | tf_op jit(solution)/shard_map/combine/pallas_call | solution.py:541
  (165 shorter events, 50.0 us)
Async XLA Ops:
  0.0 16.8 %collective-permute-start.1 = (bf16[8,288,2304]{2,1,0:T(8,128)(2,1)}, bf16[8,288,2304]{2,1,0:T(8,128)(2,1)}, u32[]{:S(2)}, u32[]{:S(2)}) collective-permute-start(bf16[8,288,2304]{2,1,0:T(8,128)(2,1)} %own_ref.7), channel_id=1, source_target_pairs={{0,1},{1,0},{2,3},{3,2},{4,5},{5,4},{6,7},{7,6},{8,9},{9,8},{10,11... | collective-permute-start | bytes 31850504 | tf_op jit(solution)/shard_map/ppermute | solution.py:152
  5.0 11.4 %collective-permute-start = (bf16[144,1152]{1,0:T(8,128)(2,1)}, bf16[144,1152]{1,0:T(8,128)(2,1)S(1)}, u32[]{:S(2)}, u32[]{:S(2)}) collective-permute-start(bf16[144,1152]{1,0:T(8,128)(2,1)} %prepare.1.block_ref.refs_0_), channel_id=1, source_target_pairs={{0,2},{1,3},{2,0},{3,1},{4,6},{5,7},{6,4},{7,5},{8,10},{9,11},{10,... | collective-permute-start | bytes 995336 | tf_op jit(solution)/shard_map/ppermute | solution.py:152
  10.6 15.8 %collective-permute-start.4 = (bf16[144,1152]{1,0:T(8,128)(2,1)}, bf16[144,1152]{1,0:T(8,128)(2,1)S(1)}, u32[]{:S(2)}, u32[]{:S(2)}) collective-permute-start(bf16[144,1152]{1,0:T(8,128)(2,1)} %get-tuple-element.66), channel_id=1, source_target_pairs={{0,2},{1,3},{2,0},{3,1},{4,6},{5,7},{6,4},{7,5},{8,10},{9,11},{10,... | collective-permute-start | bytes 995336 | tf_op jit(solution)/shard_map/ppermute | solution.py:152
  10.7 19.5 %collective-permute-start.5 = (bf16[144,1152]{1,0:T(8,128)(2,1)}, bf16[144,1152]{1,0:T(8,128)(2,1)S(1)}, u32[]{:S(2)}, u32[]{:S(2)}) collective-permute-start(bf16[144,1152]{1,0:T(8,128)(2,1)} %get-tuple-element.67), channel_id=1, source_target_pairs={{0,3},{1,2},{2,1},{3,0},{4,7},{5,6},{6,5},{7,4},{8,11},{9,10},{10,... | collective-permute-start | bytes 995336 | tf_op jit(solution)/shard_map/ppermute | solution.py:152
  16.8 31.0 %collective-permute-start.6 = (bf16[288,1152]{1,0:T(8,128)(2,1)}, bf16[288,1152]{1,0:T(8,128)(2,1)S(1)}, u32[]{:S(2)}, u32[]{:S(2)}) collective-permute-start(bf16[288,1152]{1,0:T(8,128)(2,1)} %get-tuple-element.71), channel_id=1, source_target_pairs={{0,2},{1,3},{2,0},{3,1},{4,6},{5,7},{6,4},{7,5},{8,10},{9,11},{10,... | collective-permute-start | bytes 1990664 | tf_op jit(solution)/shard_map/ppermute | solution.py:152
  22.2 25.6 %collective-permute-start.2 = (bf16[160,1152]{1,0:T(8,128)(2,1)}, bf16[160,1152]{1,0:T(8,128)(2,1)S(1)}, u32[]{:S(2)}, u32[]{:S(2)}) collective-permute-start(bf16[160,1152]{1,0:T(8,128)(2,1)} %get-tuple-element.62), channel_id=1, source_target_pairs={{0,4},{4,0},{8,12},{12,8},{1,5},{5,1},{9,13},{13,9},{2,6},{6,2},{1... | collective-permute-start | bytes 1105928 | tf_op jit(solution)/shard_map/ppermute | solution.py:152
  23.8 24.0 %collective-permute-start.3 = (bf16[160,1152]{1,0:T(8,128)(2,1)}, bf16[160,1152]{1,0:T(8,128)(2,1)S(1)}, u32[]{:S(2)}, u32[]{:S(2)}) collective-permute-start(bf16[160,1152]{1,0:T(8,128)(2,1)} %get-tuple-element.63), channel_id=1, source_target_pairs={{0,8},{4,12},{8,0},{12,4},{1,9},{5,13},{9,1},{13,5},{2,10},{6,14},... | collective-permute-start | bytes 1105928 | tf_op jit(solution)/shard_map/ppermute | solution.py:152
  30.2 10.7 %collective-permute-start.7 = (bf16[144,1152]{1,0:T(8,128)(2,1)S(1)}, bf16[144,1152]{1,0:T(8,128)(2,1)S(1)}, u32[]{:S(2)}, u32[]{:S(2)}) collective-permute-start(bf16[144,1152]{1,0:T(8,128)(2,1)S(1)} %collective-permute-done.4.refs_9_), channel_id=1, source_target_pairs={{0,16},{16,0},{1,17},{17,1},{2,18},{18,2},{3,19},{19,3},{4,20},{20... | collective-permute-start | bytes 995336 | tf_op jit(solution)/shard_map/ppermute | solution.py:152
  31.7 16.1 %collective-permute-start.8 = (bf16[144,1152]{1,0:T(8,128)(2,1)S(1)}, bf16[144,1152]{1,0:T(8,128)(2,1)S(1)}, u32[]{:S(2)}, u32[]{:S(2)}) collective-permute-start(bf16[144,1152]{1,0:T(8,128)(2,1)S(1)} %collective-permute-done.5.refs_10_), channel_id=1, source_target_pairs={{0,16},{16,0},{1,17},{17,1},{2,18},{18,2},{3,19},{19,3},{4,20},{20... | collective-permute-start | bytes 995336 | tf_op jit(solution)/shard_map/ppermute | solution.py:152
  40.9 17.8 %collective-permute-start.10 = (bf16[288,1152]{1,0:T(8,128)(2,1)}, bf16[288,1152]{1,0:T(8,128)(2,1)S(1)}, u32[]{:S(2)}, u32[]{:S(2)}) collective-permute-start(bf16[288,1152]{1,0:T(8,128)(2,1)} %get-tuple-element.77), channel_id=1, source_target_pairs={{0,3},{1,2},{2,1},{3,0},{4,7},{5,6},{6,5},{7,4},{8,11},{9,10},{10,... | collective-permute-start | bytes 1990664 | tf_op jit(solution)/shard_map/ppermute | solution.py:152
  47.8 20.7 %collective-permute-start.9 = (bf16[160,1152]{1,0:T(8,128)(2,1)}, bf16[160,1152]{1,0:T(8,128)(2,1)S(1)}, u32[]{:S(2)}, u32[]{:S(2)}) collective-permute-start(bf16[160,1152]{1,0:T(8,128)(2,1)} %get-tuple-element.75), channel_id=1, source_target_pairs={{0,12},{4,8},{8,4},{12,0},{1,13},{5,9},{9,5},{13,1},{2,14},{6,10},... | collective-permute-start | bytes 1105928 | tf_op jit(solution)/shard_map/ppermute | solution.py:152
  51.7 10.7 %collective-permute-start.11 = (bf16[144,1152]{1,0:T(8,128)(2,1)S(1)}, bf16[144,1152]{1,0:T(8,128)(2,1)S(1)}, u32[]{:S(2)}, u32[]{:S(2)}) collective-permute-start(bf16[144,1152]{1,0:T(8,128)(2,1)S(1)} %get-tuple-element.78), channel_id=1, source_target_pairs={{0,16},{16,0},{1,17},{17,1},{2,18},{18,2},{3,19},{19,3},{4,20},{20... | collective-permute-start | bytes 995336 | tf_op jit(solution)/shard_map/ppermute | solution.py:152
  53.3 15.2 %collective-permute-start.12 = (bf16[144,1152]{1,0:T(8,128)(2,1)S(1)}, bf16[144,1152]{1,0:T(8,128)(2,1)S(1)}, u32[]{:S(2)}, u32[]{:S(2)}) collective-permute-start(bf16[144,1152]{1,0:T(8,128)(2,1)S(1)} %get-tuple-element.79), channel_id=1, source_target_pairs={{0,16},{16,0},{1,17},{17,1},{2,18},{18,2},{3,19},{19,3},{4,20},{20... | collective-permute-start | bytes 995336 | tf_op jit(solution)/shard_map/ppermute | solution.py:152
  53.8 14.6 %collective-permute-start.13 = (bf16[144,1152]{1,0:T(8,128)(2,1)}, bf16[144,1152]{1,0:T(8,128)(2,1)S(1)}, u32[]{:S(2)}, u32[]{:S(2)}) collective-permute-start(bf16[144,1152]{1,0:T(8,128)(2,1)} %get-tuple-element.82), channel_id=1, source_target_pairs={{0,2},{1,3},{2,0},{3,1},{4,6},{5,7},{6,4},{7,5},{8,10},{9,11},{10,... | collective-permute-start | bytes 995336 | tf_op jit(solution)/shard_map/ppermute | solution.py:152
  69.6 12.2 %collective-permute-start.20 = (bf16[144,1152]{1,0:T(8,128)(2,1)S(1)}, bf16[144,1152]{1,0:T(8,128)(2,1)S(1)}, u32[]{:S(2)}, u32[]{:S(2)}) collective-permute-start(bf16[144,1152]{1,0:T(8,128)(2,1)S(1)} %get-tuple-element.91), channel_id=1, source_target_pairs={{0,16},{16,0},{1,17},{17,1},{2,18},{18,2},{3,19},{19,3},{4,20},{20... | collective-permute-start | bytes 995336 | tf_op jit(solution)/shard_map/ppermute | solution.py:152
  71.2 10.7 %collective-permute-start.21 = (bf16[144,1152]{1,0:T(8,128)(2,1)}, bf16[144,1152]{1,0:T(8,128)(2,1)S(1)}, u32[]{:S(2)}, u32[]{:S(2)}) collective-permute-start(bf16[144,1152]{1,0:T(8,128)(2,1)} %get-tuple-element.93), channel_id=1, source_target_pairs={{0,3},{1,2},{2,1},{3,0},{4,7},{5,6},{6,5},{7,4},{8,11},{9,10},{10,... | collective-permute-start | bytes 995336 | tf_op jit(solution)/shard_map/ppermute | solution.py:152
  72.1 14.5 %collective-permute-start.22 = (bf16[144,1152]{1,0:T(8,128)(2,1)S(1)}, bf16[144,1152]{1,0:T(8,128)(2,1)S(1)}, u32[]{:S(2)}, u32[]{:S(2)}) collective-permute-start(bf16[144,1152]{1,0:T(8,128)(2,1)S(1)} %get-tuple-element.94), channel_id=1, source_target_pairs={{0,16},{16,0},{1,17},{17,1},{2,18},{18,2},{3,19},{19,3},{4,20},{20... | collective-permute-start | bytes 995336 | tf_op jit(solution)/shard_map/ppermute | solution.py:152
  94.6 15.5 %collective-permute-start.25 = (bf16[144,1152]{1,0:T(8,128)(2,1)S(1)}, bf16[144,1152]{1,0:T(8,128)(2,1)S(1)}, u32[]{:S(2)}, u32[]{:S(2)}) collective-permute-start(bf16[144,1152]{1,0:T(8,128)(2,1)S(1)} %collective-permute-done.13.refs_9_), channel_id=1, source_target_pairs={{0,16},{16,0},{1,17},{17,1},{2,18},{18,2},{3,19},{19,3},{4,20},{20... | collective-permute-start | bytes 995336 | tf_op jit(solution)/shard_map/ppermute | solution.py:152
  96.2 15.7 %collective-permute-start.26 = (bf16[144,1152]{1,0:T(8,128)(2,1)}, bf16[144,1152]{1,0:T(8,128)(2,1)S(1)}, u32[]{:S(2)}, u32[]{:S(2)}) collective-permute-start(bf16[144,1152]{1,0:T(8,128)(2,1)} %copy-done.14), channel_id=1, source_target_pairs={{0,16},{16,0},{1,17},{17,1},{2,18},{18,2},{3,19},{19,3},{4,20},{20... | collective-permute-start | bytes 995336 | tf_op jit(solution)/shard_map/ppermute | solution.py:152
  97.9 9.9 %collective-permute-start.24 = (bf16[80,1152]{1,0:T(8,128)(2,1)S(1)}, bf16[80,1152]{1,0:T(8,128)(2,1)S(1)}, u32[]{:S(2)}, u32[]{:S(2)}) collective-permute-start(bf16[80,1152]{1,0:T(8,128)(2,1)S(1)} %add_convert_fusion.5), channel_id=1, source_target_pairs={{0,2},{1,3},{2,0},{3,1},{4,6},{5,7},{6,4},{7,5},{8,10},{9,11},{10,... | collective-permute-start | bytes 552968 | tf_op jit(solution)/shard_map/ppermute | solution.py:152
  99.5 9.4 %collective-permute-start.19 = (bf16[80,1152]{1,0:T(8,128)(2,1)S(1)}, bf16[80,1152]{1,0:T(8,128)(2,1)S(1)}, u32[]{:S(2)}, u32[]{:S(2)}) collective-permute-start(bf16[80,1152]{1,0:T(8,128)(2,1)S(1)} %add_convert_fusion.7), channel_id=1, source_target_pairs={{0,2},{1,3},{2,0},{3,1},{4,6},{5,7},{6,4},{7,5},{8,10},{9,11},{10,... | collective-permute-start | bytes 552968 | tf_op jit(solution)/shard_map/ppermute | solution.py:152
  107.5 13.1 %collective-permute-start.31 = (bf16[160,1152]{1,0:T(8,128)(2,1)}, bf16[160,1152]{1,0:T(8,128)(2,1)S(1)}, u32[]{:S(2)}, u32[]{:S(2)}) collective-permute-start(bf16[160,1152]{1,0:T(8,128)(2,1)} %get-tuple-element.104), channel_id=1, source_target_pairs={{0,1},{1,0},{2,3},{3,2},{4,5},{5,4},{6,7},{7,6},{8,9},{9,8},{10,11... | collective-permute-start | bytes 1105928 | tf_op jit(solution)/shard_map/ppermute | solution.py:152
  122.3 10.4 %collective-permute-start.29 = (bf16[40,1152]{1,0:T(8,128)(2,1)S(1)}, bf16[40,1152]{1,0:T(8,128)(2,1)S(1)}, u32[]{:S(2)}, u32[]{:S(2)}) collective-permute-start(bf16[40,1152]{1,0:T(8,128)(2,1)S(1)} %get-tuple-element.101), channel_id=1, source_target_pairs={{0,8},{4,12},{8,0},{12,4},{1,9},{5,13},{9,1},{13,5},{2,10},{6,14},... | collective-permute-start | bytes 276488 | tf_op jit(solution)/shard_map/ppermute | solution.py:152
  138.7 9.2 %collective-permute-start.35 = (bf16[40,1152]{1,0:T(8,128)(2,1)S(1)}, bf16[40,1152]{1,0:T(8,128)(2,1)S(1)}, u32[]{:S(2)}, u32[]{:S(2)}) collective-permute-start(bf16[40,1152]{1,0:T(8,128)(2,1)S(1)} %get-tuple-element.109), channel_id=1, source_target_pairs={{0,8},{4,12},{8,0},{12,4},{1,9},{5,13},{9,1},{13,5},{2,10},{6,14},... | collective-permute-start | bytes 276488 | tf_op jit(solution)/shard_map/ppermute | solution.py:152
  (53 other events, 583.4 us)

commit v5 on v4

--- a/solution.py
+++ b/solution.py
@@ -488,7 +488,7 @@
             jax.ShapeDtypeStruct((half_rows // 2, width), jnp.float32),
             jax.ShapeDtypeStruct((half_rows, width), jnp.bfloat16),
         ],
-        compiler_params=pltpu.CompilerParams(vmem_limit_bytes=54 << 20),
+        compiler_params=pltpu.CompilerParams(vmem_limit_bytes=46 << 20),
         cost_estimate=pl.CostEstimate(
             flops=2 * SPLIT * 2 * 2 * half_rows * width * columns,
             bytes_accessed=3 * (2 * SPLIT * 2 * width * columns + 16 * half_rows * width),

time: 152 us -> 150 us (0.987)
  other arithmetic: 8.24 us -> 3.14 us
  waiting for transfers between devices: 47.8 us -> 52.5 us
  local copies, waits for them, and re-layouts: 8.61 us -> 6 us
    ppermute x37, waiting for transfers between devices: 47.8 us -> 52.5 us  [crossed(): return lax.ppermute(block, axis, [(i, i ^ mask) for i in range(count)])]
    convert_element_type x4, other arithmetic: 3.24 us -> 0.28 us  [recut_weights(): wholes.append((half + given[e].astype(jnp.float32)).astype(jnp.bfloat16))]
    convert_element_type x4, other arithmetic: 2.29 us -> 0.16 us  [give(): return crossed(held.astype(jnp.bfloat16), 'fs', 2)]
    unnamed x82 -> x22, local copies, waits for them, and re-layouts: 7.75 us -> 5.75 us
  transfers between devices with their start and end apart: 37 -> 37, of which waited for: 12 -> 16; matrix products, arithmetic and copies ran while one was open for 7% -> 4% of each run, Pallas kernels for 22% -> 23%
where the time goes in v5:
time: 150 us
  waiting for transfers between devices  52.5 us (35%)
  Pallas kernels  44.1 us (29%)
  starting transfers between devices  43.7 us (29%)
  local copies, waits for them, and re-layouts  6 us (4%)
  other arithmetic  3.14 us (2%)
    ppermute x37, waiting for transfers between devices, crossed(): return lax.ppermute(block, axis, [(i, i ^ mask) for i in range(count)])  52.5 us
    ppermute x37, starting transfers between devices, crossed(): return lax.ppermute(block, axis, [(i, i ^ mask) for i in range(count)])  43.7 us
    pallas_call x4, Pallas kernels, expert_call(): pl.pallas_call(functools.partial(expert_kernel, expert, len(xs), [offset...  29.6 us
    unnamed x22, local copies, waits for them, and re-layouts  5.75 us
    pallas_call x2, Pallas kernels, combine_call(): pl.pallas_call(functools.partial(combine_kernel, experts, group, bool(fin...  4.84 us
  transfers between devices with their start and end apart: 37, of which 16 were waited for; matrix products, arithmetic and copies ran while one was open for 4% of the time, Pallas kernels for 23%

profile of v5, /device:TPU:0, one launch (start us, length us, event | category | flops | bytes accessed | tf_op | source)
XLA Modules:
  0.0 149.7 jit_solution(3211422477833852159)
XLA Ops:
  5.0 2.5 %collective-permute-start = (bf16[144,1152]{1,0:T(8,128)(2,1)}, bf16[144,1152]{1,0:T(8,128)(2,1)S(1)}, u32[]{:S(2)}, u32[]{:S(2)}) collective-permute-start(bf16[144,1152]{1,0:T(8,128)(2,1)} %prepare.1.block_ref.refs_0_), channel_id=1, source_target_pairs={{0,2},{1,3},{2,0},{3,1},{4,6},{5,7},{6,4},{7,5},{8,10},{9,11},{10,... | collective-permute-start | bytes 995336 | tf_op jit(solution)/shard_map/ppermute | solution.py:152
  7.5 2.9 %cut.1 = (bf16[144,1152]{1,0:T(8,128)(2,1)}, bf16[144,1152]{1,0:T(8,128)(2,1)}, bf16[288,1152]{1,0:T(8,128)(2,1)}, bf16[288,1152]{1,0:T(8,128)(2,1)}, bf16[144,1...) custom-call(bf16[8,288,2304]{2,1,0:T(8,128)(2,1)} %own_ref.7), custom_call_target="tpu_custom_call" | custom-call | bytes 5308416 | tf_op jit(solution)/shard_map/cut/pallas_call | solution.py:334
  12.1 4.3 %collective-permute-done.refs_1_ = bf16[144,1152]{1,0:T(8,128)(2,1)S(1)} collective-permute-done((bf16[144,1152]{1,0:T(8,128)(2,1)}, bf16[144,1152]{1,0:T(8,128)(2,1)S(1)}, u32[]{:S(2)}, u32[]{:S(2)}) %collective-permute-start) | collective-permute-done | bytes 331808 | tf_op jit(solution)/shard_map/ppermute | solution.py:152
  16.8 2.9 %collective-permute-start.6 = (bf16[288,1152]{1,0:T(8,128)(2,1)}, bf16[288,1152]{1,0:T(8,128)(2,1)S(1)}, u32[]{:S(2)}, u32[]{:S(2)}) collective-permute-start(bf16[288,1152]{1,0:T(8,128)(2,1)} %get-tuple-element.71), channel_id=1, source_target_pairs={{0,2},{1,3},{2,0},{3,1},{4,6},{5,7},{6,4},{7,5},{8,10},{9,11},{10,... | collective-permute-start | bytes 1990664 | tf_op jit(solution)/shard_map/ppermute | solution.py:152
  19.6 2.6 %dispatch.1 = (bf16[160,1152]{1,0:T(8,128)(2,1)}, bf16[160,1152]{1,0:T(8,128)(2,1)}, bf16[160,1152]{1,0:T(8,128)(2,1)}, bf16[160,1152]{1,0:T(8,128)(2,1)}) custom-call(f32[160,2]{1,0:T(8,128)} %constant.16.clone.wanted_ref, bf16[144,1152]{1,0:T(8,128)(2,1)} %prepare.1.block_ref.refs_0_, bf16[144,1152]{1,0:T(8,128)(2,1)} %copy-done.9), custom_call_target="tpu_custom_call" | custom-call | flops 424673280 | bytes 2949120 | tf_op jit(solution)/shard_map/dispatch/pallas_call | solution.py:251
  23.8 2.6 %collective-permute-start.3 = (bf16[160,1152]{1,0:T(8,128)(2,1)}, bf16[160,1152]{1,0:T(8,128)(2,1)S(1)}, u32[]{:S(2)}, u32[]{:S(2)}) collective-permute-start(bf16[160,1152]{1,0:T(8,128)(2,1)} %get-tuple-element.63), channel_id=1, source_target_pairs={{0,8},{4,12},{8,0},{12,4},{1,9},{5,13},{9,1},{13,5},{2,10},{6,14},... | collective-permute-start | bytes 1105928 | tf_op jit(solution)/shard_map/ppermute | solution.py:152
  26.4 3.8 %collective-permute-done.5.refs_10_ = bf16[144,1152]{1,0:T(8,128)(2,1)S(1)} collective-permute-done((bf16[144,1152]{1,0:T(8,128)(2,1)}, bf16[144,1152]{1,0:T(8,128)(2,1)S(1)}, u32[]{:S(2)}, u32[]{:S(2)}) %collective-permute-start.5) | collective-permute-done | bytes 331808 | tf_op jit(solution)/shard_map/ppermute | solution.py:152
  35.2 5.7 %collective-permute-done.7.refs_11_ = bf16[144,1152]{1,0:T(8,128)(2,1)S(1)} collective-permute-done((bf16[144,1152]{1,0:T(8,128)(2,1)S(1)}, bf16[144,1152]{1,0:T(8,128)(2,1)S(1)}, u32[]{:S(2)}, u32[]{:S(2)}) %collective-permute-start.7) | collective-permute-done | bytes 331808 | tf_op jit(solution)/shard_map/ppermute | solution.py:152
  42.1 5.7 %collective-permute-done.8.refs_12_ = bf16[144,1152]{1,0:T(8,128)(2,1)S(1)} collective-permute-done((bf16[144,1152]{1,0:T(8,128)(2,1)S(1)}, bf16[144,1152]{1,0:T(8,128)(2,1)S(1)}, u32[]{:S(2)}, u32[]{:S(2)}) %collective-permute-start.8) | collective-permute-done | bytes 331808 | tf_op jit(solution)/shard_map/ppermute | solution.py:152
  47.8 3.9 %collective-permute-start.9 = (bf16[160,1152]{1,0:T(8,128)(2,1)}, bf16[160,1152]{1,0:T(8,128)(2,1)S(1)}, u32[]{:S(2)}, u32[]{:S(2)}) collective-permute-start(bf16[160,1152]{1,0:T(8,128)(2,1)} %get-tuple-element.75), channel_id=1, source_target_pairs={{0,12},{4,8},{8,4},{12,0},{1,13},{5,9},{9,5},{13,1},{2,14},{6,10},... | collective-permute-start | bytes 1105928 | tf_op jit(solution)/shard_map/ppermute | solution.py:152
  55.3 3.3 %collective-permute-done.10.refs_10_ = bf16[288,1152]{1,0:T(8,128)(2,1)S(1)} collective-permute-done((bf16[288,1152]{1,0:T(8,128)(2,1)}, bf16[288,1152]{1,0:T(8,128)(2,1)S(1)}, u32[]{:S(2)}, u32[]{:S(2)}) %collective-permute-start.10) | collective-permute-done | bytes 663584 | tf_op jit(solution)/shard_map/ppermute | solution.py:152
  58.6 3.8 %collective-permute-done.11.refs_11_ = bf16[144,1152]{1,0:T(8,128)(2,1)S(1)} collective-permute-done((bf16[144,1152]{1,0:T(8,128)(2,1)S(1)}, bf16[144,1152]{1,0:T(8,128)(2,1)S(1)}, u32[]{:S(2)}, u32[]{:S(2)}) %collective-permute-start.11) | collective-permute-done | bytes 331808 | tf_op jit(solution)/shard_map/ppermute | solution.py:152
  62.5 6.0 %collective-permute-done.12.refs_11_ = bf16[144,1152]{1,0:T(8,128)(2,1)S(1)} collective-permute-done((bf16[144,1152]{1,0:T(8,128)(2,1)S(1)}, bf16[144,1152]{1,0:T(8,128)(2,1)S(1)}, u32[]{:S(2)}, u32[]{:S(2)}) %collective-permute-start.12) | collective-permute-done | bytes 331808 | tf_op jit(solution)/shard_map/ppermute | solution.py:152
  74.1 7.3 %expert.4 = (f32[80,1152]{1,0:T(8,128)S(1)}, f32[80,1152]{1,0:T(8,128)S(1)}, bf16[160,1152]{1,0:T(8,128)(2,1)S(1)}) custom-call(bf16[8,288,2304]{2,1,0:T(8,128)(2,1)} %own_ref.7, f32[8,1,640]{2,1,0:T(1,128)S(1)} %broadcast_in_dim.3.b_ref, bf16[8,576,1152]{2,1,0:T(8,128)(2,1)} %out_w_ref.7, bf16[160,1152]{1,0:T(8,128)(2,1)S(1)} %copy-done.1, ...), custom_call_target="tpu_custom_call" | custom-call | flops 1698693120 | bytes 24772608 | tf_op jit(solution)/shard_map/expert/pallas_call | solution.py:470
  81.5 5.0 %collective-permute-done.22.refs_15_.refs_12_ = bf16[144,1152]{1,0:T(8,128)(2,1)S(1)} collective-permute-done((bf16[144,1152]{1,0:T(8,128)(2,1)S(1)}, bf16[144,1152]{1,0:T(8,128)(2,1)S(1)}, u32[]{:S(2)}, u32[]{:S(2)}) %collective-permute-start.22) | collective-permute-done | bytes 331808 | tf_op jit(solution)/shard_map/ppermute | solution.py:152
  86.5 7.5 %expert.5 = (f32[80,1152]{1,0:T(8,128)S(1)}, f32[80,1152]{1,0:T(8,128)S(1)}, bf16[160,1152]{1,0:T(8,128)(2,1)S(1)}) custom-call(bf16[8,288,2304]{2,1,0:T(8,128)(2,1)} %own_ref.7, f32[8,1,640]{2,1,0:T(1,128)S(1)} %broadcast_in_dim.3.b_ref, bf16[8,576,1152]{2,1,0:T(8,128)(2,1)} %out_w_ref.7, bf16[160,1152]{1,0:T(8,128)(2,1)S(1)} %copy-done.1, ...), custom_call_target="tpu_custom_call" | custom-call | flops 1698693120 | bytes 24772608 | tf_op jit(solution)/shard_map/expert/pallas_call | solution.py:470
  99.4 7.4 %expert.7 = (f32[80,1152]{1,0:T(8,128)S(1)}, f32[80,1152]{1,0:T(8,128)S(1)}, bf16[160,1152]{1,0:T(8,128)(2,1)S(1)}) custom-call(bf16[8,288,2304]{2,1,0:T(8,128)(2,1)} %own_ref.7, f32[8,1,640]{2,1,0:T(1,128)S(1)} %broadcast_in_dim.3.b_ref, bf16[8,576,1152]{2,1,0:T(8,128)(2,1)} %out_w_ref.7, bf16[160,1152]{1,0:T(8,128)(2,1)S(1)} %copy-done.1, ...), custom_call_target="tpu_custom_call" | custom-call | flops 1698693120 | bytes 24772608 | tf_op jit(solution)/shard_map/expert/pallas_call | solution.py:470
  107.3 4.0 %collective-permute-done.26.refs_12_ = bf16[144,1152]{1,0:T(8,128)(2,1)S(1)} collective-permute-done((bf16[144,1152]{1,0:T(8,128)(2,1)S(1)}, bf16[144,1152]{1,0:T(8,128)(2,1)S(1)}, u32[]{:S(2)}, u32[]{:S(2)}) %collective-permute-start.26) | collective-permute-done | bytes 331808 | tf_op jit(solution)/shard_map/ppermute | solution.py:152
  111.4 7.4 %expert.6 = (f32[80,1152]{1,0:T(8,128)S(1)}, f32[80,1152]{1,0:T(8,128)S(1)}, bf16[160,1152]{1,0:T(8,128)(2,1)S(1)}) custom-call(bf16[8,288,2304]{2,1,0:T(8,128)(2,1)} %own_ref.7, f32[8,1,640]{2,1,0:T(1,128)S(1)} %broadcast_in_dim.3.b_ref, bf16[8,576,1152]{2,1,0:T(8,128)(2,1)} %out_w_ref.7, bf16[160,1152]{1,0:T(8,128)(2,1)S(1)} %copy-done.1, ...), custom_call_target="tpu_custom_call" | custom-call | flops 1698693120 | bytes 24772608 | tf_op jit(solution)/shard_map/expert/pallas_call | solution.py:470
  123.1 2.5 %collective-permute-start.30 = (bf16[40,1152]{1,0:T(8,128)(2,1)S(1)}, bf16[40,1152]{1,0:T(8,128)(2,1)S(1)}, u32[]{:S(2)}, u32[]{:S(2)}) collective-permute-start(bf16[40,1152]{1,0:T(8,128)(2,1)S(1)} %pad_maximum_fusion.3), channel_id=1, source_target_pairs={{0,12},{4,8},{8,4},{12,0},{1,13},{5,9},{9,5},{13,1},{2,14},{6,10},... | collective-permute-start | bytes 276488 | tf_op jit(solution)/shard_map/ppermute | solution.py:152
  127.3 4.3 %collective-permute-done.29.refs_2_ = bf16[40,1152]{1,0:T(8,128)(2,1)S(1)} collective-permute-done((bf16[40,1152]{1,0:T(8,128)(2,1)S(1)}, bf16[40,1152]{1,0:T(8,128)(2,1)S(1)}, u32[]{:S(2)}, u32[]{:S(2)}) %collective-permute-start.29) | collective-permute-done | bytes 92192 | tf_op jit(solution)/shard_map/ppermute | solution.py:152
  132.9 2.4 %combine.2.refs_0_ = f32[128,1152]{1,0:T(8,128)} custom-call(f32[128,128]{1,0:T(8,128)} %route.1.route_ref, bf16[40,1152]{1,0:T(8,128)(2,1)} %pad_maximum_fusion.refs_0_, bf16[40,1152]{1,0:T(8,128)(2,1)} %copy-done.5, bf16[40,1152]{1,0:T(8,128)(2,1)} %copy-done.6, bf16[40,1152]{1,0:T(8,128)(2,1)} %copy-done.7), custom_call_target="tpu_custom_call" | custom-call | tf_op jit(solution)/shard_map/combine/pallas_call | solution.py:541
  140.6 5.3 %collective-permute-done.35.refs_5_ = bf16[40,1152]{1,0:T(8,128)(2,1)S(1)} collective-permute-done((bf16[40,1152]{1,0:T(8,128)(2,1)S(1)}, bf16[40,1152]{1,0:T(8,128)(2,1)S(1)}, u32[]{:S(2)}, u32[]{:S(2)}) %collective-permute-start.35) | collective-permute-done | bytes 92192 | tf_op jit(solution)/shard_map/ppermute | solution.py:152
  147.2 2.5 %combine.3 = bf16[1,128,1152]{2,1,0:T(8,128)(2,1)} custom-call(f32[128,128]{1,0:T(8,128)} %route.1.route_ref, f32[128,1152]{1,0:T(8,128)} %combine.2.refs_0_, bf16[1,128,1152]{2,1,0:T(8,128)(2,1)} %refs_1_.1, f32[3,1152]{1,0:T(4,128)} %bitcast.8, bf16[40,1152]{1,0:T(8,128)(2,1)} %pad_maximum_fusion.4.refs_3_, bf16[40,1152]{1,0:T(8,128)(2,1)} %copy-done.2, ...), custom_call_target="tpu_custom_call" | custom-call | tf_op jit(solution)/shard_map/combine/pallas_call | solution.py:541
  (105 shorter events, 43.9 us)
Async XLA Ops:
  0.0 16.8 %collective-permute-start.1 = (bf16[8,288,2304]{2,1,0:T(8,128)(2,1)}, bf16[8,288,2304]{2,1,0:T(8,128)(2,1)}, u32[]{:S(2)}, u32[]{:S(2)}) collective-permute-start(bf16[8,288,2304]{2,1,0:T(8,128)(2,1)} %own_ref.7), channel_id=1, source_target_pairs={{0,1},{1,0},{2,3},{3,2},{4,5},{5,4},{6,7},{7,6},{8,9},{9,8},{10,11... | collective-permute-start | bytes 31850504 | tf_op jit(solution)/shard_map/ppermute | solution.py:152
  5.0 11.4 %collective-permute-start = (bf16[144,1152]{1,0:T(8,128)(2,1)}, bf16[144,1152]{1,0:T(8,128)(2,1)S(1)}, u32[]{:S(2)}, u32[]{:S(2)}) collective-permute-start(bf16[144,1152]{1,0:T(8,128)(2,1)} %prepare.1.block_ref.refs_0_), channel_id=1, source_target_pairs={{0,2},{1,3},{2,0},{3,1},{4,6},{5,7},{6,4},{7,5},{8,10},{9,11},{10,... | collective-permute-start | bytes 995336 | tf_op jit(solution)/shard_map/ppermute | solution.py:152
  10.5 15.9 %collective-permute-start.4 = (bf16[144,1152]{1,0:T(8,128)(2,1)}, bf16[144,1152]{1,0:T(8,128)(2,1)S(1)}, u32[]{:S(2)}, u32[]{:S(2)}) collective-permute-start(bf16[144,1152]{1,0:T(8,128)(2,1)} %get-tuple-element.66), channel_id=1, source_target_pairs={{0,2},{1,3},{2,0},{3,1},{4,6},{5,7},{6,4},{7,5},{8,10},{9,11},{10,... | collective-permute-start | bytes 995336 | tf_op jit(solution)/shard_map/ppermute | solution.py:152
  10.6 19.6 %collective-permute-start.5 = (bf16[144,1152]{1,0:T(8,128)(2,1)}, bf16[144,1152]{1,0:T(8,128)(2,1)S(1)}, u32[]{:S(2)}, u32[]{:S(2)}) collective-permute-start(bf16[144,1152]{1,0:T(8,128)(2,1)} %get-tuple-element.67), channel_id=1, source_target_pairs={{0,3},{1,2},{2,1},{3,0},{4,7},{5,6},{6,5},{7,4},{8,11},{9,10},{10,... | collective-permute-start | bytes 995336 | tf_op jit(solution)/shard_map/ppermute | solution.py:152
  16.8 31.0 %collective-permute-start.6 = (bf16[288,1152]{1,0:T(8,128)(2,1)}, bf16[288,1152]{1,0:T(8,128)(2,1)S(1)}, u32[]{:S(2)}, u32[]{:S(2)}) collective-permute-start(bf16[288,1152]{1,0:T(8,128)(2,1)} %get-tuple-element.71), channel_id=1, source_target_pairs={{0,2},{1,3},{2,0},{3,1},{4,6},{5,7},{6,4},{7,5},{8,10},{9,11},{10,... | collective-permute-start | bytes 1990664 | tf_op jit(solution)/shard_map/ppermute | solution.py:152
  22.3 25.5 %collective-permute-start.2 = (bf16[160,1152]{1,0:T(8,128)(2,1)}, bf16[160,1152]{1,0:T(8,128)(2,1)S(1)}, u32[]{:S(2)}, u32[]{:S(2)}) collective-permute-start(bf16[160,1152]{1,0:T(8,128)(2,1)} %get-tuple-element.62), channel_id=1, source_target_pairs={{0,4},{4,0},{8,12},{12,8},{1,5},{5,1},{9,13},{13,9},{2,6},{6,2},{1... | collective-permute-start | bytes 1105928 | tf_op jit(solution)/shard_map/ppermute | solution.py:152
  23.8 24.0 %collective-permute-start.3 = (bf16[160,1152]{1,0:T(8,128)(2,1)}, bf16[160,1152]{1,0:T(8,128)(2,1)S(1)}, u32[]{:S(2)}, u32[]{:S(2)}) collective-permute-start(bf16[160,1152]{1,0:T(8,128)(2,1)} %get-tuple-element.63), channel_id=1, source_target_pairs={{0,8},{4,12},{8,0},{12,4},{1,9},{5,13},{9,1},{13,5},{2,10},{6,14},... | collective-permute-start | bytes 1105928 | tf_op jit(solution)/shard_map/ppermute | solution.py:152
  30.2 10.7 %collective-permute-start.7 = (bf16[144,1152]{1,0:T(8,128)(2,1)S(1)}, bf16[144,1152]{1,0:T(8,128)(2,1)S(1)}, u32[]{:S(2)}, u32[]{:S(2)}) collective-permute-start(bf16[144,1152]{1,0:T(8,128)(2,1)S(1)} %collective-permute-done.4.refs_9_), channel_id=1, source_target_pairs={{0,16},{16,0},{1,17},{17,1},{2,18},{18,2},{3,19},{19,3},{4,20},{20... | collective-permute-start | bytes 995336 | tf_op jit(solution)/shard_map/ppermute | solution.py:152
  31.7 16.1 %collective-permute-start.8 = (bf16[144,1152]{1,0:T(8,128)(2,1)S(1)}, bf16[144,1152]{1,0:T(8,128)(2,1)S(1)}, u32[]{:S(2)}, u32[]{:S(2)}) collective-permute-start(bf16[144,1152]{1,0:T(8,128)(2,1)S(1)} %collective-permute-done.5.refs_10_), channel_id=1, source_target_pairs={{0,16},{16,0},{1,17},{17,1},{2,18},{18,2},{3,19},{19,3},{4,20},{20... | collective-permute-start | bytes 995336 | tf_op jit(solution)/shard_map/ppermute | solution.py:152
  40.9 17.8 %collective-permute-start.10 = (bf16[288,1152]{1,0:T(8,128)(2,1)}, bf16[288,1152]{1,0:T(8,128)(2,1)S(1)}, u32[]{:S(2)}, u32[]{:S(2)}) collective-permute-start(bf16[288,1152]{1,0:T(8,128)(2,1)} %get-tuple-element.77), channel_id=1, source_target_pairs={{0,3},{1,2},{2,1},{3,0},{4,7},{5,6},{6,5},{7,4},{8,11},{9,10},{10,... | collective-permute-start | bytes 1990664 | tf_op jit(solution)/shard_map/ppermute | solution.py:152
  47.8 20.6 %collective-permute-start.9 = (bf16[160,1152]{1,0:T(8,128)(2,1)}, bf16[160,1152]{1,0:T(8,128)(2,1)S(1)}, u32[]{:S(2)}, u32[]{:S(2)}) collective-permute-start(bf16[160,1152]{1,0:T(8,128)(2,1)} %get-tuple-element.75), channel_id=1, source_target_pairs={{0,12},{4,8},{8,4},{12,0},{1,13},{5,9},{9,5},{13,1},{2,14},{6,10},... | collective-permute-start | bytes 1105928 | tf_op jit(solution)/shard_map/ppermute | solution.py:152
  51.7 10.7 %collective-permute-start.11 = (bf16[144,1152]{1,0:T(8,128)(2,1)S(1)}, bf16[144,1152]{1,0:T(8,128)(2,1)S(1)}, u32[]{:S(2)}, u32[]{:S(2)}) collective-permute-start(bf16[144,1152]{1,0:T(8,128)(2,1)S(1)} %get-tuple-element.78), channel_id=1, source_target_pairs={{0,16},{16,0},{1,17},{17,1},{2,18},{18,2},{3,19},{19,3},{4,20},{20... | collective-permute-start | bytes 995336 | tf_op jit(solution)/shard_map/ppermute | solution.py:152
  53.3 15.2 %collective-permute-start.12 = (bf16[144,1152]{1,0:T(8,128)(2,1)S(1)}, bf16[144,1152]{1,0:T(8,128)(2,1)S(1)}, u32[]{:S(2)}, u32[]{:S(2)}) collective-permute-start(bf16[144,1152]{1,0:T(8,128)(2,1)S(1)} %get-tuple-element.79), channel_id=1, source_target_pairs={{0,16},{16,0},{1,17},{17,1},{2,18},{18,2},{3,19},{19,3},{4,20},{20... | collective-permute-start | bytes 995336 | tf_op jit(solution)/shard_map/ppermute | solution.py:152
  53.8 14.6 %collective-permute-start.13 = (bf16[144,1152]{1,0:T(8,128)(2,1)}, bf16[144,1152]{1,0:T(8,128)(2,1)S(1)}, u32[]{:S(2)}, u32[]{:S(2)}) collective-permute-start(bf16[144,1152]{1,0:T(8,128)(2,1)} %get-tuple-element.82), channel_id=1, source_target_pairs={{0,2},{1,3},{2,0},{3,1},{4,6},{5,7},{6,4},{7,5},{8,10},{9,11},{10,... | collective-permute-start | bytes 995336 | tf_op jit(solution)/shard_map/ppermute | solution.py:152
  69.5 11.9 %collective-permute-start.20 = (bf16[144,1152]{1,0:T(8,128)(2,1)S(1)}, bf16[144,1152]{1,0:T(8,128)(2,1)S(1)}, u32[]{:S(2)}, u32[]{:S(2)}) collective-permute-start(bf16[144,1152]{1,0:T(8,128)(2,1)S(1)} %get-tuple-element.91), channel_id=1, source_target_pairs={{0,16},{16,0},{1,17},{17,1},{2,18},{18,2},{3,19},{19,3},{4,20},{20... | collective-permute-start | bytes 995336 | tf_op jit(solution)/shard_map/ppermute | solution.py:152
  71.1 10.3 %collective-permute-start.21 = (bf16[144,1152]{1,0:T(8,128)(2,1)}, bf16[144,1152]{1,0:T(8,128)(2,1)S(1)}, u32[]{:S(2)}, u32[]{:S(2)}) collective-permute-start(bf16[144,1152]{1,0:T(8,128)(2,1)} %get-tuple-element.93), channel_id=1, source_target_pairs={{0,3},{1,2},{2,1},{3,0},{4,7},{5,6},{6,5},{7,4},{8,11},{9,10},{10,... | collective-permute-start | bytes 995336 | tf_op jit(solution)/shard_map/ppermute | solution.py:152
  72.0 14.5 %collective-permute-start.22 = (bf16[144,1152]{1,0:T(8,128)(2,1)S(1)}, bf16[144,1152]{1,0:T(8,128)(2,1)S(1)}, u32[]{:S(2)}, u32[]{:S(2)}) collective-permute-start(bf16[144,1152]{1,0:T(8,128)(2,1)S(1)} %get-tuple-element.94), channel_id=1, source_target_pairs={{0,16},{16,0},{1,17},{17,1},{2,18},{18,2},{3,19},{19,3},{4,20},{20... | collective-permute-start | bytes 995336 | tf_op jit(solution)/shard_map/ppermute | solution.py:152
  94.0 13.3 %collective-permute-start.25 = (bf16[144,1152]{1,0:T(8,128)(2,1)S(1)}, bf16[144,1152]{1,0:T(8,128)(2,1)S(1)}, u32[]{:S(2)}, u32[]{:S(2)}) collective-permute-start(bf16[144,1152]{1,0:T(8,128)(2,1)S(1)} %collective-permute-done.13.refs_9_), channel_id=1, source_target_pairs={{0,16},{16,0},{1,17},{17,1},{2,18},{18,2},{3,19},{19,3},{4,20},{20... | collective-permute-start | bytes 995336 | tf_op jit(solution)/shard_map/ppermute | solution.py:152
  95.6 15.7 %collective-permute-start.26 = (bf16[144,1152]{1,0:T(8,128)(2,1)S(1)}, bf16[144,1152]{1,0:T(8,128)(2,1)S(1)}, u32[]{:S(2)}, u32[]{:S(2)}) collective-permute-start(bf16[144,1152]{1,0:T(8,128)(2,1)S(1)} %collective-permute-done.21.refs_14_.refs_10_), channel_id=1, source_target_pairs={{0,16},{16,0},{1,17},{17,1},{2,18},{18,2},{3,19},{19,3},{4,20},{20... | collective-permute-start | bytes 995336 | tf_op jit(solution)/shard_map/ppermute | solution.py:152
  96.2 10.8 %collective-permute-start.24 = (bf16[80,1152]{1,0:T(8,128)(2,1)S(1)}, bf16[80,1152]{1,0:T(8,128)(2,1)S(1)}, u32[]{:S(2)}, u32[]{:S(2)}) collective-permute-start(bf16[80,1152]{1,0:T(8,128)(2,1)S(1)} %add_convert_fusion.5), channel_id=1, source_target_pairs={{0,2},{1,3},{2,0},{3,1},{4,6},{5,7},{6,4},{7,5},{8,10},{9,11},{10,... | collective-permute-start | bytes 552968 | tf_op jit(solution)/shard_map/ppermute | solution.py:152
  97.9 9.4 %collective-permute-start.19 = (bf16[80,1152]{1,0:T(8,128)(2,1)S(1)}, bf16[80,1152]{1,0:T(8,128)(2,1)S(1)}, u32[]{:S(2)}, u32[]{:S(2)}) collective-permute-start(bf16[80,1152]{1,0:T(8,128)(2,1)S(1)} %add_convert_fusion.7), channel_id=1, source_target_pairs={{0,2},{1,3},{2,0},{3,1},{4,6},{5,7},{6,4},{7,5},{8,10},{9,11},{10,... | collective-permute-start | bytes 552968 | tf_op jit(solution)/shard_map/ppermute | solution.py:152
  106.8 12.8 %collective-permute-start.31 = (bf16[160,1152]{1,0:T(8,128)(2,1)S(1)}, bf16[160,1152]{1,0:T(8,128)(2,1)S(1)}, u32[]{:S(2)}, u32[]{:S(2)}) collective-permute-start(bf16[160,1152]{1,0:T(8,128)(2,1)S(1)} %get-tuple-element.104), channel_id=1, source_target_pairs={{0,1},{1,0},{2,3},{3,2},{4,5},{5,4},{6,7},{7,6},{8,9},{9,8},{10,11... | collective-permute-start | bytes 1105928 | tf_op jit(solution)/shard_map/ppermute | solution.py:152
  121.2 10.4 %collective-permute-start.29 = (bf16[40,1152]{1,0:T(8,128)(2,1)S(1)}, bf16[40,1152]{1,0:T(8,128)(2,1)S(1)}, u32[]{:S(2)}, u32[]{:S(2)}) collective-permute-start(bf16[40,1152]{1,0:T(8,128)(2,1)S(1)} %get-tuple-element.101), channel_id=1, source_target_pairs={{0,8},{4,12},{8,0},{12,4},{1,9},{5,13},{9,1},{13,5},{2,10},{6,14},... | collective-permute-start | bytes 276488 | tf_op jit(solution)/shard_map/ppermute | solution.py:152
  125.6 9.6 %collective-permute-start.33 = (bf16[80,1152]{1,0:T(8,128)(2,1)S(1)}, bf16[80,1152]{1,0:T(8,128)(2,1)S(1)}, u32[]{:S(2)}, u32[]{:S(2)}) collective-permute-start(bf16[80,1152]{1,0:T(8,128)(2,1)S(1)} %add_convert_fusion.1), channel_id=1, source_target_pairs={{0,2},{1,3},{2,0},{3,1},{4,6},{5,7},{6,4},{7,5},{8,10},{9,11},{10,... | collective-permute-start | bytes 552968 | tf_op jit(solution)/shard_map/ppermute | solution.py:152
  (23 other events, 148.5 us)
